TPU v7x, 128 devices: a whole 4x4x4 slice. The times are simulated.
128 devices in a mesh: shard: 128 (over z, x, y, core).
Axes of the slice: x: 4, y: 4, z: 4, core: 2. Of those that a mesh axis runs over, the one named last changes fastest.
Arguments:
- entity_table: float32 [262144, 400], P('shard'), may hold values from -2.5 to 2.5
- entity_accum: float32 [262144], P('shard'), may hold values from 0.001 to 0.1
- hub_table: float32 [1024, 400], replicated, may hold values from -2.5 to 2.5
- hub_accum: float32 [1024], replicated, may hold values from 0.001 to 0.1
- relation_table: float32 [512, 400], replicated, may hold values from -2.5 to 2.5
- relation_accum: float32 [512], replicated, may hold values from 0.001 to 0.1
- head_ids: int32 [65536], P('shard'), may hold values from 0 to 3071
- relation_ids: int32 [65536], P('shard'), may hold values from 0 to 511
- tail_owner: int32 [65536, 1], P('shard'), may hold values from 0 to 127; in each aligned block of 512 rows (0 to 511, 512 to 1023, ...) at most 8 rows name the same one
- tail_rows: int32 [65536], P('shard'), may hold values from 0 to 2047
- negative_rows: int32 [2048], P('shard'), may hold values from 0 to 2047
Outputs:
- entity_new: float32 [262144, 400], P('shard')
- entity_accum_new: float32 [262144], P('shard')
- hub_new: float32 [1024, 400], replicated
- hub_accum_new: float32 [1024], replicated
- relation_new: float32 [512, 400], replicated
- relation_accum_new: float32 [512], replicated
- triple_loss: float32 [65536], P('shard')
Inputs may be any that keep to these rules, and one draw needn't show every extreme that they name: Below 1024 a head is hub head_ids; otherwise it is row head_ids - 1024 of the entities held by the triple's own device. `tail_owner`: among the 512 triples of one device, at most 8 have their tail on one owner, and in every draw some owner is named exactly 8 times. `negative_rows`: entry j is a row of the entities held by device j // 16; rows may repeat.
All inputs are finite; a program needn't handle non-finite values.
Results may differ from a plain program's by a relative error of at most 0.0001.
Values sent between devices are 32-bit elements; how exact they have to be, the bound alone decides.
No kernel may reach another device: no remote copies, remote signals or barrier semaphores. Data moves between devices by JAX's collectives and lax.ppermute only.
A program may use at most 128 MiB of HBM per device.

v0:
```python
import jax
import jax.numpy as jnp
from jax import lax
from jax.sharding import PartitionSpec as P

LEARN_RATE = 0.1


def compose(head_rows, rel_rows):
    half_width = head_rows.shape[-1] // 2
    head_re, head_im = (head_rows[..., :half_width], head_rows[..., half_width:])
    rel_re, rel_im = (rel_rows[..., :half_width], rel_rows[..., half_width:])
    return jnp.concatenate(
        [head_re * rel_re - head_im * rel_im, head_re * rel_im + head_im * rel_re], axis=-1
    )


def spread(grad_query, head_rows, rel_rows):
    half_width = head_rows.shape[-1] // 2
    head_re, head_im = (head_rows[..., :half_width], head_rows[..., half_width:])
    rel_re, rel_im = (rel_rows[..., :half_width], rel_rows[..., half_width:])
    grad_re, grad_im = (grad_query[..., :half_width], grad_query[..., half_width:])
    grad_head = jnp.concatenate(
        [grad_re * rel_re + grad_im * rel_im, grad_im * rel_re - grad_re * rel_im], axis=-1
    )
    grad_rel = jnp.concatenate(
        [grad_re * head_re + grad_im * head_im, grad_im * head_re - grad_re * head_im], axis=-1
    )
    return (grad_head, grad_rel)


def adagrad(table_rows, accum_rows, grad_rows):
    new_accum = accum_rows + jnp.mean(grad_rows * grad_rows, axis=-1)
    return (table_rows - LEARN_RATE * grad_rows / jnp.sqrt(new_accum)[:, None], new_accum)


def body(
    entity_table,
    entity_accum,
    hub_table,
    hub_accum,
    relation_table,
    relation_accum,
    head_ids,
    relation_ids,
    tail_owner,
    tail_rows,
    negative_rows,
):
    highest = lax.Precision.HIGHEST
    shards = lax.axis_size("shard")
    ent_dev, width = entity_table.shape
    hub_count = hub_table.shape[0]
    trip_dev = head_ids.shape[0]
    capacity = 2 * trip_dev // shards
    is_hub = head_ids < hub_count
    hub_head = jnp.clip(head_ids, 0, hub_count - 1)
    ent_head = jnp.clip(head_ids - hub_count, 0, ent_dev - 1)
    head_vecs = jnp.where(is_hub[:, None], hub_table[hub_head], entity_table[ent_head])
    rel_vecs = relation_table[relation_ids]
    queries = compose(head_vecs, rel_vecs)
    neg_vecs = lax.all_gather(entity_table[negative_rows], "shard", axis=0, tiled=True)
    neg_total = neg_vecs.shape[0]
    scores = jnp.dot(queries, neg_vecs.T, precision=highest, preferred_element_type=jnp.float32)
    neg_loss = jnp.mean(jax.nn.softplus(scores), axis=1)
    grad_neg = jax.nn.sigmoid(scores) / neg_total
    owner_ids = tail_owner[:, 0]
    owner_hot = (owner_ids[:, None] == jnp.arange(shards, dtype=jnp.int32)[None, :]).astype(
        jnp.int32
    )
    slot_ids = jnp.sum((jnp.cumsum(owner_hot, axis=0) - 1) * owner_hot, axis=1)
    request = jnp.zeros((shards, capacity), jnp.int32).at[owner_ids, slot_ids].set(tail_rows)
    asked_rows = lax.all_to_all(request, "shard", split_axis=0, concat_axis=0, tiled=True)
    fetched = lax.all_to_all(
        entity_table[asked_rows], "shard", split_axis=0, concat_axis=0, tiled=True
    )
    tail_vecs = fetched[owner_ids, slot_ids]
    positive = jnp.sum(queries * tail_vecs, axis=-1)
    grad_pos = -jax.nn.sigmoid(-positive)
    tail_term = grad_pos[:, None] * tail_vecs
    slot_grads = (
        jnp.zeros((shards, capacity, width), jnp.float32)
        .at[owner_ids, slot_ids]
        .set(grad_pos[:, None] * queries)
    )
    owned_grads = lax.all_to_all(slot_grads, "shard", split_axis=0, concat_axis=0, tiled=True)
    triple_loss = jax.nn.softplus(-positive) + neg_loss
    grad_query = tail_term + jnp.dot(
        grad_neg, neg_vecs, precision=highest, preferred_element_type=jnp.float32
    )
    grad_negvec = lax.psum_scatter(
        jnp.dot(grad_neg.T, queries, precision=highest, preferred_element_type=jnp.float32),
        "shard",
        scatter_dimension=0,
        tiled=True,
    )
    grad_head, grad_rel = spread(grad_query, head_vecs, rel_vecs)
    entity_grad = jnp.zeros((ent_dev, width), jnp.float32)
    entity_grad = entity_grad.at[ent_head].add(jnp.where(is_hub[:, None], 0.0, grad_head))
    entity_grad = entity_grad.at[asked_rows.reshape(-1)].add(owned_grads.reshape(-1, width))
    entity_grad = entity_grad.at[negative_rows].add(grad_negvec)
    hub_grad = (
        jnp.zeros((hub_count, width), jnp.float32)
        .at[hub_head]
        .add(jnp.where(is_hub[:, None], grad_head, 0.0))
    )
    relation_grad = jnp.zeros(relation_table.shape, jnp.float32).at[relation_ids].add(grad_rel)
    entity_new, entity_accum_new = adagrad(entity_table, entity_accum, entity_grad)
    hub_sum, relation_sum = lax.psum((hub_grad, relation_grad), "shard")
    hub_new, hub_accum_new = adagrad(hub_table, hub_accum, hub_sum)
    relation_new, relation_accum_new = adagrad(relation_table, relation_accum, relation_sum)
    return (
        entity_new,
        entity_accum_new,
        hub_new,
        hub_accum_new,
        relation_new,
        relation_accum_new,
        triple_loss,
    )


def solution(mesh):
    placed = (
        P("shard", None),
        P("shard"),
        P(),
        P(),
        P(),
        P(),
        P("shard"),
        P("shard"),
        P("shard", None),
        P("shard"),
        P("shard"),
    )
    return jax.shard_map(
        body,
        mesh=mesh,
        in_specs=placed,
        out_specs=(P("shard", None), P("shard"), P(), P(), P(), P(), P("shard")),
        check_vma=False,
    )
```

profile of v0, /device:TPU:0, one launch (start us, length us, event | category | flops | bytes accessed | tf_op | source)
XLA Modules:
  0.0 994.2 jit_solution(5146026220580438977)
XLA Ops:
  7.9 5.0 copy.72
  12.9 3.4 gather_fusion.5
  17.1 22.0 %scatter_fusion = s32[128,8]{0,1:T(8,128)S(1)} fusion(s32[128,8]{0,1:T(8,128)S(1)} %broadcast.123, s32[512]{0:T(512)S(1)} %bitcast.27, s32[512]{0:T(512)S(1)} %copy-done.11), kind=kCustom, calls=%fused_computation.6 | custom fusion | bytes 10240 | tf_op jit(solution)/shard_map/scatter | solution.py:72
  39.8 11.1 %all-to-all-start = ((s32[128,1,8]{2,1,0:T(1,128)}), s32[128,1,8]{2,1,0:T(1,128)S(1)}, u32[]{:S(2)}, u32[]{:S(2)}) async-start(s32[128,1,8]{2,1,0:T(1,128)} %copy.65), calls=%async_computation | async-start | bytes 131072 | tf_op jit(solution)/shard_map/all_to_all | solution.py:73
  51.3 8.9 all-to-all-done
  60.3 7.5 gather_fusion.3
  67.8 5.9 all-to-all-start.1
  84.6 5.0 gather_fusion.1
  96.8 9.9 all-to-all-done.1
  106.6 9.0 gather_fusion.4
  119.6 17.1 %fusion = (f32[512]{0:T(512)S(1)}, f32[512,2048]{1,0:T(8,128)S(1)}) fusion(f32[2048,400]{1,0:T(8,128)} %all-gather.3.cloned.1.call-done, f32[512,200]{0,1:T(8,128)} %get-tuple-element.36, f32[512,200]{0,1:T(8,128)} %get-tuple-element.35), kind=kOutput, calls=%fused_computation.14 | convolution fusion | flops 5040709120 | bytes 8292352 | tf_op jit(solution)/shard_map/dot_general | solution.py:64
  137.4 8.4 convolution_add_fusion
  147.9 2.5 copy.76
  150.4 2.5 fusion.8
  152.9 2.5 copy.73
  155.3 5.2 scatter_custom_fusion.6
  160.6 5.9 scatter_custom_fusion.5
  166.5 16.8 %fusion.7 = f32[2048,400]{1,0:T(8,128)} fusion(f32[512,2048]{1,0:T(8,128)} %copy-done.15, f32[512,200]{0,1:T(8,128)} %get-tuple-element.36, f32[512,200]{0,1:T(8,128)} %get-tuple-element.35), kind=kOutput, calls=%fused_computation.33 | convolution fusion | flops 5037563904 | bytes 8290304 | tf_op jit(solution)/shard_map/dot_general | solution.py:92
  186.9 2.5 copy.71
  190.9 63.9 %scatter_fusion.1 = f32[128,8,400]{2,1,0:T(8,128)} fusion(f32[128,8,400]{2,1,0:T(8,128)} %broadcast_in_dim.47, s32[512]{0:T(512)S(1)} %bitcast.28, f32[512,400]{1,0:T(8,128)} %copy.71), kind=kCustom, calls=%fused_computation.8 | custom fusion | bytes 2461696 | tf_op jit(solution)/shard_map/scatter | solution.py:84
  254.8 6.0 all-to-all-start.2
  260.9 2.5 copy.70
  263.3 6.4 scatter_custom_fusion.1
  269.8 55.6 %all-reduce.3.cloned.1.call-done = (f32[1024,400]{1,0:T(8,128)}, f32[512,400]{1,0:T(8,128)}) async-done(((f32[1024,400]{1,0:T(8,128)}, f32[512,400]{1,0:T(8,128)}), (f32[1024,400]{1,0:T(8,128)}, f32[512,400]{1,0:T(8,128)})) %all-reduce.3.cloned.1.call-update) | async-done | bytes 2457616 | tf_op jit(solution)/shard_map/psum | solution.py:109
  334.6 3.4 divide_subtract_fusion.1
  338.0 2.7 copy.79
  340.7 11.5 %scatter_custom_fusion.3 = f32[2048,400]{1,0:T(8,128)} fusion(f32[2048,400]{1,0:T(8,128)} %scatter_custom_fusion.1, s32[1024]{0:T(1024)S(1)} %bitcast.34, f32[128,8,400]{2,1,0:T(8,128)} %all-to-all-done.2), kind=kCustom, calls=%fused_computation.18 | custom fusion | flops 409600 | bytes 5373952 | tf_op jit(solution)/shard_map/scatter-add | solution.py:100
  352.2 616.6 %reduce-scatter.2.cloned.1.call-done = f32[16,400]{1,0:T(8,128)} async-done(((f32[2048,400]{1,0:T(8,128)}), f32[16,400]{1,0:T(8,128)}) %reduce-scatter.2.cloned.1.call-update) | async-done | bytes 25616 | tf_op jit(solution)/shard_map/reduce_scatter | solution.py:91
  968.8 5.0 scatter_fusion.2
  973.8 2.7 multiply_reduce_fusion
  977.2 4.8 divide_subtract_fusion
  982.0 5.2 copy.78
  (90 shorter events, 42.4 us)
Async XLA Ops:
  7.2 9.2 copy-start.7
  7.2 112.4 %all-gather.3.cloned.1.call-start = ((), (), s32[]{:S(2)}) async-start(), calls=%async_computation.5 | async-start | bytes 4227072 | tf_op jit(solution)/shard_map/all_gather | solution.py:62
  7.9 9.2 copy-start.11
  12.9 38.1 %copy-start.6 = (f32[512,400]{0,1:T(8,128)S(1)}, f32[512,400]{0,1:T(8,128)}, u32[]{:S(2)}) copy-start(f32[512,400]{0,1:T(8,128)} %param.15) | copy-start | bytes 2457604
  39.8 20.4 %all-to-all-start = ((s32[128,1,8]{2,1,0:T(1,128)}), s32[128,1,8]{2,1,0:T(1,128)S(1)}, u32[]{:S(2)}, u32[]{:S(2)}) async-start(s32[128,1,8]{2,1,0:T(1,128)} %copy.65), calls=%async_computation | async-start | bytes 131072 | tf_op jit(solution)/shard_map/all_to_all | solution.py:73
  67.8 6.4 copy-start.12
  67.8 38.8 %all-to-all-start.1 = ((f32[128,8,400]{2,1,0:T(8,128)}), f32[128,8,400]{2,1,0:T(8,128)}, u32[]{:S(2)}, u32[]{:S(2)}) async-start(f32[128,8,400]{2,1,0:T(8,128)} %bitcast.9), calls=%async_computation.1 | async-start | bytes 4194304 | tf_op jit(solution)/shard_map/all_to_all | solution.py:74
  73.7 251.7 %all-reduce.3.cloned.1.call-start = ((), (), s32[]{:S(2)}) async-start(), calls=%async_computation.6 | async-start | bytes 6291456 | tf_op jit(solution)/shard_map/psum | solution.py:109
  75.9 4.0 copy-start.8
  93.6 0.9 copy-start.1
  119.6 17.8 %copy-start.5 = (f32[512,400]{0,1:T(8,128)S(1)}, f32[512,400]{0,1:T(8,128)}, u32[]{:S(2)}) copy-start(f32[512,400]{0,1:T(8,128)} %copy.67) | copy-start | bytes 2457604
  119.6 17.8 %copy-start.14 = (f32[2048,400]{1,0:T(8,128)S(1)}, f32[2048,400]{1,0:T(8,128)}, u32[]{:S(2)}) copy-start(f32[2048,400]{1,0:T(8,128)} %all-gather.3.cloned.1.call-done) | copy-start | bytes 9830404
  136.7 9.1 copy-start.15
  137.4 8.4 copy-start.2
  137.4 8.4 copy-start.3
  137.4 8.4 copy-start.4
  166.5 802.3 %reduce-scatter.2.cloned.1.call-start = ((), (), s32[]{:S(2)}) async-start(), calls=%async_computation.4 | async-start | bytes 4227072 | tf_op jit(solution)/shard_map/reduce_scatter | solution.py:91
  254.8 85.9 %all-to-all-start.2 = ((f32[128,8,400]{2,1,0:T(8,128)}), f32[128,8,400]{2,1,0:T(8,128)}, u32[]{:S(2)}, u32[]{:S(2)}) async-start(f32[128,8,400]{2,1,0:T(8,128)} %scatter_fusion.1), calls=%async_computation.2 | async-start | bytes 4194304 | tf_op jit(solution)/shard_map/all_to_all | solution.py:86
  260.8 65.9 %copy-start.13 = (f32[512]{0:T(512)S(1)}, f32[512]{0:T(512)}, u32[]{:S(2)}) copy-start(f32[512]{0:T(512)} %param.16) | copy-start | bytes 6148
  269.8 64.2 %copy-start.10 = (f32[1024]{0:T(1024)S(1)}, f32[1024]{0:T(1024)}, u32[]{:S(2)}) copy-start(f32[1024]{0:T(1024)} %param.14) | copy-start | bytes 12292
  340.7 635.8 %copy-start.9 = (f32[2048]{0:T(1024)S(1)}, f32[2048]{0:T(1024)}, u32[]{:S(2)}) copy-start(f32[2048]{0:T(1024)} %param.12) | copy-start | bytes 24580
  973.8 3.4 copy-start
Sparse Core Ops, SparseCore 0:
  16.5 80.0 all-gather.2
  166.6 158.7 all-reduce.2
  327.9 640.8 reduce-scatter.1
where the time goes:
time: 1000 us; the launch traced here: 994 us
  waiting for transfers between devices  691 us (69%)
  local copies, waits for them, and re-layouts  156 us (16%)
  other arithmetic  67.1 us (7%)
  matrix products  42.2 us (4%)
  starting transfers between devices  23.7 us (2%)
  between operations  14.6 us (1%)
    reduce_scatter x1, waiting for transfers between devices, body(): lax.psum_scatter(jnp.dot(grad_neg.T, queries, precision=highest, preferre...  617 us
    scatter x1, local copies, waits for them, and re-layouts, body(): slot_grads = jnp.zeros((shards, capacity, width), jnp.float32).at[owner_i...  63.9 us
    psum x1, waiting for transfers between devices, body(): hub_sum, relation_sum = lax.psum((hub_grad, relation_grad), 'shard')  55.6 us
    scatter x1, local copies, waits for them, and re-layouts, body(): jnp.zeros((shards, capacity), jnp.int32).at[owner_ids, slot_ids]  22 us
    unnamed x40, local copies, waits for them, and re-layouts  20.5 us
  transfers between devices with their start and end apart: 6, of which 4 were waited for; matrix products, arithmetic and copies ran while one was open for 19% of the time, Pallas kernels for 0%

commit v1 on v0

v1 whole, which is shorter than its diff:
```python
import jax
import jax.numpy as jnp
from jax import lax
from jax.experimental import pallas as pl
from jax.experimental.pallas import tpu as pltpu
from jax.sharding import Mesh, PartitionSpec as P

LEARN_RATE = 0.1
CHIPS = ("z", "x", "y")
SHARD = ("z", "x", "y", "core")
SIZES = (4, 4, 4, 2)
SWAP = [(0, 1), (1, 0)]
F32, BF16, I32 = jnp.float32, jnp.bfloat16, jnp.int32

WIDTH, HALF, SIDE, WIDE, AUX = 400, 200, 256, 512, 200
ENT, HUB, REL, TRIP, CHIP_COUNT, CAP, NEG = 2048, 1024, 512, 512, 64, 8, 16
SLOTS = 2 * CHIP_COUNT * CAP
HUB_OWN, REL_OWN, OWN = 8, 4, 16
VMEM = pl.BlockSpec(memory_space=pltpu.VMEM)
SMEM = pl.BlockSpec(memory_space=pltpu.SMEM)
LIMIT = 56 << 20


def params(**more):
    return pltpu.CompilerParams(vmem_limit_bytes=LIMIT, **more)


def cost(flops, nbytes):
    return pl.CostEstimate(flops=int(flops), bytes_accessed=int(nbytes), transcendentals=0)


def split(x):
    high = x.astype(BF16)
    return high, (x - high.astype(F32)).astype(BF16)


def dot(a, b, contract=((1,), (0,))):
    return lax.dot_general(a, b, (contract, ((), ())), preferred_element_type=F32)


def hot(condition):
    return jnp.where(condition, 1.0, 0.0).astype(BF16)


def iota(shape, axis):
    return lax.broadcasted_iota(I32, shape, axis)


def aux_column(rows):
    part = rows[:, 128:SIDE]
    return jnp.sum(jnp.where(iota(part.shape, 1) == AUX - 128, part, 0.0), axis=1, keepdims=True)


def without_aux(rows):
    return jnp.where(iota(rows.shape, 1) == AUX, 0.0, rows)


def widen(re, im, aux=None):
    n = re.shape[1]
    gap = jnp.zeros((SIDE - HALF, n), F32)
    if aux is not None:
        first = jnp.where(iota((8, n), 0) == 0, aux, 0.0)
        middle = jnp.concatenate([first, jnp.zeros((SIDE - HALF - 8, n), F32)], axis=0)
    else:
        middle = gap
    return jnp.concatenate([re, middle, im, gap], axis=0)


def pick_negatives(rows_ref, ent_ref, out_ref, held_ref):
    held_ref[...] = jnp.zeros_like(held_ref)
    lane = iota((WIDTH, 128), 1)
    for j in range(NEG):
        row = rows_ref[j]
        block = ent_ref[:, pl.ds(pl.multiple_of((row // 128) * 128, 128), 128)]
        block = pltpu.roll(block, (j - row % 128 + 128) % 128, 1)
        here = lane == j
        held_ref[0:HALF, :] = jnp.where(here[:HALF], block[:HALF], held_ref[0:HALF, :])
        held_ref[SIDE : SIDE + HALF, :] = jnp.where(
            here[:HALF], block[HALF:], held_ref[SIDE : SIDE + HALF, :]
        )
    out_ref[...] = held_ref[...].T[:NEG]


def prepare(head_ref, rel_ref, owner_ref, tail_ref, ent_ref, hub_ref, relt_ref,
            query_ref, headv_ref, relv_ref, sent_ref, place_ref):
    head = head_ref[...]

    def gather(table, ids):
        marks = hot(iota((table.shape[1], TRIP), 0) == ids)
        high, low = split(table)
        return dot(high, marks) + dot(low, marks)

    heads = gather(hub_ref[...], head) + gather(ent_ref[...], head - HUB)
    rels = gather(relt_ref[...], rel_ref[...])
    h_re, h_im, r_re, r_im = heads[:HALF], heads[HALF:], rels[:HALF], rels[HALF:]
    q_re = h_re * r_re - h_im * r_im
    q_im = h_re * r_im + h_im * r_re
    headv_ref[...] = widen(h_re, h_im).T
    relv_ref[...] = widen(r_re, r_im).T
    query_ref[...] = widen(q_re, q_im).T

    owner = owner_ref[...]
    owned = hot(iota((2 * CHIP_COUNT, TRIP), 0) == owner)
    before = hot(iota((TRIP, TRIP), 0) < iota((TRIP, TRIP), 1))
    rank = jnp.sum(dot(owned, before) * owned.astype(F32), axis=0, keepdims=True)
    place = owner * CAP + rank.astype(I32)
    place_ref[...] = jnp.broadcast_to(place.astype(F32), (128, TRIP)).T.astype(I32)

    marks = hot(iota((SLOTS, TRIP), 0) == place)
    high, low = split(widen(q_re, q_im, tail_ref[...].astype(F32) + 1.0).T)
    sent_ref[...] = dot(marks, high) + dot(marks, low)


def turn_tables(own_ref, ent_ref, hub_ref, relt_ref, hubacc_ref, relacc_ref,
                high_ref, low_ref, mine_ref, held_ref):
    for block in range(ENT // 512):
        part = ent_ref[:, block * 512 : (block + 1) * 512]
        high, low = split(widen(part[:HALF], part[HALF:]).T)
        high_ref[block * 512 : (block + 1) * 512, :] = high
        low_ref[block * 512 : (block + 1) * 512, :] = low
    own = own_ref[0]
    lane = iota((1, 128), 1)

    def rows_of(ref, first, at):
        block = ref[:, pl.ds(pl.multiple_of((first // 128) * 128, 128), 128)]
        return pltpu.roll(block, (at - first % 128 + 128) % 128, 1)

    hub = rows_of(hub_ref, own * HUB_OWN, 0)
    rel = rows_of(relt_ref, own * REL_OWN, HUB_OWN)
    hub_acc = rows_of(hubacc_ref, own * HUB_OWN, 0)
    rel_acc = rows_of(relacc_ref, own * REL_OWN, HUB_OWN)
    is_hub, is_rel = lane < HUB_OWN, (lane >= HUB_OWN) & (lane < HUB_OWN + REL_OWN)
    both = jnp.where(is_hub, hub, jnp.where(is_rel, rel, 0.0))
    acc = jnp.where(is_hub, hub_acc, jnp.where(is_rel, rel_acc, 1.0))
    held_ref[...] = widen(both[:HALF], both[HALF:], acc)
    mine_ref[...] = held_ref[...].T[:OWN]


def answer_queries(asked_ref, high_ref, low_ref, out_ref):
    asked = asked_ref[...]
    row = aux_column(asked).astype(I32) - 1
    marks = hot(iota((asked.shape[0], ENT), 1) == row)
    tails = dot(marks, high_ref[...]) + dot(marks, low_ref[...])
    positive = jnp.sum(asked * tails, axis=1, keepdims=True)
    slope = -jax.nn.sigmoid(-positive)
    out_ref[...] = jnp.where(iota(tails.shape, 1) == AUX, positive, slope * tails)


def score(core_ref, query_ref, neg_ref, mine_ref, other_ref, grad_ref, loss_ref,
          qh_ref, ql_ref, sum_ref):
    side, step = pl.program_id(0), pl.program_id(1)

    @pl.when((side == 0) & (step == 0))
    def _():
        high, low = split(query_ref[...])
        qh_ref[...] = high
        ql_ref[...] = low
        grad_ref[...] = jnp.zeros_like(grad_ref)
        sum_ref[...] = jnp.zeros_like(sum_ref)

    neg = neg_ref[...].reshape(-1, WIDE)
    nh, nl = split(neg)
    qh, ql = qh_ref[...], ql_ref[...]
    nt = ((1,), (1,))
    s = dot(qh, nh, nt) + (dot(qh, nl, nt) + dot(ql, nh, nt))
    small = jnp.exp(-jnp.abs(s))
    loss = jnp.maximum(s, 0.0) + jnp.log1p(small)
    total = sum_ref[...]
    for part in range(loss.shape[1] // 128):
        total = total + loss[:, part * 128 : (part + 1) * 128]
    sum_ref[...] = total
    weight = jnp.where(s >= 0.0, 1.0, small) / (1.0 + small) * (1.0 / (ENT_NEGS))
    gh, gl = split(weight)
    grad_ref[...] += dot(gh, nh) + (dot(gh, nl) + dot(gl, nh))
    tn = ((0,), (0,))
    back = (dot(gh, qh, tn) + (dot(gh, ql, tn) + dot(gl, qh, tn))).reshape(mine_ref.shape)

    @pl.when(side == 0)
    def _():
        mine_ref[...] = back

    @pl.when(side == 1)
    def _():
        other_ref[...] = back

    loss_ref[...] = total


ENT_NEGS = 2 * CHIP_COUNT * NEG


def close_triples(core_ref, back_ref, place_ref, headv_ref, relv_ref, gradq_ref, loss_ref,
                  head_ref, rel_ref, gradh_ref, mine_ref, other_ref, out_ref):
    place = place_ref[...]
    lane = iota((TRIP, 128), 1)
    marks = jnp.concatenate(
        [hot(place == lane + part * 128) for part in range(SLOTS // 128)], axis=1
    )
    high, low = split(back_ref[...])
    tail = dot(marks, high) + dot(marks, low)
    positive = aux_column(tail)
    neg_loss = jnp.sum(loss_ref[...], axis=1, keepdims=True) * (1.0 / ENT_NEGS)
    drop = -positive
    loss = jnp.maximum(drop, 0.0) + jnp.log1p(jnp.exp(-jnp.abs(drop))) + neg_loss
    out_ref[...] = jnp.broadcast_to(loss, (TRIP, 128)).T[:1]
    grad = without_aux(tail) + gradq_ref[...]
    g_re, g_im = grad[:, :SIDE], grad[:, SIDE:]
    heads, rels = headv_ref[...], relv_ref[...]
    h_re, h_im, r_re, r_im = heads[:, :SIDE], heads[:, SIDE:], rels[:, :SIDE], rels[:, SIDE:]
    gh = jnp.concatenate([g_re * r_re + g_im * r_im, g_im * r_re - g_re * r_im], axis=1)
    gr = jnp.concatenate([g_re * h_re + g_im * h_im, g_im * h_re - g_re * h_im], axis=1)
    gradh_ref[...] = gh

    core = core_ref[0]
    at = iota((2 * CHIP_COUNT * 8, TRIP), 0)
    head, rel = head_ref[...], rel_ref[...]
    hub_id = (at + core * (HUB // 2)) % HUB
    rel_id = (at // 8 * REL_OWN + at % 8 + core * (REL // 2)) % REL
    hub_marks = hot(hub_id == head)
    rel_marks = hot((rel_id == rel) & (at % 8 < REL_OWN))
    for first, marks, value in ((0, hub_marks, gh), (8, rel_marks, gr)):
        high, low = split(value)
        sums = (dot(marks, high) + dot(marks, low)).reshape(2, CHIP_COUNT, 8, WIDE)
        mine_ref[:, first : first + 8, :] = sums[0]
        other_ref[:, first : first + 8, :] = sums[1]


def add_pairs(a_ref, b_ref, c_ref, d_ref, out_ref):
    out_ref[:, :NEG, :] = a_ref[...] + b_ref[...]
    out_ref[:, NEG:, :] = c_ref[...] + d_ref[...]


def scatter_entities(head_ref, gradh_ref, asked_ref, answer_ref, out_ref,
                     th_ref, tl_ref, hh_ref, hl_ref, row_ref):
    @pl.when(pl.program_id(0) == 0)
    def _():
        asked = asked_ref[...]
        row_ref[...] = jnp.broadcast_to(aux_column(asked).astype(I32) - 1, (SLOTS, 128))
        slope = -jax.nn.sigmoid(-aux_column(answer_ref[...]))
        high, low = split((without_aux(asked) * slope).T)
        th_ref[...] = high
        tl_ref[...] = low
        high, low = split(gradh_ref[...].T)
        hh_ref[...] = high
        hl_ref[...] = low

    count = out_ref.shape[1]
    first = pl.program_id(0) * count
    rows = row_ref[...]
    lane = iota((SLOTS, 128), 1) + first
    marks = jnp.concatenate([hot(rows == lane + k * 128) for k in range(count // 128)], axis=1)
    grad = dot(th_ref[...], marks) + dot(tl_ref[...], marks)
    marks = hot(iota((count, TRIP), 0) + first == head_ref[...] - HUB)
    nt = ((1,), (1,))
    grad = grad + (dot(hh_ref[...], marks, nt) + dot(hl_ref[...], marks, nt))
    out_ref[:HALF, :] = grad[:HALF]
    out_ref[HALF:, :] = grad[SIDE : SIDE + HALF]


def update_own(sums_ref, mine_ref, neg_ref, out_ref):
    total = jnp.sum(sums_ref[...], axis=0)
    neg_ref[...] = total[:NEG]
    grad = total[NEG:]
    mine = mine_ref[...]
    accum = aux_column(mine) + jnp.sum(grad * grad, axis=1, keepdims=True) / WIDTH
    new = mine - LEARN_RATE * grad / jnp.sqrt(accum)
    new = jnp.where(iota(new.shape, 1) == AUX, accum, new)
    out_ref[...] = jnp.broadcast_to(new[None], out_ref.shape)


def place_new(core_ref, mine_ref, other_ref, hub_ref, hubacc_ref, rel_ref, relacc_ref, held_ref):
    core = core_ref[0]
    for part_ref, side in ((mine_ref, core), (other_ref, 1 - core)):
        hubs = part_ref[:, :HUB_OWN, :].reshape(HUB // 2, WIDE).T
        at = pl.ds(pl.multiple_of(side * (HUB // 2), 128), HUB // 2)
        hub_ref[:HALF, at] = hubs[:HALF]
        hub_ref[HALF:, at] = hubs[SIDE : SIDE + HALF]
        hubacc_ref[:, at] = hubs[AUX : AUX + 1]
        for chip in range(CHIP_COUNT):
            held_ref[chip * REL_OWN : (chip + 1) * REL_OWN, :] = part_ref[
                chip, HUB_OWN : HUB_OWN + REL_OWN, :
            ]
        rels = held_ref[...].T
        at = pl.ds(pl.multiple_of(side * (REL // 2), 128), REL // 2)
        rel_ref[:HALF, at] = rels[:HALF]
        rel_ref[HALF:, at] = rels[SIDE : SIDE + HALF]
        relacc_ref[:, at] = rels[AUX : AUX + 1]


def update_entities(rows_ref, neg_ref, ent_ref, acc_ref, grad_ref, new_ref, newacc_ref):
    count = ent_ref.shape[1]
    first = pl.program_id(0) * count
    rows = rows_ref[...][:, :1]
    marks = hot(iota((NEG, count), 1) + first == rows)
    high, low = split(neg_ref[...])
    tn = ((0,), (0,))
    more = dot(high, marks, tn) + dot(low, marks, tn)
    g_re = grad_ref[:HALF, :] + more[:HALF]
    g_im = grad_ref[HALF:, :] + more[SIDE : SIDE + HALF]
    square = jnp.sum(g_re * g_re, axis=0, keepdims=True) + jnp.sum(
        g_im * g_im, axis=0, keepdims=True
    )
    accum = acc_ref[...] + square / WIDTH
    newacc_ref[...] = accum
    root = jnp.sqrt(accum)
    new_ref[:HALF, :] = ent_ref[:HALF, :] - LEARN_RATE * g_re / root
    new_ref[HALF:, :] = ent_ref[HALF:, :] - LEARN_RATE * g_im / root


def shape(*dims, dtype=F32):
    return jax.ShapeDtypeStruct(dims, dtype)


def body(
    entity_table,
    entity_accum,
    hub_table,
    hub_accum,
    relation_table,
    relation_accum,
    head_ids,
    relation_ids,
    tail_owner,
    tail_rows,
    negative_rows,
):
    core = lax.axis_index("core").astype(I32)
    chip = lax.axis_index(CHIPS).astype(I32)
    core_arg = core.reshape(1)
    own_arg = (core * CHIP_COUNT + chip).reshape(1)
    ent_t, hub_t, rel_t = entity_table.T, hub_table.T, relation_table.T
    head_row, rel_row = head_ids.reshape(1, TRIP), relation_ids.reshape(1, TRIP)
    owner_row, tail_row = tail_owner.reshape(1, TRIP), tail_rows.reshape(1, TRIP)

    picked = pl.pallas_call(
        pick_negatives,
        out_shape=shape(NEG, WIDE),
        in_specs=[SMEM, VMEM],
        out_specs=VMEM,
        scratch_shapes=[pltpu.VMEM((WIDE, 128), F32)],
        compiler_params=params(),
        name="pick_negatives",
    )(negative_rows, ent_t)
    negs = lax.all_gather(picked, SHARD, axis=0, tiled=True)

    query, heads, rels, sent, place = pl.pallas_call(
        prepare,
        out_shape=[
            shape(TRIP, WIDE), shape(TRIP, WIDE), shape(TRIP, WIDE), shape(SLOTS, WIDE),
            shape(TRIP, 128, dtype=I32),
        ],
        in_specs=[VMEM] * 7,
        out_specs=[VMEM] * 5,
        compiler_params=params(),
        name="prepare",
    )(head_row, rel_row, owner_row, tail_row, ent_t, hub_t, rel_t)

    def exchange(rows):
        parts = rows.reshape(2 * CHIP_COUNT, CAP, WIDE)
        got = lax.all_to_all(parts, SHARD, split_axis=0, concat_axis=0, tiled=True)
        return got.reshape(SLOTS, WIDE)

    asked = exchange(sent)
    ent_high, ent_low, mine_rows = pl.pallas_call(
        turn_tables,
        out_shape=[
            shape(ENT, WIDE, dtype=BF16), shape(ENT, WIDE, dtype=BF16), shape(OWN, WIDE)
        ],
        in_specs=[SMEM] + [VMEM] * 5,
        out_specs=[VMEM] * 3,
        scratch_shapes=[pltpu.VMEM((WIDE, 128), F32)],
        compiler_params=params(),
        cost_estimate=cost(1e6, 12e6),
        name="turn_tables",
    )(own_arg, ent_t, hub_t, rel_t, hub_accum.reshape(1, HUB), relation_accum.reshape(1, REL))

    rows = 256
    answer = pl.pallas_call(
        answer_queries,
        out_shape=shape(SLOTS, WIDE),
        grid=(SLOTS // rows,),
        in_specs=[pl.BlockSpec((rows, WIDE), lambda i: (i, 0)), VMEM, VMEM],
        out_specs=pl.BlockSpec((rows, WIDE), lambda i: (i, 0)),
        compiler_params=params(),
        name="answer_queries",
    )(asked, ent_high, ent_low)
    back = exchange(answer)

    group = 16
    steps = CHIP_COUNT // group
    neg_mine, neg_other, grad_q, loss_sum = pl.pallas_call(
        score,
        out_shape=[
            shape(CHIP_COUNT, NEG, WIDE), shape(CHIP_COUNT, NEG, WIDE), shape(TRIP, WIDE),
            shape(TRIP, 128),
        ],
        grid_spec=pltpu.PrefetchScalarGridSpec(
            num_scalar_prefetch=1,
            grid=(2, steps),
            in_specs=[
                pl.BlockSpec((TRIP, WIDE), lambda i, c, core: (0, 0)),
                pl.BlockSpec(
                    (group, 1, NEG, WIDE), lambda i, c, core: (c, (i + core[0]) % 2, 0, 0)
                ),
            ],
            out_specs=[
                pl.BlockSpec(
                    (group, NEG, WIDE), lambda i, c, core: (jnp.where(i == 0, c, steps - 1), 0, 0)
                ),
                pl.BlockSpec(
                    (group, NEG, WIDE), lambda i, c, core: (jnp.where(i == 0, 0, c), 0, 0)
                ),
                pl.BlockSpec((TRIP, WIDE), lambda i, c, core: (0, 0)),
                pl.BlockSpec((TRIP, 128), lambda i, c, core: (0, 0)),
            ],
            scratch_shapes=[
                pltpu.VMEM((TRIP, WIDE), BF16), pltpu.VMEM((TRIP, WIDE), BF16),
                pltpu.VMEM((TRIP, 128), F32),
            ],
        ),
        compiler_params=params(),
        cost_estimate=cost(20e9, 12e6),
        name="score",
    )(core_arg, query, negs.reshape(CHIP_COUNT, 2, NEG, WIDE))
    neg_swapped = lax.ppermute(neg_other, "core", SWAP)

    grad_head, both_mine, both_other, loss = pl.pallas_call(
        close_triples,
        out_shape=[
            shape(TRIP, WIDE), shape(CHIP_COUNT, OWN, WIDE), shape(CHIP_COUNT, OWN, WIDE),
            shape(1, TRIP),
        ],
        in_specs=[SMEM] + [VMEM] * 8,
        out_specs=[VMEM] * 4,
        compiler_params=params(),
        name="close_triples",
    )(core_arg, back, place, heads, rels, grad_q, loss_sum, head_row, rel_row)
    both_swapped = lax.ppermute(both_other, "core", SWAP)

    block = pl.BlockSpec((8, NEG, WIDE), lambda i: (i, 0, 0))
    paired = pl.pallas_call(
        add_pairs,
        out_shape=shape(CHIP_COUNT, NEG + OWN, WIDE),
        grid=(CHIP_COUNT // 8,),
        in_specs=[block] * 4,
        out_specs=pl.BlockSpec((8, NEG + OWN, WIDE), lambda i: (i, 0, 0)),
        compiler_params=params(),
        name="add_pairs",
    )(neg_mine, neg_swapped, both_mine, both_swapped)
    sums = lax.all_to_all(paired, CHIPS, split_axis=0, concat_axis=0, tiled=True)

    columns = 256
    whole = pl.BlockSpec((SLOTS, WIDE), lambda i: (0, 0))
    entity_grad = pl.pallas_call(
        scatter_entities,
        out_shape=shape(WIDTH, ENT),
        grid=(ENT // columns,),
        in_specs=[
            pl.BlockSpec((1, TRIP), lambda i: (0, 0)),
            pl.BlockSpec((TRIP, WIDE), lambda i: (0, 0)),
            whole,
            whole,
        ],
        out_specs=pl.BlockSpec((WIDTH, columns), lambda i: (0, i)),
        scratch_shapes=[
            pltpu.VMEM((WIDE, SLOTS), BF16), pltpu.VMEM((WIDE, SLOTS), BF16),
            pltpu.VMEM((WIDE, TRIP), BF16), pltpu.VMEM((WIDE, TRIP), BF16),
            pltpu.VMEM((SLOTS, 128), I32),
        ],
        compiler_params=params(),
        cost_estimate=cost(10e9, 12e6),
        name="scatter_entities",
    )(head_row, grad_head, asked, answer)

    neg_grad, own_new = pl.pallas_call(
        update_own,
        out_shape=[shape(NEG, WIDE), shape(CHIP_COUNT, OWN, WIDE)],
        in_specs=[VMEM] * 2,
        out_specs=[VMEM] * 2,
        compiler_params=params(),
        name="update_own",
    )(sums, mine_rows)
    new_mine = lax.all_to_all(own_new, CHIPS, split_axis=0, concat_axis=0, tiled=True)
    new_other = lax.ppermute(new_mine, "core", SWAP)

    columns = 512
    entity_new, entity_accum_new = pl.pallas_call(
        update_entities,
        out_shape=[shape(WIDTH, ENT), shape(1, ENT)],
        grid=(ENT // columns,),
        in_specs=[
            pl.BlockSpec((NEG, 128), lambda i: (0, 0)),
            pl.BlockSpec((NEG, WIDE), lambda i: (0, 0)),
            pl.BlockSpec((WIDTH, columns), lambda i: (0, i)),
            pl.BlockSpec((1, columns), lambda i: (0, i)),
            pl.BlockSpec((WIDTH, columns), lambda i: (0, i)),
        ],
        out_specs=[
            pl.BlockSpec((WIDTH, columns), lambda i: (0, i)),
            pl.BlockSpec((1, columns), lambda i: (0, i)),
        ],
        compiler_params=params(),
        cost_estimate=cost(1e9, 14e6),
        name="update_entities",
    )(
        jnp.broadcast_to(negative_rows[:, None], (NEG, 128)),
        neg_grad,
        ent_t,
        entity_accum.reshape(1, ENT),
        entity_grad,
    )

    hub_new, hub_accum_new, rel_new, rel_accum_new = pl.pallas_call(
        place_new,
        out_shape=[shape(WIDTH, HUB), shape(1, HUB), shape(WIDTH, REL), shape(1, REL)],
        in_specs=[SMEM, VMEM, VMEM],
        out_specs=[VMEM] * 4,
        scratch_shapes=[pltpu.VMEM((REL // 2, WIDE), F32)],
        compiler_params=params(),
        name="place_new",
    )(core_arg, new_mine, new_other)
    return (
        entity_new.T,
        entity_accum_new.reshape(ENT),
        hub_new.T,
        hub_accum_new.reshape(HUB),
        rel_new.T,
        rel_accum_new.reshape(REL),
        loss.reshape(TRIP),
    )


def solution(mesh):
    fine = Mesh(mesh.devices.reshape(SIZES), SHARD)
    rows, vector = P(SHARD, None), P(SHARD)
    placed = (rows, vector, P(), P(), P(), P(), vector, vector, rows, vector, vector)
    return jax.shard_map(
        body,
        mesh=fine,
        in_specs=placed,
        out_specs=(rows, vector, P(), P(), P(), P(), vector),
        check_vma=False,
    )
```

time: 1000 us -> 291 us (0.29)
  waiting for transfers between devices: 691 us -> 55.8 us
  local copies, waits for them, and re-layouts: 156 us -> 6.05 us
  blocking collectives: 0 us -> 101 us
  Pallas kernels: 0 us -> 96.2 us
  other arithmetic: 67.1 us -> 0 us
  matrix products: 42.2 us -> 0 us
    reduce_scatter x1 -> x0, waiting for transfers between devices: 617 us -> none  [body(): lax.psum_scatter(jnp.dot(grad_neg.T, queries, precision=highest, preferre...]
    all_to_all x0 -> x2, blocking collectives: none -> 101 us  [the longest x1 66.2 us: body(): lax.all_to_all(paired, CHIPS, split_axis=0, concat_axis=0, tiled=True)]
    pallas_call x0 -> x11, Pallas kernels: none -> 96.2 us  [the longest x1 24 us: body(): pl.pallas_call(score, out_shape=[shape(CHIP_COUNT, NEG, WIDE), shape(CHIP...]
    scatter x2 -> x0, local copies, waits for them, and re-layouts: 85.9 us -> none  [the longest x1 63.9 us: body(): slot_grads = jnp.zeros((shards, capacity, width), jnp.float32).at[owner_i...]
    psum x1 -> x0, waiting for transfers between devices: 55.6 us -> none  [body(): hub_sum, relation_sum = lax.psum((hub_grad, relation_grad), 'shard')]
    dot_general x3 -> x0, matrix products: 42.2 us -> none  [the longest x1 17.1 us: body(): jnp.dot(queries, neg_vecs.T, precision=highest, preferred_element_type=jn...]
    gather x9 -> x0, local copies, waits for them, and re-layouts: 36.1 us -> none  [the longest x2 11.4 us: body(): tail_vecs = fetched[owner_ids, slot_ids]]
    scatter-add x5 -> x0, other arithmetic: 34.1 us -> none  [the longest x1 11.5 us: body(): entity_grad.at[asked_rows.reshape(-1)].add(owned_grads.reshape(-1, width))]
  transfers between devices with their start and end apart: 6 -> 6, of which waited for: 4 -> 4; matrix products, arithmetic and copies ran while one was open for 19% -> 0% of each run, Pallas kernels for 0% -> 24%
where the time goes in v1:
time: 291 us; the launch traced here: 290 us
  blocking collectives  101 us (35%)
  Pallas kernels  96.2 us (33%)
  waiting for transfers between devices  55.8 us (19%)
  starting transfers between devices  16.5 us (6%)
  between operations  14.1 us (5%)
  local copies, waits for them, and re-layouts  6.05 us (2%)
    all_to_all x1, blocking collectives, body(): lax.all_to_all(paired, CHIPS, split_axis=0, concat_axis=0, tiled=True)  66.2 us
    all_to_all x1, blocking collectives, body(): lax.all_to_all(own_new, CHIPS, split_axis=0, concat_axis=0, tiled=True)  35 us
    all_to_all x2, waiting for transfers between devices, exchange(): got = lax.all_to_all(parts, SHARD, split_axis=0, concat_axis=0, tiled=True)  24.9 us
    pallas_call x1, Pallas kernels, body(): pl.pallas_call(score, out_shape=[shape(CHIP_COUNT, NEG, WIDE), shape(CHIP...  24 us
    all_gather x1, waiting for transfers between devices, body(): negs = lax.all_gather(picked, SHARD, axis=0, tiled=True)  23.9 us
    all_to_all x2, starting transfers between devices, exchange(): got = lax.all_to_all(parts, SHARD, split_axis=0, concat_axis=0, tiled=True)  16 us
    pallas_call x1, Pallas kernels, body(): pl.pallas_call(scatter_entities, out_shape=shape(WIDTH, ENT), grid=(ENT /...  13.6 us
    pallas_call x1, Pallas kernels, body(): pl.pallas_call(prepare, out_shape=[shape(TRIP, WIDE), shape(TRIP, WIDE),...  9.36 us
  transfers between devices with their start and end apart: 6, of which 4 were waited for; matrix products, arithmetic and copies ran while one was open for 0% of the time, Pallas kernels for 24%

profile of v1, /device:TPU:0, one launch (start us, length us, event | category | flops | bytes accessed | tf_op | source)
XLA Modules:
  0.0 289.8 jit_solution(18093224683377931025)
XLA Ops:
  7.2 0.0 all-gather.2.cloned.1.call-start
  7.2 3.5 %pick_negatives.1 = f32[16,512]{1,0:T(8,128)} custom-call(s32[16]{0:T(128)} %rows_ref.1, f32[400,2048]{1,0:T(8,128)} %bitcast.24), custom_call_target="tpu_custom_call" | custom-call | tf_op jit(solution)/shard_map/pick_negatives/pallas_call | solution.py:335
  10.8 0.0 all-gather.2.cloned.1.call-update
  10.8 9.4 %prepare.1 = (f32[512,512]{1,0:T(8,128)}, f32[512,512]{1,0:T(8,128)}, f32[512,512]{1,0:T(8,128)}, f32[1024,512]{1,0:T(8,128)}, s32[512,128]{1,0:T(8,128)}) custom-call(s32[1,512]{1,0:T(1,128)} %bitcast.40, s32[1,512]{1,0:T(1,128)} %bitcast.38, s32[1,512]{1,0:T(1,128)} %bitcast.44, s32[1,512]{1,0:T(1,128)} %bitcast.45, f32[400,2048]{1,0:T(8,128)} %bitcast.25, ...), custom_call_target="tpu_custom_call" | custom-call | tf_op jit(solution)/shard_map/prepare/pallas_call | solution.py:346
  20.1 11.1 %all-to-all-start = ((f32[128,8,512]{2,1,0:T(8,128)}), f32[128,8,512]{2,1,0:T(8,128)S(1)}, u32[]{:S(2)}, u32[]{:S(2)}) async-start(f32[128,8,512]{2,1,0:T(8,128)} %bitcast.36), calls=%async_computation | async-start | bytes 4194304 | tf_op jit(solution)/shard_map/all_to_all | solution.py:360
  31.3 5.9 %turn_tables.1 = (bf16[2048,512]{1,0:T(8,128)(2,1)}, bf16[2048,512]{1,0:T(8,128)(2,1)}, f32[16,512]{1,0:T(8,128)}) custom-call(s32[1]{0:T(128)} %bitcast.11.own_ref, f32[400,2048]{1,0:T(8,128)} %bitcast.26, f32[400,1024]{1,0:T(8,128)} %bitcast.33, f32[400,512]{1,0:T(8,128)} %bitcast.35, f32[1,1024]{1,0:T(1,128)} %bitcast.43, f32[1,512]{1,0:T(1,128)} %bitcast.46), custom_call_target="tpu_custom_call" | custom-call | flops 1000000 | bytes 12000000 | tf_op jit(solution)/shard_map/turn_tables/pallas_call | solution.py:364
  37.2 24.9 %all-to-all-done = f32[128,8,512]{2,1,0:T(8,128)S(1)} async-done(((f32[128,8,512]{2,1,0:T(8,128)}), f32[128,8,512]{2,1,0:T(8,128)S(1)}, u32[]{:S(2)}, u32[]{:S(2)}) %all-to-all-start) | async-done | bytes 2097184 | tf_op jit(solution)/shard_map/all_to_all | solution.py:360
  62.2 1.4 copy-done.1
  63.6 8.9 %answer_queries.1.answer_ref = f32[1024,512]{1,0:T(8,128)} custom-call(f32[1024,512]{1,0:T(8,128)} %bitcast.28, bf16[2048,512]{1,0:T(8,128)(2,1)} %get-tuple-element.35.high_ref, bf16[2048,512]{1,0:T(8,128)(2,1)} %get-tuple-element.36.low_ref), custom_call_target="tpu_custom_call" | custom-call | tf_op jit(solution)/shard_map/answer_queries/pallas_call | solution.py:378
  72.5 4.8 %all-to-all-start.1 = ((f32[128,8,512]{2,1,0:T(8,128)}), f32[128,8,512]{2,1,0:T(8,128)S(1)}, u32[]{:S(2)}, u32[]{:S(2)}) async-start(f32[128,8,512]{2,1,0:T(8,128)} %bitcast.30), calls=%async_computation.1 | async-start | bytes 4194304 | tf_op jit(solution)/shard_map/all_to_all | solution.py:360
  77.3 23.9 %all-gather.2.cloned.1.call-done = f32[2048,512]{1,0:T(8,128)} async-done(((f32[16,512]{1,0:T(8,128)}), f32[2048,512]{1,0:T(8,128)}) %all-gather.2.cloned.1.call-update) | async-done | bytes 4194320 | tf_op jit(solution)/shard_map/all_gather | solution.py:344
  101.2 24.0 %score.1 = (f32[64,16,512]{2,1,0:T(8,128)}, f32[64,16,512]{2,1,0:T(8,128)}, f32[512,512]{1,0:T(8,128)}, f32[512,128]{1,0:T(8,128)}) custom-call(s32[1]{0:T(128)} %bitcast.core_ref, f32[512,512]{1,0:T(8,128)} %get-tuple-element.31.query_ref, f32[64,2,16,512]{3,2,1,0:T(8,128)} %bitcast.47), custom_call_target="tpu_custom_call" | custom-call | flops 20000000000 | bytes 12000000 | tf_op jit(solution)/shard_map/score/pallas_call | solution.py:391
  125.3 0.0 all-to-all-done.1
  125.3 1.3 copy-done.2
  126.6 8.5 %close_triples.1 = (f32[512,512]{1,0:T(8,128)}, f32[64,16,512]{2,1,0:T(8,128)}, f32[64,16,512]{2,1,0:T(8,128)}, f32[1,512]{1,0:T(1,128)}) custom-call(s32[1]{0:T(128)} %bitcast.core_ref, f32[1024,512]{1,0:T(8,128)} %bitcast.31, s32[512,128]{1,0:T(8,128)} %get-tuple-element.37.place_ref, f32[512,512]{1,0:T(8,128)} %get-tuple-element.38.headv_ref, ...), custom_call_target="tpu_custom_call" | custom-call | tf_op jit(solution)/shard_map/close_triples/pallas_call | solution.py:427
  135.2 0.3 collective-permute-start.1
  135.4 0.3 collective-permute-start
  135.7 3.9 %collective-permute-done.1.d_ref = f32[64,16,512]{2,1,0:T(8,128)S(1)} collective-permute-done((f32[64,16,512]{2,1,0:T(8,128)}, f32[64,16,512]{2,1,0:T(8,128)S(1)}, u32[]{:S(2)}, u32[]{:S(2)}) %collective-permute-start.1) | collective-permute-done | bytes 2097184 | tf_op jit(solution)/shard_map/ppermute | solution.py:438
  139.5 3.0 %collective-permute-done.b_ref = f32[64,16,512]{2,1,0:T(8,128)S(1)} collective-permute-done((f32[64,16,512]{2,1,0:T(8,128)}, f32[64,16,512]{2,1,0:T(8,128)S(1)}, u32[]{:S(2)}, u32[]{:S(2)}) %collective-permute-start) | collective-permute-done | bytes 2097184 | tf_op jit(solution)/shard_map/ppermute | solution.py:425
  142.5 1.3 copy-done.5
  143.9 7.5 %add_pairs.1 = f32[64,32,512]{2,1,0:T(8,128)} custom-call(f32[64,16,512]{2,1,0:T(8,128)} %get-tuple-element.32.a_ref, f32[64,16,512]{2,1,0:T(8,128)} %copy-done.5, f32[64,16,512]{2,1,0:T(8,128)} %get-tuple-element.42.c_ref, f32[64,16,512]{2,1,0:T(8,128)} %copy-done.4), custom_call_target="tpu_custom_call" | custom-call | tf_op jit(solution)/shard_map/add_pairs/pallas_call | solution.py:441
  151.4 66.2 %all_to_all.20.sums_ref = f32[64,32,512]{2,1,0:T(8,128)} all-to-all(f32[64,32,512]{2,1,0:T(8,128)} %add_pairs.1), channel_id=1, replica_groups=mesh['z'=4,'x'=4,'y'=4,'core'=2] {'z','x','y'}, dimensions={0} | all-to-all | bytes 8388608 | tf_op jit(solution)/shard_map/all_to_all | solution.py:450
  217.6 3.9 %update_own.1 = (f32[16,512]{1,0:T(8,128)}, f32[64,16,512]{2,1,0:T(8,128)}) custom-call(f32[64,32,512]{2,1,0:T(8,128)} %all_to_all.20.sums_ref, f32[16,512]{1,0:T(8,128)} %get-tuple-element.44.mine_ref), custom_call_target="tpu_custom_call" | custom-call | tf_op jit(solution)/shard_map/update_own/pallas_call | solution.py:475
  221.5 35.0 %all_to_all.21.mine_ref = f32[64,16,512]{2,1,0:T(8,128)S(1)} all-to-all(f32[64,16,512]{2,1,0:T(8,128)} %get-tuple-element.49), channel_id=1, replica_groups=mesh['z'=4,'x'=4,'y'=4,'core'=2] {'z','x','y'}, dimensions={0} | all-to-all | bytes 4194304 | tf_op jit(solution)/shard_map/all_to_all | solution.py:483
  256.5 0.0 collective-permute-start.2
  256.5 13.6 %scatter_entities.1.grad_ref = f32[400,2048]{1,0:T(8,128)} custom-call(s32[1,512]{1,0:T(1,128)} %bitcast.42, f32[512,512]{1,0:T(8,128)} %get-tuple-element.46.gradh_ref, f32[1024,512]{1,0:T(8,128)} %bitcast.29, f32[1024,512]{1,0:T(8,128)} %answer_queries.1.answer_ref), custom_call_target="tpu_custom_call" | custom-call | flops 10000000000 | bytes 12000000 | tf_op jit(solution)/shard_map/scatter_entities/pallas_call | solution.py:454
  270.1 0.7 broadcast_in_dim.2.rows_ref
  270.8 6.4 %update_entities.1 = (f32[400,2048]{1,0:T(8,128)}, f32[1,2048]{1,0:T(1,128)}) custom-call(s32[16,128]{1,0:T(8,128)} %broadcast_in_dim.2.rows_ref, f32[16,512]{1,0:T(8,128)} %get-tuple-element.45.neg_ref, f32[400,2048]{1,0:T(8,128)} %bitcast.27, f32[1,2048]{1,0:T(1,128)} %bitcast.37, f32[400,2048]{1,0:T(8,128)} %scatter_entities.1.grad_ref), custom_call_target="tpu_custom_call" | custom-call | flops 1000000000 | bytes 14000000 | tf_op jit(solution)/shard_map/update_entities/pallas_call | solution.py:487
  277.1 0.0 collective-permute-done.2.other_ref
  277.2 0.0 copy-start.3
  277.2 1.3 copy-done.3
  278.5 4.5 %place_new.1 = (f32[400,1024]{1,0:T(8,128)}, f32[1,1024]{1,0:T(1,128)}, f32[400,512]{1,0:T(8,128)}, f32[1,512]{1,0:T(1,128)}) custom-call(s32[1]{0:T(128)} %bitcast.core_ref, f32[64,16,512]{2,1,0:T(8,128)} %copy-done, f32[64,16,512]{2,1,0:T(8,128)} %copy-done.3), custom_call_target="tpu_custom_call" | custom-call | tf_op jit(solution)/shard_map/place_new/pallas_call | solution.py:513
  (9 shorter events, 0.0 us)
Async XLA Ops:
  7.2 94.1 %all-gather.2.cloned.1.call-start = ((), (), s32[]{:S(2)}) async-start(), calls=%async_computation.4 | async-start | bytes 4227072 | tf_op jit(solution)/shard_map/all_gather | solution.py:344
  20.1 42.0 %all-to-all-start = ((f32[128,8,512]{2,1,0:T(8,128)}), f32[128,8,512]{2,1,0:T(8,128)S(1)}, u32[]{:S(2)}, u32[]{:S(2)}) async-start(f32[128,8,512]{2,1,0:T(8,128)} %bitcast.36), calls=%async_computation | async-start | bytes 4194304 | tf_op jit(solution)/shard_map/all_to_all | solution.py:360
  62.2 1.4 copy-start.1
  72.5 52.8 %all-to-all-start.1 = ((f32[128,8,512]{2,1,0:T(8,128)}), f32[128,8,512]{2,1,0:T(8,128)S(1)}, u32[]{:S(2)}, u32[]{:S(2)}) async-start(f32[128,8,512]{2,1,0:T(8,128)} %bitcast.30), calls=%async_computation.1 | async-start | bytes 4194304 | tf_op jit(solution)/shard_map/all_to_all | solution.py:360
  125.3 1.3 copy-start.2
  135.2 4.4 %collective-permute-start.1 = (f32[64,16,512]{2,1,0:T(8,128)}, f32[64,16,512]{2,1,0:T(8,128)S(1)}, u32[]{:S(2)}, u32[]{:S(2)}) collective-permute-start(f32[64,16,512]{2,1,0:T(8,128)} %get-tuple-element.43), channel_id=1, source_target_pairs={{0,1},{1,0},{2,3},{3,2},{4,5},{5,4},{6,7},{7,6},{8,9},{9,8},{10,11... | collective-permute-start | bytes 6291464 | tf_op jit(solution)/shard_map/ppermute | solution.py:438
  135.4 7.1 %collective-permute-start = (f32[64,16,512]{2,1,0:T(8,128)}, f32[64,16,512]{2,1,0:T(8,128)S(1)}, u32[]{:S(2)}, u32[]{:S(2)}) collective-permute-start(f32[64,16,512]{2,1,0:T(8,128)} %get-tuple-element.33), channel_id=1, source_target_pairs={{0,1},{1,0},{2,3},{3,2},{4,5},{5,4},{6,7},{7,6},{8,9},{9,8},{10,11... | collective-permute-start | bytes 6291464 | tf_op jit(solution)/shard_map/ppermute | solution.py:425
  139.5 3.0 %copy-start.4 = (f32[64,16,512]{2,1,0:T(8,128)}, f32[64,16,512]{2,1,0:T(8,128)S(1)}, u32[]{:S(2)}) copy-start(f32[64,16,512]{2,1,0:T(8,128)S(1)} %collective-permute-done.1.d_ref) | copy-start | bytes 6291460
  142.5 1.3 copy-start.5
  256.5 13.6 %copy-start = (f32[64,16,512]{2,1,0:T(8,128)}, f32[64,16,512]{2,1,0:T(8,128)S(1)}, u32[]{:S(2)}) copy-start(f32[64,16,512]{2,1,0:T(8,128)S(1)} %all_to_all.21.mine_ref) | copy-start | bytes 6291460
  256.5 20.7 %collective-permute-start.2 = (f32[64,16,512]{2,1,0:T(8,128)S(1)}, f32[64,16,512]{2,1,0:T(8,128)S(1)}, u32[]{:S(2)}, u32[]{:S(2)}) collective-permute-start(f32[64,16,512]{2,1,0:T(8,128)S(1)} %all_to_all.21.mine_ref), channel_id=1, source_target_pairs={{0,1},{1,0},{2,3},{3,2},{4,5},{5,4},{6,7},{7,6},{8,9},{9,8},{10,11... | collective-permute-start | bytes 6291464 | tf_op jit(solution)/shard_map/ppermute | solution.py:484
  256.5 13.6 %copy-start.6 = (s32[16]{0:T(128)S(1)}, s32[16]{0:T(128)}, u32[]{:S(2)}) copy-start(s32[16]{0:T(128)} %rows_ref.1) | copy-start | bytes 196
  277.2 1.3 copy-start.3
Sparse Core Ops, SparseCore 0:
  11.1 90.0 all-gather.1

commit v2 on v1

--- a/solution.py
+++ b/solution.py
@@ -15,14 +15,13 @@
 WIDTH, HALF, SIDE, WIDE, AUX = 400, 200, 256, 512, 200
 ENT, HUB, REL, TRIP, CHIP_COUNT, CAP, NEG = 2048, 1024, 512, 512, 64, 8, 16
 SLOTS = 2 * CHIP_COUNT * CAP
-HUB_OWN, REL_OWN, OWN = 8, 4, 16
+HUB_OWN, REL_OWN, OWN = 8, 4, 40
 VMEM = pl.BlockSpec(memory_space=pltpu.VMEM)
 SMEM = pl.BlockSpec(memory_space=pltpu.SMEM)
-LIMIT = 56 << 20
-
-
-def params(**more):
-    return pltpu.CompilerParams(vmem_limit_bytes=LIMIT, **more)
+
+
+def params(mib):
+    return pltpu.CompilerParams(vmem_limit_bytes=mib << 20)
 
 
 def cost(flops, nbytes):
@@ -133,7 +132,28 @@
     both = jnp.where(is_hub, hub, jnp.where(is_rel, rel, 0.0))
     acc = jnp.where(is_hub, hub_acc, jnp.where(is_rel, rel_acc, 1.0))
     held_ref[...] = widen(both[:HALF], both[HALF:], acc)
-    mine_ref[...] = held_ref[...].T[:OWN]
+    held_ref[SIDE + HALF : SIDE + HALF + 8, :] = jnp.broadcast_to(acc, (8, 128))
+    rows = held_ref[...].T
+    rel = rows[HUB_OWN : HUB_OWN + 8]
+    rel = jnp.where(iota(rel.shape, 0) < REL_OWN, rel, pltpu.roll(rel, REL_OWN, 0))
+    for k, tile in enumerate(pack(rows[:HUB_OWN], rel)):
+        mine_ref[k * 8 : (k + 1) * 8, :] = tile
+
+
+def pack(hub, rel):
+    lane, low = iota((hub.shape[0], 128), 1), iota((hub.shape[0], 128), 0) % 8 < REL_OWN
+    hubs = [hub[:, k * 128 : (k + 1) * 128] for k in range(4)]
+    rels = [rel[:, k * 128 : (k + 1) * 128] for k in range(4)]
+    turned = pltpu.roll(hubs[3], 72, 1)
+    tail = pltpu.roll(jnp.where(low, rels[1], rels[3]), 16, 1)
+    last = jnp.where(lane < 16, turned, jnp.where(lane < 89, tail, pltpu.roll(hubs[1], 17, 1)))
+    return (
+        hubs[0],
+        hubs[2],
+        jnp.where(low, rels[0], rels[2]),
+        jnp.where(lane < 72, hubs[1], turned),
+        jnp.where(lane < 90, last, 0.0),
+    )
 
 
 def answer_queries(asked_ref, high_ref, low_ref, out_ref):
@@ -146,43 +166,24 @@
     out_ref[...] = jnp.where(iota(tails.shape, 1) == AUX, positive, slope * tails)
 
 
-def score(core_ref, query_ref, neg_ref, mine_ref, other_ref, grad_ref, loss_ref,
-          qh_ref, ql_ref, sum_ref):
-    side, step = pl.program_id(0), pl.program_id(1)
-
-    @pl.when((side == 0) & (step == 0))
-    def _():
-        high, low = split(query_ref[...])
-        qh_ref[...] = high
-        ql_ref[...] = low
-        grad_ref[...] = jnp.zeros_like(grad_ref)
-        sum_ref[...] = jnp.zeros_like(sum_ref)
-
-    neg = neg_ref[...].reshape(-1, WIDE)
-    nh, nl = split(neg)
-    qh, ql = qh_ref[...], ql_ref[...]
-    nt = ((1,), (1,))
-    s = dot(qh, nh, nt) + (dot(qh, nl, nt) + dot(ql, nh, nt))
-    small = jnp.exp(-jnp.abs(s))
-    loss = jnp.maximum(s, 0.0) + jnp.log1p(small)
-    total = sum_ref[...]
-    for part in range(loss.shape[1] // 128):
-        total = total + loss[:, part * 128 : (part + 1) * 128]
-    sum_ref[...] = total
-    weight = jnp.where(s >= 0.0, 1.0, small) / (1.0 + small) * (1.0 / (ENT_NEGS))
-    gh, gl = split(weight)
-    grad_ref[...] += dot(gh, nh) + (dot(gh, nl) + dot(gl, nh))
-    tn = ((0,), (0,))
-    back = (dot(gh, qh, tn) + (dot(gh, ql, tn) + dot(gl, qh, tn))).reshape(mine_ref.shape)
-
-    @pl.when(side == 0)
-    def _():
-        mine_ref[...] = back
-
-    @pl.when(side == 1)
-    def _():
-        other_ref[...] = back
-
+def score(query_ref, neg_ref, grad_in, loss_in, back_ref, grad_ref, loss_ref):
+    qh, ql = split(query_ref[...])
+    grad, total = grad_in[...], loss_in[...]
+    step = 256
+    for first in range(0, neg_ref.shape[0], step):
+        nh, nl = split(neg_ref[first : first + step, :])
+        nt = ((1,), (1,))
+        s = dot(qh, nh, nt) + (dot(qh, nl, nt) + dot(ql, nh, nt))
+        small = jnp.exp(-jnp.abs(s))
+        loss = jnp.maximum(s, 0.0) + jnp.log1p(small)
+        for part in range(step // 128):
+            total = total + loss[:, part * 128 : (part + 1) * 128]
+        weight = jnp.where(s >= 0.0, 1.0, small) / (1.0 + small) * (1.0 / ENT_NEGS)
+        gh, gl = split(weight)
+        grad = grad + (dot(gh, nh) + (dot(gh, nl) + dot(gl, nh)))
+        tn = ((0,), (0,))
+        back_ref[first : first + step, :] = dot(gh, qh, tn) + (dot(gh, ql, tn) + dot(gl, qh, tn))
+    grad_ref[...] = grad
     loss_ref[...] = total
 
 
@@ -215,19 +216,15 @@
     at = iota((2 * CHIP_COUNT * 8, TRIP), 0)
     head, rel = head_ref[...], rel_ref[...]
     hub_id = (at + core * (HUB // 2)) % HUB
-    rel_id = (at // 8 * REL_OWN + at % 8 + core * (REL // 2)) % REL
-    hub_marks = hot(hub_id == head)
-    rel_marks = hot((rel_id == rel) & (at % 8 < REL_OWN))
-    for first, marks, value in ((0, hub_marks, gh), (8, rel_marks, gr)):
+    rel_id = (at // 8 * REL_OWN + at % REL_OWN + core * (REL // 2)) % REL
+    sums = []
+    for marks, value in ((hot(hub_id == head), gh), (hot(rel_id == rel), gr)):
         high, low = split(value)
-        sums = (dot(marks, high) + dot(marks, low)).reshape(2, CHIP_COUNT, 8, WIDE)
-        mine_ref[:, first : first + 8, :] = sums[0]
-        other_ref[:, first : first + 8, :] = sums[1]
-
-
-def add_pairs(a_ref, b_ref, c_ref, d_ref, out_ref):
-    out_ref[:, :NEG, :] = a_ref[...] + b_ref[...]
-    out_ref[:, NEG:, :] = c_ref[...] + d_ref[...]
+        sums.append(dot(marks, high) + dot(marks, low))
+    for k, tile in enumerate(pack(*sums)):
+        tile = tile.reshape(2, CHIP_COUNT, 8, 128)
+        mine_ref[:, k * 8 : (k + 1) * 8, :] = tile[0]
+        other_ref[:, k * 8 : (k + 1) * 8, :] = tile[1]
 
 
 def scatter_entities(head_ref, gradh_ref, asked_ref, answer_ref, out_ref,
@@ -257,34 +254,58 @@
     out_ref[HALF:, :] = grad[SIDE : SIDE + HALF]
 
 
-def update_own(sums_ref, mine_ref, neg_ref, out_ref):
-    total = jnp.sum(sums_ref[...], axis=0)
-    neg_ref[...] = total[:NEG]
-    grad = total[NEG:]
-    mine = mine_ref[...]
-    accum = aux_column(mine) + jnp.sum(grad * grad, axis=1, keepdims=True) / WIDTH
-    new = mine - LEARN_RATE * grad / jnp.sqrt(accum)
-    new = jnp.where(iota(new.shape, 1) == AUX, accum, new)
-    out_ref[...] = jnp.broadcast_to(new[None], out_ref.shape)
+def update_own(sums_ref, mine_ref, out_ref):
+    lane = iota((8, 128), 1)
+    grads = [jnp.sum(sums_ref[:, k * 8 : (k + 1) * 8, :], axis=0) for k in range(5)]
+    mine = [mine_ref[k * 8 : (k + 1) * 8, :] for k in range(5)]
+
+    def across(x):
+        return jnp.sum(x, axis=1, keepdims=True)
+
+    in_hub, in_rel = lane < 16, (lane >= 16) & (lane < 88)
+    squares = [g * g for g in grads]
+    hub = across(squares[0] + squares[1] + squares[3] + jnp.where(in_hub, squares[4], 0.0))
+    rel = jnp.broadcast_to(across(squares[2] + jnp.where(in_rel, squares[4], 0.0)), (8, 128))
+    rel = rel + pltpu.roll(rel, REL_OWN, 0)
+    hub_acc = across(jnp.where(lane == 89, mine[4], 0.0)) + hub / WIDTH
+    rel_acc = across(jnp.where(lane == 88, mine[4], 0.0)) + rel / WIDTH
+    hub_root, rel_root = jnp.sqrt(hub_acc), jnp.sqrt(rel_acc)
+    mixed = jnp.where(in_hub, hub_root, rel_root)
+    roots = (hub_root, hub_root, rel_root, hub_root, mixed)
+    new = [m - LEARN_RATE * g / root for m, g, root in zip(mine, grads, roots)]
+    new[4] = jnp.where(lane == 88, rel_acc, jnp.where(lane == 89, hub_acc, new[4]))
+    for k in range(5):
+        out_ref[:, k * 8 : (k + 1) * 8, :] = jnp.broadcast_to(new[k][None], (CHIP_COUNT, 8, 128))
 
 
 def place_new(core_ref, mine_ref, other_ref, hub_ref, hubacc_ref, rel_ref, relacc_ref, held_ref):
     core = core_ref[0]
     for part_ref, side in ((mine_ref, core), (other_ref, 1 - core)):
-        hubs = part_ref[:, :HUB_OWN, :].reshape(HUB // 2, WIDE).T
+        def turned(k):
+            return part_ref[:, k * 8 : (k + 1) * 8, :].reshape(CHIP_COUNT * 8, 128).T
+
         at = pl.ds(pl.multiple_of(side * (HUB // 2), 128), HUB // 2)
-        hub_ref[:HALF, at] = hubs[:HALF]
-        hub_ref[HALF:, at] = hubs[SIDE : SIDE + HALF]
-        hubacc_ref[:, at] = hubs[AUX : AUX + 1]
+        hub_ref[0:128, at] = turned(0)
+        hub_ref[HALF : HALF + 128, at] = turned(1)
+        mixed = turned(3)
+        hub_ref[128:HALF, at] = mixed[:72]
+        hub_ref[HALF + 128 : HALF + 184, at] = mixed[72:]
+        last = turned(4)
+        hub_ref[HALF + 184 : WIDTH, at] = last[:16]
+        hubacc_ref[:, at] = last[89:90]
         for chip in range(CHIP_COUNT):
-            held_ref[chip * REL_OWN : (chip + 1) * REL_OWN, :] = part_ref[
-                chip, HUB_OWN : HUB_OWN + REL_OWN, :
-            ]
-        rels = held_ref[...].T
+            here = slice(chip * REL_OWN, (chip + 1) * REL_OWN)
+            held_ref[0, here, :] = part_ref[chip, 16:20, :]
+            held_ref[1, here, :] = part_ref[chip, 32:36, :]
+            held_ref[2, here, :] = part_ref[chip, 20:24, :]
+            held_ref[3, here, :] = part_ref[chip, 36:40, :]
         at = pl.ds(pl.multiple_of(side * (REL // 2), 128), REL // 2)
-        rel_ref[:HALF, at] = rels[:HALF]
-        rel_ref[HALF:, at] = rels[SIDE : SIDE + HALF]
-        relacc_ref[:, at] = rels[AUX : AUX + 1]
+        for half in range(2):
+            rel_ref[half * HALF : half * HALF + 128, at] = held_ref[2 * half].T
+            last = held_ref[2 * half + 1].T
+            rel_ref[half * HALF + 128 : (half + 1) * HALF, at] = last[16:88]
+            if half == 0:
+                relacc_ref[:, at] = last[88:89]
 
 
 def update_entities(rows_ref, neg_ref, ent_ref, acc_ref, grad_ref, new_ref, newacc_ref):
@@ -305,6 +326,19 @@
     root = jnp.sqrt(accum)
     new_ref[:HALF, :] = ent_ref[:HALF, :] - LEARN_RATE * g_re / root
     new_ref[HALF:, :] = ent_ref[HALF:, :] - LEARN_RATE * g_im / root
+
+
+def around(block, axis):
+    count = SIZES[SHARD.index(axis)]
+    turns = [[(i, (i + k) % count) for i in range(count)] for k in range(1, count)]
+    return [block] + [lax.ppermute(block, axis, turn) for turn in turns]
+
+
+def add_around(blocks, axis):
+    count = SIZES[SHARD.index(axis)]
+    turns = [[((i + k) % count, i) for i in range(count)] for k in range(1, count)]
+    one, two, three = [lax.ppermute(blocks[k + 1], axis, turn) for k, turn in enumerate(turns)]
+    return (blocks[0] + one) + (two + three)
 
 
 def shape(*dims, dtype=F32):
@@ -338,10 +372,11 @@
         in_specs=[SMEM, VMEM],
         out_specs=VMEM,
         scratch_shapes=[pltpu.VMEM((WIDE, 128), F32)],
-        compiler_params=params(),
+        compiler_params=params(12),
         name="pick_negatives",
     )(negative_rows, ent_t)
-    negs = lax.all_gather(picked, SHARD, axis=0, tiled=True)
+    picked, head_row = lax.optimization_barrier((picked, head_row))
+    near = jnp.concatenate(around(picked, "z"), axis=0)
 
     query, heads, rels, sent, place = pl.pallas_call(
         prepare,
@@ -351,7 +386,7 @@
         ],
         in_specs=[VMEM] * 7,
         out_specs=[VMEM] * 5,
-        compiler_params=params(),
+        compiler_params=params(24),
         name="prepare",
     )(head_row, rel_row, owner_row, tail_row, ent_t, hub_t, rel_t)
 
@@ -360,16 +395,20 @@
         got = lax.all_to_all(parts, SHARD, split_axis=0, concat_axis=0, tiled=True)
         return got.reshape(SLOTS, WIDE)
 
+    sent, near = lax.optimization_barrier((sent, near))
+    near = jnp.concatenate(around(near, "x"), axis=0)
+    near = lax.all_gather(near, "y", axis=0, tiled=True)
+    far = lax.ppermute(near, "core", SWAP)
     asked = exchange(sent)
     ent_high, ent_low, mine_rows = pl.pallas_call(
         turn_tables,
         out_shape=[
-            shape(ENT, WIDE, dtype=BF16), shape(ENT, WIDE, dtype=BF16), shape(OWN, WIDE)
+            shape(ENT, WIDE, dtype=BF16), shape(ENT, WIDE, dtype=BF16), shape(OWN, 128)
         ],
         in_specs=[SMEM] + [VMEM] * 5,
         out_specs=[VMEM] * 3,
         scratch_shapes=[pltpu.VMEM((WIDE, 128), F32)],
-        compiler_params=params(),
+        compiler_params=params(22),
         cost_estimate=cost(1e6, 12e6),
         name="turn_tables",
     )(own_arg, ent_t, hub_t, rel_t, hub_accum.reshape(1, HUB), relation_accum.reshape(1, REL))
@@ -381,72 +420,46 @@
         grid=(SLOTS // rows,),
         in_specs=[pl.BlockSpec((rows, WIDE), lambda i: (i, 0)), VMEM, VMEM],
         out_specs=pl.BlockSpec((rows, WIDE), lambda i: (i, 0)),
-        compiler_params=params(),
+        compiler_params=params(16),
         name="answer_queries",
     )(asked, ent_high, ent_low)
     back = exchange(answer)
 
-    group = 16
-    steps = CHIP_COUNT // group
-    neg_mine, neg_other, grad_q, loss_sum = pl.pallas_call(
-        score,
-        out_shape=[
-            shape(CHIP_COUNT, NEG, WIDE), shape(CHIP_COUNT, NEG, WIDE), shape(TRIP, WIDE),
-            shape(TRIP, 128),
-        ],
-        grid_spec=pltpu.PrefetchScalarGridSpec(
-            num_scalar_prefetch=1,
-            grid=(2, steps),
-            in_specs=[
-                pl.BlockSpec((TRIP, WIDE), lambda i, c, core: (0, 0)),
-                pl.BlockSpec(
-                    (group, 1, NEG, WIDE), lambda i, c, core: (c, (i + core[0]) % 2, 0, 0)
-                ),
-            ],
-            out_specs=[
-                pl.BlockSpec(
-                    (group, NEG, WIDE), lambda i, c, core: (jnp.where(i == 0, c, steps - 1), 0, 0)
-                ),
-                pl.BlockSpec(
-                    (group, NEG, WIDE), lambda i, c, core: (jnp.where(i == 0, 0, c), 0, 0)
-                ),
-                pl.BlockSpec((TRIP, WIDE), lambda i, c, core: (0, 0)),
-                pl.BlockSpec((TRIP, 128), lambda i, c, core: (0, 0)),
-            ],
-            scratch_shapes=[
-                pltpu.VMEM((TRIP, WIDE), BF16), pltpu.VMEM((TRIP, WIDE), BF16),
-                pltpu.VMEM((TRIP, 128), F32),
-            ],
-        ),
-        compiler_params=params(),
-        cost_estimate=cost(20e9, 12e6),
-        name="score",
-    )(core_arg, query, negs.reshape(CHIP_COUNT, 2, NEG, WIDE))
-    neg_swapped = lax.ppermute(neg_other, "core", SWAP)
+    def scored(block, grad, loss):
+        return pl.pallas_call(
+            score,
+            out_shape=[shape(*block.shape), shape(TRIP, WIDE), shape(TRIP, 128)],
+            in_specs=[VMEM] * 4,
+            out_specs=[VMEM] * 3,
+            compiler_params=params(24),
+            cost_estimate=cost(10e9, 8e6),
+            name="score",
+        )(query, block, grad, loss)
+
+    zeros = jnp.zeros((TRIP, WIDE), F32), jnp.zeros((TRIP, 128), F32)
+    near_back, grad_q, loss_sum = scored(near, *zeros)
+    far_back, grad_q, loss_sum = scored(far, grad_q, loss_sum)
+    part = near_back + lax.ppermute(far_back, "core", SWAP)
+    part = lax.psum_scatter(part, "y", scatter_dimension=0, tiled=True)
+    for axis in ("x", "z"):
+        part = add_around(jnp.split(part, 4, axis=0), axis)
+    neg_grad = part
 
     grad_head, both_mine, both_other, loss = pl.pallas_call(
         close_triples,
         out_shape=[
-            shape(TRIP, WIDE), shape(CHIP_COUNT, OWN, WIDE), shape(CHIP_COUNT, OWN, WIDE),
+            shape(TRIP, WIDE), shape(CHIP_COUNT, OWN, 128), shape(CHIP_COUNT, OWN, 128),
             shape(1, TRIP),
         ],
         in_specs=[SMEM] + [VMEM] * 8,
         out_specs=[VMEM] * 4,
-        compiler_params=params(),
+        compiler_params=params(24),
         name="close_triples",
     )(core_arg, back, place, heads, rels, grad_q, loss_sum, head_row, rel_row)
     both_swapped = lax.ppermute(both_other, "core", SWAP)
 
-    block = pl.BlockSpec((8, NEG, WIDE), lambda i: (i, 0, 0))
-    paired = pl.pallas_call(
-        add_pairs,
-        out_shape=shape(CHIP_COUNT, NEG + OWN, WIDE),
-        grid=(CHIP_COUNT // 8,),
-        in_specs=[block] * 4,
-        out_specs=pl.BlockSpec((8, NEG + OWN, WIDE), lambda i: (i, 0, 0)),
-        compiler_params=params(),
-        name="add_pairs",
-    )(neg_mine, neg_swapped, both_mine, both_swapped)
+    paired = both_mine + both_swapped
+    paired, asked, answer = lax.optimization_barrier((paired, asked, answer))
     sums = lax.all_to_all(paired, CHIPS, split_axis=0, concat_axis=0, tiled=True)
 
     columns = 256
@@ -467,22 +480,21 @@
             pltpu.VMEM((WIDE, TRIP), BF16), pltpu.VMEM((WIDE, TRIP), BF16),
             pltpu.VMEM((SLOTS, 128), I32),
         ],
-        compiler_params=params(),
+        compiler_params=params(26),
         cost_estimate=cost(10e9, 12e6),
         name="scatter_entities",
     )(head_row, grad_head, asked, answer)
 
-    neg_grad, own_new = pl.pallas_call(
+    sums, entity_grad = lax.optimization_barrier((sums, entity_grad))
+    own_new = pl.pallas_call(
         update_own,
-        out_shape=[shape(NEG, WIDE), shape(CHIP_COUNT, OWN, WIDE)],
+        out_shape=shape(CHIP_COUNT, OWN, 128),
         in_specs=[VMEM] * 2,
-        out_specs=[VMEM] * 2,
-        compiler_params=params(),
+        out_specs=VMEM,
+        compiler_params=params(12),
         name="update_own",
     )(sums, mine_rows)
     new_mine = lax.all_to_all(own_new, CHIPS, split_axis=0, concat_axis=0, tiled=True)
-    new_other = lax.ppermute(new_mine, "core", SWAP)
-
     columns = 512
     entity_new, entity_accum_new = pl.pallas_call(
         update_entities,
@@ -499,7 +511,7 @@
             pl.BlockSpec((WIDTH, columns), lambda i: (0, i)),
             pl.BlockSpec((1, columns), lambda i: (0, i)),
         ],
-        compiler_params=params(),
+        compiler_params=params(12),
         cost_estimate=cost(1e9, 14e6),
         name="update_entities",
     )(
@@ -510,13 +522,14 @@
         entity_grad,
     )
 
+    new_other = lax.ppermute(new_mine, "core", SWAP)
     hub_new, hub_accum_new, rel_new, rel_accum_new = pl.pallas_call(
         place_new,
         out_shape=[shape(WIDTH, HUB), shape(1, HUB), shape(WIDTH, REL), shape(1, REL)],
         in_specs=[SMEM, VMEM, VMEM],
         out_specs=[VMEM] * 4,
-        scratch_shapes=[pltpu.VMEM((REL // 2, WIDE), F32)],
-        compiler_params=params(),
+        scratch_shapes=[pltpu.VMEM((4, REL // 2, 128), F32)],
+        compiler_params=params(14),
         name="place_new",
     )(core_arg, new_mine, new_other)
     return (

time: 291 us -> 274 us (0.942); the launches traced: 290 us -> 269 us
  blocking collectives: 101 us -> 26.9 us
  local copies, waits for them, and re-layouts: 6.05 us -> 38.4 us
  starting transfers between devices: 16.5 us -> 43.9 us
  Pallas kernels: 96.2 us -> 71.6 us
  waiting for transfers between devices: 55.8 us -> 65.5 us
  other arithmetic: 0 us -> 8.16 us
    all_to_all x1 -> x0, blocking collectives: 66.2 us -> none  [body(): lax.all_to_all(paired, CHIPS, split_axis=0, concat_axis=0, tiled=True)]
    unnamed x14 -> x86, local copies, waits for them, and re-layouts: 5.38 us -> 37 us
    all_to_all x2, waiting for transfers between devices: 24.9 us -> 0.01 us  [exchange(): got = lax.all_to_all(parts, SHARD, split_axis=0, concat_axis=0, tiled=True)]
    all_gather x1, waiting for transfers between devices: 23.9 us -> 41.8 us  [body(): near = lax.all_gather(near, 'y', axis=0, tiled=True)]
    ppermute x1 -> x14, starting transfers between devices: 0.25 us -> 15.5 us  [the longest x6 9.93 us: around(): return [block] + [lax.ppermute(block, axis, turn) for turn in turns]]
    ppermute x1 -> x14, waiting for transfers between devices: 3 us -> 15.4 us  [the longest x6 8.63 us: add_around(): lax.ppermute(blocks[k + 1], axis, turn)]
    all_to_all x0 -> x1, starting transfers between devices: none -> 10.3 us  [body(): lax.all_to_all(paired, CHIPS, split_axis=0, concat_axis=0, tiled=True)]
    all_to_all x0 -> x1, waiting for transfers between devices: none -> 8.29 us  [body(): lax.all_to_all(paired, CHIPS, split_axis=0, concat_axis=0, tiled=True)]
  transfers between devices with their start and end apart: 6 -> 21, of which waited for: 4 -> 9; matrix products, arithmetic and copies ran while one was open for 0% -> 3% of each run, Pallas kernels for 24% -> 25%
where the time goes in v2:
time: 274 us; the launch traced here: 269 us
  Pallas kernels  71.6 us (26%)
  waiting for transfers between devices  65.5 us (24%)
  starting transfers between devices  43.9 us (16%)
  local copies, waits for them, and re-layouts  38.4 us (14%)
  blocking collectives  26.9 us (10%)
  between operations  14.5 us (5%)
  other arithmetic  8.16 us (3%)
    all_gather x1, waiting for transfers between devices, body(): near = lax.all_gather(near, 'y', axis=0, tiled=True)  41.8 us
    unnamed x86, local copies, waits for them, and re-layouts  37 us
    pallas_call x2, Pallas kernels, scored(): pl.pallas_call(score, out_shape=[shape(*block.shape), shape(TRIP, WIDE),...  28 us
    all_to_all x1, blocking collectives, body(): lax.all_to_all(own_new, CHIPS, split_axis=0, concat_axis=0, tiled=True)  26.9 us
    all_to_all x2, starting transfers between devices, exchange(): got = lax.all_to_all(parts, SHARD, split_axis=0, concat_axis=0, tiled=True)  17.2 us
    pallas_call x1, Pallas kernels, body(): pl.pallas_call(scatter_entities, out_shape=shape(WIDTH, ENT), grid=(ENT /...  11.2 us
    all_to_all x1, starting transfers between devices, body(): lax.all_to_all(paired, CHIPS, split_axis=0, concat_axis=0, tiled=True)  10.3 us
    ppermute x6, starting transfers between devices, around(): return [block] + [lax.ppermute(block, axis, turn) for turn in turns]  9.93 us
  transfers between devices with their start and end apart: 21, of which 9 were waited for; matrix products, arithmetic and copies ran while one was open for 3% of the time, Pallas kernels for 25%

profile of v2, /device:TPU:0, one launch (start us, length us, event | category | flops | bytes accessed | tf_op | source)
XLA Modules:
  0.0 269.0 jit_solution(1368343332220529276)
XLA Ops:
  7.2 1.9 copy-done
  11.4 4.2 %collective-permute-start.2 = (f32[16,512]{1,0:T(8,128)S(1)}, f32[16,512]{1,0:T(8,128)S(1)}, u32[]{:S(2)}, u32[]{:S(2)}) collective-permute-start(f32[16,512]{1,0:T(8,128)S(1)} %pick_negatives.1), channel_id=1, source_target_pairs={{0,96},{32,0},{64,32},{96,64},{1,97},{33,1},{65,33},{97,65},{2,98}... | collective-permute-start | bytes 98312 | tf_op jit(solution)/shard_map/ppermute | solution.py:334
  19.4 5.0 %prepare.1 = (f32[512,512]{1,0:T(8,128)S(1)}, f32[512,512]{1,0:T(8,128)S(1)}, f32[512,512]{1,0:T(8,128)S(1)}, f32[1024,512]{1,0:T(8,128)S(1)}, s32[512,128]{1,0:T(8,128)S(1)}) custom-call(s32[1,512]{1,0:T(1,128)S(1)} %bitcast.36, s32[1,512]{1,0:T(1,128)S(1)} %bitcast.34, s32[1,512]{1,0:T(1,128)S(1)} %bitcast.40, s32[1,512]{1,0:T(1,128)S(1)} %bitcast.41, ...), custom_call_target="tpu_custom_call" | custom-call | tf_op jit(solution)/shard_map/prepare/pallas_call | solution.py:381
  28.8 2.8 %collective-permute-start.5 = (f32[64,512]{1,0:T(8,128)S(1)}, f32[64,512]{1,0:T(8,128)S(1)}, u32[]{:S(2)}, u32[]{:S(2)}) collective-permute-start(f32[64,512]{1,0:T(8,128)S(1)} %pad_maximum_fusion.1), channel_id=1, source_target_pairs={{0,24},{8,0},{16,8},{24,16},{1,25},{9,1},{17,9},{25,17},{2,26},{10... | collective-permute-start | bytes 393224 | tf_op jit(solution)/shard_map/ppermute | solution.py:334
  33.3 3.1 %collective-permute-done.5 = f32[64,512]{1,0:T(8,128)S(1)} collective-permute-done((f32[64,512]{1,0:T(8,128)S(1)}, f32[64,512]{1,0:T(8,128)S(1)}, u32[]{:S(2)}, u32[]{:S(2)}) %collective-permute-start.5) | collective-permute-done | bytes 131104 | tf_op jit(solution)/shard_map/ppermute | solution.py:334
  36.4 2.3 collective-permute-done.4
  41.0 7.9 %all-to-all-start = ((f32[128,8,512]{2,1,0:T(8,128)}), f32[128,8,512]{2,1,0:T(8,128)}, u32[]{:S(2)}, u32[]{:S(2)}) async-start(f32[128,8,512]{2,1,0:T(8,128)} %bitcast.32), calls=%async_computation.1 | async-start | bytes 4194304 | tf_op jit(solution)/shard_map/all_to_all | solution.py:395
  48.9 41.8 %all-gather.2.cloned.1.call-done.neg_ref = f32[1024,512]{1,0:T(8,128)} async-done(((f32[256,512]{1,0:T(8,128)}), f32[1024,512]{1,0:T(8,128)}) %all-gather.2.cloned.1.call-update) | async-done | bytes 2097168 | tf_op jit(solution)/shard_map/all_gather | solution.py:400
  93.3 2.5 turn_tables.1
  99.1 1.6 copy-done.14
  100.7 1.6 copy-done.16
  102.3 6.7 %answer_queries.1.answer_ref = f32[1024,512]{1,0:T(8,128)S(1)} custom-call(f32[1024,512]{1,0:T(8,128)} %bitcast.10.asked_ref, bf16[2048,512]{1,0:T(8,128)(2,1)S(1)} %copy-done.14, bf16[2048,512]{1,0:T(8,128)(2,1)S(1)} %copy-done.16), custom_call_target="tpu_custom_call" | custom-call | tf_op jit(solution)/shard_map/answer_queries/pallas_call | solution.py:417
  110.3 9.3 %all-to-all-start.1 = ((f32[128,8,512]{2,1,0:T(8,128)}), f32[128,8,512]{2,1,0:T(8,128)}, u32[]{:S(2)}, u32[]{:S(2)}) async-start(f32[128,8,512]{2,1,0:T(8,128)} %bitcast.27), calls=%async_computation.2 | async-start | bytes 4194304 | tf_op jit(solution)/shard_map/all_to_all | solution.py:395
  120.1 1.6 copy-done.37
  122.9 8.0 %score.2 = (f32[1024,512]{1,0:T(8,128)S(1)}, f32[512,512]{1,0:T(8,128)S(1)}, f32[512,128]{1,0:T(8,128)S(1)}) custom-call(f32[512,512]{1,0:T(8,128)S(1)} %copy-done.39, f32[1024,512]{1,0:T(8,128)S(1)} %copy-done.37, f32[512,512]{1,0:T(8,128)S(1)} %broadcast_in_dim.13.grad_in, f32[512,128]{1,0:T(8,128)S(1)} %broadcast_in_dim.14.loss_in), custom_call_target="tpu_custom_call" | custom-call | flops 10000000000 | bytes 8000000 | tf_op jit(solution)/shard_map/score/pallas_call | solution.py:429
  132.2 20.0 %score.3 = (f32[1024,512]{1,0:T(8,128)}, f32[512,512]{1,0:T(8,128)S(1)}, f32[512,128]{1,0:T(8,128)S(1)}) custom-call(f32[512,512]{1,0:T(8,128)S(1)} %copy-done.40, f32[1024,512]{1,0:T(8,128)} %collective-permute-done.6.neg_ref, f32[512,512]{1,0:T(8,128)S(1)} %get-tuple-element.46.grad_in, f32[512,128]{1,0:T(8,128)S(1)} %get-tuple-element.47.loss_in), custom_call_target="tpu_custom_call" | custom-call | flops 10000000000 | bytes 8000000 | tf_op jit(solution)/shard_map/score/pallas_call | solution.py:429
  158.6 7.0 %close_triples.1 = (f32[512,512]{1,0:T(8,128)S(1)}, f32[64,40,128]{2,1,0:T(8,128)S(1)}, f32[64,40,128]{2,1,0:T(8,128)}, f32[1,512]{1,0:T(1,128)}) custom-call(s32[1]{0:T(128)} %bitcast.8.core_ref, f32[1024,512]{1,0:T(8,128)} %bitcast.15.back_ref, s32[512,128]{1,0:T(8,128)S(1)} %get-tuple-element.52.place_ref, f32[512,512]{1,0:T(8,128)S(1)} %copy-done.19, ...), custom_call_target="tpu_custom_call" | custom-call | tf_op jit(solution)/shard_map/close_triples/pallas_call | solution.py:448
  168.1 3.5 %add.35 = f32[1024,512]{1,0:T(8,128)} add(f32[1024,512]{1,0:T(8,128)S(1)} %copy-done.11, f32[1024,512]{1,0:T(8,128)} %collective-permute-done.7) | non-fusion elementwise | flops 524288 | bytes 6291456 | tf_op jit(solution)/shard_map/add | solution.py:442
  171.6 2.9 %add.45 = f32[64,40,128]{2,1,0:T(8,128)} add(f32[64,40,128]{2,1,0:T(8,128)} %copy-done.17, f32[64,40,128]{2,1,0:T(8,128)} %collective-permute-done.14) | non-fusion elementwise | flops 327680 | bytes 3932160 | tf_op jit(solution)/shard_map/add | solution.py:461
  174.5 10.3 %all-to-all-start.2 = ((f32[64,40,128]{2,1,0:T(8,128)}), f32[64,40,128]{2,1,0:T(8,128)}, u32[]{:S(2)}, u32[]{:S(2)}) async-start(f32[64,40,128]{2,1,0:T(8,128)} %add.45), calls=%async_computation.3 | async-start | bytes 2621440 | tf_op jit(solution)/shard_map/all_to_all | solution.py:463
  184.8 1.6 copy-done.3
  187.7 11.2 %scatter_entities.1.grad_ref = f32[400,2048]{1,0:T(8,128)S(1)} custom-call(s32[1,512]{1,0:T(1,128)S(1)} %bitcast.38, f32[512,512]{1,0:T(8,128)S(1)} %copy-done.42, f32[1024,512]{1,0:T(8,128)} %bitcast.10.asked_ref, f32[1024,512]{1,0:T(8,128)S(1)} %copy-done.3), custom_call_target="tpu_custom_call" | custom-call | flops 10000000000 | bytes 12000000 | tf_op jit(solution)/shard_map/scatter_entities/pallas_call | solution.py:467
  198.8 1.7 copy-done.6
  200.5 8.3 %all-to-all-done.2.sums_ref = f32[64,40,128]{2,1,0:T(8,128)} async-done(((f32[64,40,128]{2,1,0:T(8,128)}), f32[64,40,128]{2,1,0:T(8,128)}, u32[]{:S(2)}, u32[]{:S(2)}) %all-to-all-start.2) | async-done | bytes 1310752 | tf_op jit(solution)/shard_map/all_to_all | solution.py:463
  208.8 1.6 update_own.1
  210.4 26.9 %all_to_all.20.mine_ref = f32[64,40,128]{2,1,0:T(8,128)} all-to-all(f32[64,40,128]{2,1,0:T(8,128)S(1)} %update_own.1), channel_id=1, replica_groups=mesh['z'=4,'x'=4,'y'=4,'core'=2] {'z','x','y'}, dimensions={0} | all-to-all | bytes 2621440 | tf_op jit(solution)/shard_map/all_to_all | solution.py:497
  239.2 2.1 collective-permute-start.9
  241.3 3.6 %collective-permute-done.8 = f32[64,512]{1,0:T(8,128)S(1)} collective-permute-done((f32[64,512]{1,0:T(8,128)S(1)}, f32[64,512]{1,0:T(8,128)S(1)}, u32[]{:S(2)}, u32[]{:S(2)}) %collective-permute-start.8) | collective-permute-done | bytes 131104 | tf_op jit(solution)/shard_map/ppermute | solution.py:340
  245.0 2.1 collective-permute-done.9
  247.1 2.1 collective-permute-done.10
  252.9 4.0 %place_new.1 = (f32[400,1024]{1,0:T(8,128)}, f32[1,1024]{1,0:T(1,128)}, f32[400,512]{1,0:T(8,128)}, f32[1,512]{1,0:T(1,128)}) custom-call(s32[1]{0:T(128)} %bitcast.8.core_ref, f32[64,40,128]{2,1,0:T(8,128)} %all_to_all.20.mine_ref, f32[64,40,128]{2,1,0:T(8,128)} %collective-permute-done.15.other_ref), custom_call_target="tpu_custom_call" | custom-call | tf_op jit(solution)/shard_map/place_new/pallas_call | solution.py:526
  257.8 4.1 %update_entities.1 = (f32[400,2048]{1,0:T(8,128)}, f32[1,2048]{1,0:T(1,128)}) custom-call(s32[16,128]{1,0:T(8,128)S(1)} %broadcast_in_dim.12.rows_ref, f32[16,512]{1,0:T(8,128)S(1)} %fusion.1.neg_ref, f32[400,2048]{1,0:T(8,128)S(1)} %bitcast.26, f32[1,2048]{1,0:T(1,128)S(1)} %bitcast.33, f32[400,2048]{1,0:T(8,128)S(1)} %copy-done.7), custom_call_target="tpu_custom_call" | custom-call | flops 1000000000 | bytes 14000000 | tf_op jit(solution)/shard_map/update_entities/pallas_call | solution.py:499
  (121 shorter events, 41.3 us)
Async XLA Ops:
  7.2 83.5 %all-gather.2.cloned.1.call-start = ((), (), s32[]{:S(2)}) async-start(), calls=%async_computation.5 | async-start | bytes 2621440 | tf_op jit(solution)/shard_map/all_gather | solution.py:400
  9.8 7.0 %copy-start.30 = (s32[512]{0:T(512)S(1)}, s32[512]{0:T(512)}, u32[]{:S(2)}) copy-start(s32[512]{0:T(512)} %param.17) | copy-start | bytes 6148
  9.8 7.0 %copy-start.32 = (s32[512,1]{0,1:T(1,128)S(1)}, s32[512,1]{0,1:T(1,128)}, u32[]{:S(2)}) copy-start(s32[512,1]{0,1:T(1,128)} %param.19) | copy-start | bytes 6148
  9.8 7.0 %copy-start.33 = (s32[512]{0:T(512)S(1)}, s32[512]{0:T(512)}, u32[]{:S(2)}) copy-start(s32[512]{0:T(512)} %param.20) | copy-start | bytes 6148
  11.4 17.5 %collective-permute-start.2 = (f32[16,512]{1,0:T(8,128)S(1)}, f32[16,512]{1,0:T(8,128)S(1)}, u32[]{:S(2)}, u32[]{:S(2)}) collective-permute-start(f32[16,512]{1,0:T(8,128)S(1)} %pick_negatives.1), channel_id=1, source_target_pairs={{0,96},{32,0},{64,32},{96,64},{1,97},{33,1},{65,33},{97,65},{2,98}... | collective-permute-start | bytes 98312 | tf_op jit(solution)/shard_map/ppermute | solution.py:334
  15.5 13.3 %collective-permute-start.1 = (f32[16,512]{1,0:T(8,128)S(1)}, f32[16,512]{1,0:T(8,128)S(1)}, u32[]{:S(2)}, u32[]{:S(2)}) collective-permute-start(f32[16,512]{1,0:T(8,128)S(1)} %pick_negatives.1), channel_id=1, source_target_pairs={{0,64},{32,96},{64,0},{96,32},{1,65},{33,97},{65,1},{97,33},{2,66}... | collective-permute-start | bytes 98312 | tf_op jit(solution)/shard_map/ppermute | solution.py:334
  15.5 13.3 %collective-permute-start = (f32[16,512]{1,0:T(8,128)S(1)}, f32[16,512]{1,0:T(8,128)S(1)}, u32[]{:S(2)}, u32[]{:S(2)}) collective-permute-start(f32[16,512]{1,0:T(8,128)S(1)} %pick_negatives.1), channel_id=1, source_target_pairs={{0,32},{32,64},{64,96},{96,0},{1,33},{33,65},{65,97},{97,1},{2,34}... | collective-permute-start | bytes 98312 | tf_op jit(solution)/shard_map/ppermute | solution.py:334
  28.8 7.6 %collective-permute-start.5 = (f32[64,512]{1,0:T(8,128)S(1)}, f32[64,512]{1,0:T(8,128)S(1)}, u32[]{:S(2)}, u32[]{:S(2)}) collective-permute-start(f32[64,512]{1,0:T(8,128)S(1)} %pad_maximum_fusion.1), channel_id=1, source_target_pairs={{0,24},{8,0},{16,8},{24,16},{1,25},{9,1},{17,9},{25,17},{2,26},{10... | collective-permute-start | bytes 393224 | tf_op jit(solution)/shard_map/ppermute | solution.py:334
  31.7 7.1 %collective-permute-start.4 = (f32[64,512]{1,0:T(8,128)S(1)}, f32[64,512]{1,0:T(8,128)S(1)}, u32[]{:S(2)}, u32[]{:S(2)}) collective-permute-start(f32[64,512]{1,0:T(8,128)S(1)} %pad_maximum_fusion.1), channel_id=1, source_target_pairs={{0,16},{8,24},{16,0},{24,8},{1,17},{9,25},{17,1},{25,9},{2,18},{10... | collective-permute-start | bytes 393224 | tf_op jit(solution)/shard_map/ppermute | solution.py:334
  32.5 7.6 %collective-permute-start.3 = (f32[64,512]{1,0:T(8,128)S(1)}, f32[64,512]{1,0:T(8,128)S(1)}, u32[]{:S(2)}, u32[]{:S(2)}) collective-permute-start(f32[64,512]{1,0:T(8,128)S(1)} %pad_maximum_fusion.1), channel_id=1, source_target_pairs={{0,8},{8,16},{16,24},{24,0},{1,9},{9,17},{17,25},{25,1},{2,10},{10... | collective-permute-start | bytes 393224 | tf_op jit(solution)/shard_map/ppermute | solution.py:334
  40.9 49.8 %copy-start.31 = (f32[1024]{0:T(1024)S(1)}, f32[1024]{0:T(1024)}, u32[]{:S(2)}) copy-start(f32[1024]{0:T(1024)} %param.14) | copy-start | bytes 12292
  41.0 49.8 %copy-start.34 = (f32[512]{0:T(512)S(1)}, f32[512]{0:T(512)}, u32[]{:S(2)}) copy-start(f32[512]{0:T(512)} %param.16) | copy-start | bytes 6148
  41.0 58.1 %all-to-all-start = ((f32[128,8,512]{2,1,0:T(8,128)}), f32[128,8,512]{2,1,0:T(8,128)}, u32[]{:S(2)}, u32[]{:S(2)}) async-start(f32[128,8,512]{2,1,0:T(8,128)} %bitcast.32), calls=%async_computation.1 | async-start | bytes 4194304 | tf_op jit(solution)/shard_map/all_to_all | solution.py:395
  90.7 41.6 %collective-permute-start.6 = (f32[1024,512]{1,0:T(8,128)}, f32[1024,512]{1,0:T(8,128)}, u32[]{:S(2)}, u32[]{:S(2)}) collective-permute-start(f32[1024,512]{1,0:T(8,128)} %all-gather.2.cloned.1.call-done.neg_ref), channel_id=1, source_target_pairs={{0,1},{1,0},{2,3},{3,2},{4,5},{5,4},{6,7},{7,6},{8,9},{9,8},{10,11... | collective-permute-start | bytes 6291464 | tf_op jit(solution)/shard_map/ppermute | solution.py:401
  110.3 43.6 %all-to-all-start.1 = ((f32[128,8,512]{2,1,0:T(8,128)}), f32[128,8,512]{2,1,0:T(8,128)}, u32[]{:S(2)}, u32[]{:S(2)}) async-start(f32[128,8,512]{2,1,0:T(8,128)} %bitcast.27), calls=%async_computation.2 | async-start | bytes 4194304 | tf_op jit(solution)/shard_map/all_to_all | solution.py:395
  119.6 117.8 %reduce-scatter.2.cloned.1.call-start = ((), (), s32[]{:S(2)}) async-start(), calls=%async_computation.6 | async-start | bytes 2621440 | tf_op jit(solution)/shard_map/reduce_scatter | solution.py:443
  122.9 9.4 %copy-start.40 = (f32[512,512]{1,0:T(8,128)S(1)}, f32[512,512]{1,0:T(8,128)}, u32[]{:S(2)}) copy-start(f32[512,512]{1,0:T(8,128)} %copy-done.38) | copy-start | bytes 3145732
  153.9 14.2 %collective-permute-start.7 = (f32[1024,512]{1,0:T(8,128)}, f32[1024,512]{1,0:T(8,128)}, u32[]{:S(2)}, u32[]{:S(2)}) collective-permute-start(f32[1024,512]{1,0:T(8,128)} %get-tuple-element.48), channel_id=1, source_target_pairs={{0,1},{1,0},{2,3},{3,2},{4,5},{5,4},{6,7},{7,6},{8,9},{9,8},{10,11... | collective-permute-start | bytes 6291464 | tf_op jit(solution)/shard_map/ppermute | solution.py:442
  158.6 9.6 %copy-start.11 = (f32[1024,512]{1,0:T(8,128)S(1)}, f32[1024,512]{1,0:T(8,128)}, u32[]{:S(2)}) copy-start(f32[1024,512]{1,0:T(8,128)} %copy-done.10) | copy-start | bytes 6291460
  167.6 4.0 %collective-permute-start.14 = (f32[64,40,128]{2,1,0:T(8,128)}, f32[64,40,128]{2,1,0:T(8,128)}, u32[]{:S(2)}, u32[]{:S(2)}) collective-permute-start(f32[64,40,128]{2,1,0:T(8,128)} %get-tuple-element.58), channel_id=1, source_target_pairs={{0,1},{1,0},{2,3},{3,2},{4,5},{5,4},{6,7},{7,6},{8,9},{9,8},{10,11... | collective-permute-start | bytes 3932168 | tf_op jit(solution)/shard_map/ppermute | solution.py:459
  174.5 34.3 %all-to-all-start.2 = ((f32[64,40,128]{2,1,0:T(8,128)}), f32[64,40,128]{2,1,0:T(8,128)}, u32[]{:S(2)}, u32[]{:S(2)}) async-start(f32[64,40,128]{2,1,0:T(8,128)} %add.45), calls=%async_computation.3 | async-start | bytes 2621440 | tf_op jit(solution)/shard_map/all_to_all | solution.py:463
  187.6 21.2 %copy-start.27 = (f32[40,128]{1,0:T(8,128)S(1)}, f32[40,128]{1,0:T(8,128)}, u32[]{:S(2)}) copy-start(f32[40,128]{1,0:T(8,128)} %copy-done.26) | copy-start | bytes 61444
  237.4 20.4 %copy-start.36 = (s32[16]{0:T(128)S(1)}, s32[16]{0:T(128)}, u32[]{:S(2)}) copy-start(s32[16]{0:T(128)} %rows_ref.1) | copy-start | bytes 196
  237.4 20.5 %copy-start.28 = (f32[2048]{0:T(1024)S(1)}, f32[2048]{0:T(1024)}, u32[]{:S(2)}) copy-start(f32[2048]{0:T(1024)} %param.12) | copy-start | bytes 24580
  237.4 15.6 %collective-permute-start.15 = (f32[64,40,128]{2,1,0:T(8,128)}, f32[64,40,128]{2,1,0:T(8,128)}, u32[]{:S(2)}, u32[]{:S(2)}) collective-permute-start(f32[64,40,128]{2,1,0:T(8,128)} %all_to_all.20.mine_ref), channel_id=1, source_target_pairs={{0,1},{1,0},{2,3},{3,2},{4,5},{5,4},{6,7},{7,6},{8,9},{9,8},{10,11... | collective-permute-start | bytes 3932168 | tf_op jit(solution)/shard_map/ppermute | solution.py:525
  237.4 20.4 %copy-start.7 = (f32[400,2048]{1,0:T(8,128)S(1)}, f32[400,2048]{1,0:T(8,128)}, u32[]{:S(2)}) copy-start(f32[400,2048]{1,0:T(8,128)} %copy-done.6) | copy-start | bytes 9830404
  238.6 6.4 %collective-permute-start.8 = (f32[64,512]{1,0:T(8,128)S(1)}, f32[64,512]{1,0:T(8,128)S(1)}, u32[]{:S(2)}, u32[]{:S(2)}) collective-permute-start(f32[64,512]{1,0:T(8,128)S(1)} %get-tuple-element.75), channel_id=1, source_target_pairs={{8,0},{16,8},{24,16},{0,24},{9,1},{17,9},{25,17},{1,25},{10,2},{18... | collective-permute-start | bytes 393224 | tf_op jit(solution)/shard_map/ppermute | solution.py:340
  239.2 7.8 %collective-permute-start.9 = (f32[64,512]{1,0:T(8,128)S(1)}, f32[64,512]{1,0:T(8,128)S(1)}, u32[]{:S(2)}, u32[]{:S(2)}) collective-permute-start(f32[64,512]{1,0:T(8,128)S(1)} %get-tuple-element.74), channel_id=1, source_target_pairs={{16,0},{24,8},{0,16},{8,24},{17,1},{25,9},{1,17},{9,25},{18,2},{26... | collective-permute-start | bytes 393224 | tf_op jit(solution)/shard_map/ppermute | solution.py:340
  241.3 7.8 %collective-permute-start.10 = (f32[64,512]{1,0:T(8,128)S(1)}, f32[64,512]{1,0:T(8,128)S(1)}, u32[]{:S(2)}, u32[]{:S(2)}) collective-permute-start(f32[64,512]{1,0:T(8,128)S(1)} %get-tuple-element.73), channel_id=1, source_target_pairs={{24,0},{0,8},{8,16},{16,24},{25,1},{1,9},{9,17},{17,25},{26,2},{2,... | collective-permute-start | bytes 393224 | tf_op jit(solution)/shard_map/ppermute | solution.py:340
  250.1 6.8 %collective-permute-start.11 = (f32[16,512]{1,0:T(8,128)S(1)}, f32[16,512]{1,0:T(8,128)S(1)}, u32[]{:S(2)}, u32[]{:S(2)}) collective-permute-start(f32[16,512]{1,0:T(8,128)S(1)} %get-tuple-element.78), channel_id=1, source_target_pairs={{32,0},{64,32},{96,64},{0,96},{33,1},{65,33},{97,65},{1,97},{34,2}... | collective-permute-start | bytes 98312 | tf_op jit(solution)/shard_map/ppermute | solution.py:340
  251.3 5.6 %collective-permute-start.12 = (f32[16,512]{1,0:T(8,128)S(1)}, f32[16,512]{1,0:T(8,128)S(1)}, u32[]{:S(2)}, u32[]{:S(2)}) collective-permute-start(f32[16,512]{1,0:T(8,128)S(1)} %get-tuple-element.77), channel_id=1, source_target_pairs={{64,0},{96,32},{0,64},{32,96},{65,1},{97,33},{1,65},{33,97},{66,2}... | collective-permute-start | bytes 98312 | tf_op jit(solution)/shard_map/ppermute | solution.py:340
  252.6 5.1 %collective-permute-start.13 = (f32[16,512]{1,0:T(8,128)S(1)}, f32[16,512]{1,0:T(8,128)S(1)}, u32[]{:S(2)}, u32[]{:S(2)}) collective-permute-start(f32[16,512]{1,0:T(8,128)S(1)} %get-tuple-element.76), channel_id=1, source_target_pairs={{96,0},{0,32},{32,64},{64,96},{97,1},{1,33},{33,65},{65,97},{98,2}... | collective-permute-start | bytes 98312 | tf_op jit(solution)/shard_map/ppermute | solution.py:340
  (32 other events, 51.0 us)
Sparse Core Ops, SparseCore 0:
  41.1 49.5 all-gather.1
  171.7 44.7 reduce-scatter.1

commit v3 on v2

--- a/solution.py
+++ b/solution.py
@@ -20,8 +20,8 @@
 SMEM = pl.BlockSpec(memory_space=pltpu.SMEM)
 
 
-def params(mib):
-    return pltpu.CompilerParams(vmem_limit_bytes=mib << 20)
+def params():
+    return pltpu.CompilerParams(vmem_limit_bytes=56 << 20)
 
 
 def cost(flops, nbytes):
@@ -372,7 +372,7 @@
         in_specs=[SMEM, VMEM],
         out_specs=VMEM,
         scratch_shapes=[pltpu.VMEM((WIDE, 128), F32)],
-        compiler_params=params(12),
+        compiler_params=params(),
         name="pick_negatives",
     )(negative_rows, ent_t)
     picked, head_row = lax.optimization_barrier((picked, head_row))
@@ -386,7 +386,7 @@
         ],
         in_specs=[VMEM] * 7,
         out_specs=[VMEM] * 5,
-        compiler_params=params(24),
+        compiler_params=params(),
         name="prepare",
     )(head_row, rel_row, owner_row, tail_row, ent_t, hub_t, rel_t)
 
@@ -395,10 +395,8 @@
         got = lax.all_to_all(parts, SHARD, split_axis=0, concat_axis=0, tiled=True)
         return got.reshape(SLOTS, WIDE)
 
-    sent, near = lax.optimization_barrier((sent, near))
-    near = jnp.concatenate(around(near, "x"), axis=0)
-    near = lax.all_gather(near, "y", axis=0, tiled=True)
-    far = lax.ppermute(near, "core", SWAP)
+    sent, near, own_arg = lax.optimization_barrier((sent, near, own_arg))
+    near = lax.all_gather(near, ("x", "y"), axis=0, tiled=True)
     asked = exchange(sent)
     ent_high, ent_low, mine_rows = pl.pallas_call(
         turn_tables,
@@ -408,7 +406,7 @@
         in_specs=[SMEM] + [VMEM] * 5,
         out_specs=[VMEM] * 3,
         scratch_shapes=[pltpu.VMEM((WIDE, 128), F32)],
-        compiler_params=params(22),
+        compiler_params=params(),
         cost_estimate=cost(1e6, 12e6),
         name="turn_tables",
     )(own_arg, ent_t, hub_t, rel_t, hub_accum.reshape(1, HUB), relation_accum.reshape(1, REL))
@@ -420,9 +418,11 @@
         grid=(SLOTS // rows,),
         in_specs=[pl.BlockSpec((rows, WIDE), lambda i: (i, 0)), VMEM, VMEM],
         out_specs=pl.BlockSpec((rows, WIDE), lambda i: (i, 0)),
-        compiler_params=params(16),
+        compiler_params=params(),
         name="answer_queries",
     )(asked, ent_high, ent_low)
+    near, answer = lax.optimization_barrier((near, answer))
+    far = lax.ppermute(near, "core", SWAP)
     back = exchange(answer)
 
     def scored(block, grad, loss):
@@ -431,19 +431,22 @@
             out_shape=[shape(*block.shape), shape(TRIP, WIDE), shape(TRIP, 128)],
             in_specs=[VMEM] * 4,
             out_specs=[VMEM] * 3,
-            compiler_params=params(24),
+            compiler_params=params(),
             cost_estimate=cost(10e9, 8e6),
             name="score",
         )(query, block, grad, loss)
 
     zeros = jnp.zeros((TRIP, WIDE), F32), jnp.zeros((TRIP, 128), F32)
-    near_back, grad_q, loss_sum = scored(near, *zeros)
-    far_back, grad_q, loss_sum = scored(far, grad_q, loss_sum)
-    part = near_back + lax.ppermute(far_back, "core", SWAP)
-    part = lax.psum_scatter(part, "y", scatter_dimension=0, tiled=True)
-    for axis in ("x", "z"):
-        part = add_around(jnp.split(part, 4, axis=0), axis)
-    neg_grad = part
+    far_back, grad_q, loss_sum = scored(far, *zeros)
+    far_back = lax.ppermute(far_back, "core", SWAP)
+    near_back, grad_q, loss_sum = scored(near, grad_q, loss_sum)
+    part, back = lax.optimization_barrier((near_back + far_back, back))
+    part = lax.psum_scatter(part, "x", scatter_dimension=0, tiled=True)
+    y = lax.axis_index("y").astype(I32)
+    blocks = part.reshape(4, 4 * NEG, WIDE)
+    blocks = [lax.dynamic_index_in_dim(blocks, (y + 4 - k) & 3, 0, keepdims=False) for k in range(4)]
+    part = add_around(blocks, "y")
+    neg_grad = add_around(jnp.split(part, 4, axis=0), "z")
 
     grad_head, both_mine, both_other, loss = pl.pallas_call(
         close_triples,
@@ -453,7 +456,7 @@
         ],
         in_specs=[SMEM] + [VMEM] * 8,
         out_specs=[VMEM] * 4,
-        compiler_params=params(24),
+        compiler_params=params(),
         name="close_triples",
     )(core_arg, back, place, heads, rels, grad_q, loss_sum, head_row, rel_row)
     both_swapped = lax.ppermute(both_other, "core", SWAP)
@@ -480,7 +483,7 @@
             pltpu.VMEM((WIDE, TRIP), BF16), pltpu.VMEM((WIDE, TRIP), BF16),
             pltpu.VMEM((SLOTS, 128), I32),
         ],
-        compiler_params=params(26),
+        compiler_params=params(),
         cost_estimate=cost(10e9, 12e6),
         name="scatter_entities",
     )(head_row, grad_head, asked, answer)
@@ -491,7 +494,7 @@
         out_shape=shape(CHIP_COUNT, OWN, 128),
         in_specs=[VMEM] * 2,
         out_specs=VMEM,
-        compiler_params=params(12),
+        compiler_params=params(),
         name="update_own",
     )(sums, mine_rows)
     new_mine = lax.all_to_all(own_new, CHIPS, split_axis=0, concat_axis=0, tiled=True)
@@ -511,7 +514,7 @@
             pl.BlockSpec((WIDTH, columns), lambda i: (0, i)),
             pl.BlockSpec((1, columns), lambda i: (0, i)),
         ],
-        compiler_params=params(12),
+        compiler_params=params(),
         cost_estimate=cost(1e9, 14e6),
         name="update_entities",
     )(
@@ -523,13 +526,14 @@
     )
 
     new_other = lax.ppermute(new_mine, "core", SWAP)
+    new_mine, entity_new = lax.optimization_barrier((new_mine, entity_new))
     hub_new, hub_accum_new, rel_new, rel_accum_new = pl.pallas_call(
         place_new,
         out_shape=[shape(WIDTH, HUB), shape(1, HUB), shape(WIDTH, REL), shape(1, REL)],
         in_specs=[SMEM, VMEM, VMEM],
         out_specs=[VMEM] * 4,
         scratch_shapes=[pltpu.VMEM((4, REL // 2, 128), F32)],
-        compiler_params=params(14),
+        compiler_params=params(),
         name="place_new",
     )(core_arg, new_mine, new_other)
     return (

time: 274 us -> 254 us (0.927); the launches traced: 269 us -> 253 us
  local copies, waits for them, and re-layouts: 38.4 us -> 8.85 us
  Pallas kernels: 71.6 us -> 86.9 us
  starting transfers between devices: 43.9 us -> 35.5 us
  waiting for transfers between devices: 65.5 us -> 72.1 us
    all_to_all x2, waiting for transfers between devices: 0.01 us -> 39.5 us  [exchange(): got = lax.all_to_all(parts, SHARD, split_axis=0, concat_axis=0, tiled=True)]
    all_gather x1, waiting for transfers between devices: 41.8 us -> 6.56 us  [body(): near = lax.all_gather(near, ('x', 'y'), axis=0, tiled=True)]
    unnamed x86 -> x16, local copies, waits for them, and re-layouts: 37 us -> 4.73 us
    ppermute x6 -> x3, waiting for transfers between devices: 6.76 us -> 0.01 us  [around(): return [block] + [lax.ppermute(block, axis, turn) for turn in turns]]
    all_to_all x1, starting transfers between devices: 10.3 us -> 4.93 us  [body(): lax.all_to_all(paired, CHIPS, split_axis=0, concat_axis=0, tiled=True)]
    pallas_call x1, Pallas kernels: 2.5 us -> 7.32 us  [body(): pl.pallas_call(turn_tables, out_shape=[shape(ENT, WIDE, dtype=BF16), shap...]
    pallas_call x2, Pallas kernels: 28 us -> 23.5 us  [scored(): pl.pallas_call(score, out_shape=[shape(*block.shape), shape(TRIP, WIDE),...]
    ppermute x1, waiting for transfers between devices: 0.01 us -> 4.37 us  [body(): far = lax.ppermute(near, 'core', SWAP)]
  transfers between devices with their start and end apart: 21 -> 18, of which waited for: 9 -> 11; matrix products, arithmetic and copies ran while one was open for 3% -> 4% of each run, Pallas kernels for 25% -> 27%
where the time goes in v3:
time: 254 us; the launch traced here: 253 us
  Pallas kernels  86.9 us (34%)
  waiting for transfers between devices  72.1 us (28%)
  starting transfers between devices  35.5 us (14%)
  blocking collectives  26.6 us (10%)
  between operations  14.1 us (6%)
  local copies, waits for them, and re-layouts  8.85 us (3%)
  other arithmetic  8.76 us (3%)
    all_to_all x2, waiting for transfers between devices, exchange(): got = lax.all_to_all(parts, SHARD, split_axis=0, concat_axis=0, tiled=True)  39.5 us
    all_to_all x1, blocking collectives, body(): lax.all_to_all(own_new, CHIPS, split_axis=0, concat_axis=0, tiled=True)  26.6 us
    pallas_call x2, Pallas kernels, scored(): pl.pallas_call(score, out_shape=[shape(*block.shape), shape(TRIP, WIDE),...  23.5 us
    all_to_all x2, starting transfers between devices, exchange(): got = lax.all_to_all(parts, SHARD, split_axis=0, concat_axis=0, tiled=True)  16.2 us
    pallas_call x1, Pallas kernels, body(): pl.pallas_call(scatter_entities, out_shape=shape(WIDTH, ENT), grid=(ENT /...  12.9 us
    pallas_call x1, Pallas kernels, body(): pl.pallas_call(prepare, out_shape=[shape(TRIP, WIDE), shape(TRIP, WIDE),...  9.36 us
    all_to_all x1, waiting for transfers between devices, body(): lax.all_to_all(paired, CHIPS, split_axis=0, concat_axis=0, tiled=True)  9.22 us
    ppermute x6, waiting for transfers between devices, add_around(): lax.ppermute(blocks[k + 1], axis, turn)  9.2 us
  transfers between devices with their start and end apart: 18, of which 11 were waited for; matrix products, arithmetic and copies ran while one was open for 4% of the time, Pallas kernels for 27%

profile of v3, /device:TPU:0, one launch (start us, length us, event | category | flops | bytes accessed | tf_op | source)
XLA Modules:
  0.0 252.9 jit_solution(9783812707877353096)
XLA Ops:
  7.2 3.6 %pick_negatives.1 = f32[16,512]{1,0:T(8,128)} custom-call(s32[16]{0:T(128)} %rows_ref.1, f32[400,2048]{1,0:T(8,128)} %bitcast.34), custom_call_target="tpu_custom_call" | custom-call | tf_op jit(solution)/shard_map/pick_negatives/pallas_call | solution.py:369
  10.8 2.0 collective-permute-start
  12.8 3.6 %collective-permute-start.1 = (f32[16,512]{1,0:T(8,128)}, f32[16,512]{1,0:T(8,128)S(1)}, u32[]{:S(2)}, u32[]{:S(2)}) collective-permute-start(f32[16,512]{1,0:T(8,128)} %pick_negatives.1), channel_id=1, source_target_pairs={{0,64},{32,96},{64,0},{96,32},{1,65},{33,97},{65,1},{97,33},{2,66}... | collective-permute-start | bytes 98312 | tf_op jit(solution)/shard_map/ppermute | solution.py:334
  17.4 9.4 %prepare.1 = (f32[512,512]{1,0:T(8,128)}, f32[512,512]{1,0:T(8,128)}, f32[512,512]{1,0:T(8,128)}, f32[1024,512]{1,0:T(8,128)}, s32[512,128]{1,0:T(8,128)}) custom-call(s32[1,512]{1,0:T(1,128)} %bitcast.51, s32[1,512]{1,0:T(1,128)} %bitcast.49, s32[1,512]{1,0:T(1,128)} %bitcast.55, s32[1,512]{1,0:T(1,128)} %bitcast.56, f32[400,2048]{1,0:T(8,128)} %bitcast.35, ...), custom_call_target="tpu_custom_call" | custom-call | tf_op jit(solution)/shard_map/prepare/pallas_call | solution.py:381
  27.4 8.0 %all-to-all-start = ((f32[128,8,512]{2,1,0:T(8,128)}), f32[128,8,512]{2,1,0:T(8,128)S(1)}, u32[]{:S(2)}, u32[]{:S(2)}) async-start(f32[128,8,512]{2,1,0:T(8,128)} %bitcast.45), calls=%async_computation | async-start | bytes 4194304 | tf_op jit(solution)/shard_map/all_to_all | solution.py:395
  35.5 7.3 %turn_tables.1 = (bf16[2048,512]{1,0:T(8,128)(2,1)}, bf16[2048,512]{1,0:T(8,128)(2,1)}, f32[40,128]{1,0:T(8,128)}) custom-call(s32[1]{0:T(128)} %bitcast.8.own_ref, f32[400,2048]{1,0:T(8,128)} %bitcast.36, f32[400,1024]{1,0:T(8,128)} %bitcast.42, f32[400,512]{1,0:T(8,128)} %bitcast.44, f32[1,1024]{1,0:T(1,128)} %bitcast.54, f32[1,512]{1,0:T(1,128)} %bitcast.57), custom_call_target="tpu_custom_call" | custom-call | flops 1000000 | bytes 12000000 | tf_op jit(solution)/shard_map/turn_tables/pallas_call | solution.py:401
  42.8 25.1 %all-to-all-done = f32[128,8,512]{2,1,0:T(8,128)S(1)} async-done(((f32[128,8,512]{2,1,0:T(8,128)}), f32[128,8,512]{2,1,0:T(8,128)S(1)}, u32[]{:S(2)}, u32[]{:S(2)}) %all-to-all-start) | async-done | bytes 2097184 | tf_op jit(solution)/shard_map/all_to_all | solution.py:395
  67.9 1.3 copy-done
  69.3 9.0 %answer_queries.1.answer_ref = f32[1024,512]{1,0:T(8,128)} custom-call(f32[1024,512]{1,0:T(8,128)} %bitcast.38, bf16[2048,512]{1,0:T(8,128)(2,1)} %get-tuple-element.54.high_ref, bf16[2048,512]{1,0:T(8,128)(2,1)} %get-tuple-element.55.low_ref), custom_call_target="tpu_custom_call" | custom-call | tf_op jit(solution)/shard_map/answer_queries/pallas_call | solution.py:415
  78.3 6.6 %all-gather.2.cloned.1.call-done.neg_ref = f32[1024,512]{1,0:T(8,128)} async-done(((f32[64,512]{1,0:T(8,128)}), f32[1024,512]{1,0:T(8,128)}) %all-gather.2.cloned.1.call-update) | async-done | bytes 2097168 | tf_op jit(solution)/shard_map/all_gather | solution.py:399
  84.9 4.4 %collective-permute-done.3.neg_ref = f32[1024,512]{1,0:T(8,128)S(1)} collective-permute-done((f32[1024,512]{1,0:T(8,128)}, f32[1024,512]{1,0:T(8,128)S(1)}, u32[]{:S(2)}, u32[]{:S(2)}) %collective-permute-start.3) | collective-permute-done | bytes 2097184 | tf_op jit(solution)/shard_map/ppermute | solution.py:425
  91.2 11.8 %score.2 = (f32[1024,512]{1,0:T(8,128)}, f32[512,512]{1,0:T(8,128)}, f32[512,128]{1,0:T(8,128)}) custom-call(f32[512,512]{1,0:T(8,128)} %get-tuple-element.48.query_ref, f32[1024,512]{1,0:T(8,128)} %copy-done.7, f32[512,512]{1,0:T(8,128)} %broadcast_in_dim.12.grad_in, f32[512,128]{1,0:T(8,128)} %broadcast_in_dim.13.loss_in), custom_call_target="tpu_custom_call" | custom-call | flops 10000000000 | bytes 8000000 | tf_op jit(solution)/shard_map/score/pallas_call | solution.py:429
  103.1 8.2 %all-to-all-start.1 = ((f32[128,8,512]{2,1,0:T(8,128)}), f32[128,8,512]{2,1,0:T(8,128)S(1)}, u32[]{:S(2)}, u32[]{:S(2)}) async-start(f32[128,8,512]{2,1,0:T(8,128)} %bitcast.13), calls=%async_computation.1 | async-start | bytes 4194304 | tf_op jit(solution)/shard_map/all_to_all | solution.py:395
  111.5 11.7 %score.3 = (f32[1024,512]{1,0:T(8,128)}, f32[512,512]{1,0:T(8,128)}, f32[512,128]{1,0:T(8,128)}) custom-call(f32[512,512]{1,0:T(8,128)} %get-tuple-element.48.query_ref, f32[1024,512]{1,0:T(8,128)} %all-gather.2.cloned.1.call-done.neg_ref, f32[512,512]{1,0:T(8,128)} %get-tuple-element.57.grad_in, f32[512,128]{1,0:T(8,128)} %get-tuple-element.58.loss_in), custom_call_target="tpu_custom_call" | custom-call | flops 10000000000 | bytes 8000000 | tf_op jit(solution)/shard_map/score/pallas_call | solution.py:429
  123.2 4.0 %add.66 = f32[1024,512]{1,0:T(8,128)} add(f32[1024,512]{1,0:T(8,128)} %get-tuple-element.59, f32[1024,512]{1,0:T(8,128)} %collective-permute-done.4) | non-fusion elementwise | flops 524288 | bytes 6291456 | tf_op jit(solution)/shard_map/add | solution.py:443
  127.3 14.3 %all-to-all-done.1 = f32[128,8,512]{2,1,0:T(8,128)S(1)} async-done(((f32[128,8,512]{2,1,0:T(8,128)}), f32[128,8,512]{2,1,0:T(8,128)S(1)}, u32[]{:S(2)}, u32[]{:S(2)}) %all-to-all-start.1) | async-done | bytes 2097184 | tf_op jit(solution)/shard_map/all_to_all | solution.py:395
  142.9 8.2 %close_triples.1 = (f32[512,512]{1,0:T(8,128)}, f32[64,40,128]{2,1,0:T(8,128)}, f32[64,40,128]{2,1,0:T(8,128)}, f32[1,512]{1,0:T(1,128)}) custom-call(s32[1]{0:T(128)} %bitcast.core_ref, f32[1024,512]{1,0:T(8,128)} %bitcast.40, s32[512,128]{1,0:T(8,128)} %get-tuple-element.63.place_ref, f32[512,512]{1,0:T(8,128)} %get-tuple-element.64.headv_ref, ...), custom_call_target="tpu_custom_call" | custom-call | tf_op jit(solution)/shard_map/close_triples/pallas_call | solution.py:451
  151.1 3.2 %collective-permute-done.5 = f32[64,40,128]{2,1,0:T(8,128)S(1)} collective-permute-done((f32[64,40,128]{2,1,0:T(8,128)}, f32[64,40,128]{2,1,0:T(8,128)S(1)}, u32[]{:S(2)}, u32[]{:S(2)}) %collective-permute-start.5) | collective-permute-done | bytes 1310752 | tf_op jit(solution)/shard_map/ppermute | solution.py:462
  154.4 2.5 add.67
  156.9 4.9 %all-to-all-start.2 = ((f32[64,40,128]{2,1,0:T(8,128)}), f32[64,40,128]{2,1,0:T(8,128)S(1)}, u32[]{:S(2)}, u32[]{:S(2)}) async-start(f32[64,40,128]{2,1,0:T(8,128)} %add.67), calls=%async_computation.2 | async-start | bytes 2621440 | tf_op jit(solution)/shard_map/all_to_all | solution.py:466
  161.8 12.9 %scatter_entities.1.grad_ref = f32[400,2048]{1,0:T(8,128)} custom-call(s32[1,512]{1,0:T(1,128)} %bitcast.53, f32[512,512]{1,0:T(8,128)} %get-tuple-element.71.gradh_ref, f32[1024,512]{1,0:T(8,128)} %bitcast.39, f32[1024,512]{1,0:T(8,128)} %answer_queries.1.answer_ref), custom_call_target="tpu_custom_call" | custom-call | flops 10000000000 | bytes 12000000 | tf_op jit(solution)/shard_map/scatter_entities/pallas_call | solution.py:470
  174.7 9.2 %all-to-all-done.2.sums_ref = f32[64,40,128]{2,1,0:T(8,128)S(1)} async-done(((f32[64,40,128]{2,1,0:T(8,128)}), f32[64,40,128]{2,1,0:T(8,128)S(1)}, u32[]{:S(2)}, u32[]{:S(2)}) %all-to-all-start.2) | async-done | bytes 1310752 | tf_op jit(solution)/shard_map/all_to_all | solution.py:466
  185.0 2.7 %update_own.1 = f32[64,40,128]{2,1,0:T(8,128)} custom-call(f32[64,40,128]{2,1,0:T(8,128)} %copy-done.3, f32[40,128]{1,0:T(8,128)} %get-tuple-element.75.mine_ref), custom_call_target="tpu_custom_call" | custom-call | tf_op jit(solution)/shard_map/update_own/pallas_call | solution.py:492
  187.7 26.6 %all_to_all.20.mine_ref = f32[64,40,128]{2,1,0:T(8,128)S(1)} all-to-all(f32[64,40,128]{2,1,0:T(8,128)} %update_own.1), channel_id=1, replica_groups=mesh['z'=4,'x'=4,'y'=4,'core'=2] {'z','x','y'}, dimensions={0} | all-to-all | bytes 2621440 | tf_op jit(solution)/shard_map/all_to_all | solution.py:500
  214.3 1.5 dynamic-slice_bitcast_fusion
  216.6 2.2 collective-permute-start.7
  218.8 3.5 %collective-permute-done.6 = f32[64,512]{1,0:T(8,128)S(1)} collective-permute-done((f32[64,512]{1,0:T(8,128)S(1)}, f32[64,512]{1,0:T(8,128)S(1)}, u32[]{:S(2)}, u32[]{:S(2)}) %collective-permute-start.6) | collective-permute-done | bytes 131104 | tf_op jit(solution)/shard_map/ppermute | solution.py:340
  222.2 2.1 collective-permute-done.7
  224.4 1.7 collective-permute-done.8
  228.9 2.6 %collective-permute-start.9 = (f32[16,512]{1,0:T(8,128)S(1)}, f32[16,512]{1,0:T(8,128)S(1)}, u32[]{:S(2)}, u32[]{:S(2)}) collective-permute-start(f32[16,512]{1,0:T(8,128)S(1)} %get-tuple-element.92), channel_id=1, source_target_pairs={{32,0},{64,32},{96,64},{0,96},{33,1},{65,33},{97,65},{1,97},{34,2}... | collective-permute-start | bytes 98312 | tf_op jit(solution)/shard_map/ppermute | solution.py:340
  234.6 6.4 %update_entities.1 = (f32[400,2048]{1,0:T(8,128)}, f32[1,2048]{1,0:T(1,128)}) custom-call(s32[16,128]{1,0:T(8,128)} %broadcast_in_dim.14.rows_ref, f32[16,512]{1,0:T(8,128)} %fusion.1.neg_ref, f32[400,2048]{1,0:T(8,128)} %bitcast.37, f32[1,2048]{1,0:T(1,128)} %bitcast.48, f32[400,2048]{1,0:T(8,128)} %scatter_entities.1.grad_ref), custom_call_target="tpu_custom_call" | custom-call | flops 1000000000 | bytes 14000000 | tf_op jit(solution)/shard_map/update_entities/pallas_call | solution.py:502
  242.1 4.0 %place_new.1 = (f32[400,1024]{1,0:T(8,128)}, f32[1,1024]{1,0:T(1,128)}, f32[400,512]{1,0:T(8,128)}, f32[1,512]{1,0:T(1,128)}) custom-call(s32[1]{0:T(128)} %bitcast.core_ref, f32[64,40,128]{2,1,0:T(8,128)} %copy-done.2, f32[64,40,128]{2,1,0:T(8,128)} %copy-done.4), custom_call_target="tpu_custom_call" | custom-call | tf_op jit(solution)/shard_map/place_new/pallas_call | solution.py:530
  (44 shorter events, 14.2 us)
Async XLA Ops:
  7.2 77.7 %all-gather.2.cloned.1.call-start = ((), (), s32[]{:S(2)}) async-start(), calls=%async_computation.5 | async-start | bytes 2228224 | tf_op jit(solution)/shard_map/all_gather | solution.py:399
  10.8 15.9 %collective-permute-start = (f32[16,512]{1,0:T(8,128)}, f32[16,512]{1,0:T(8,128)S(1)}, u32[]{:S(2)}, u32[]{:S(2)}) collective-permute-start(f32[16,512]{1,0:T(8,128)} %pick_negatives.1), channel_id=1, source_target_pairs={{0,32},{32,64},{64,96},{96,0},{1,33},{33,65},{65,97},{97,1},{2,34}... | collective-permute-start | bytes 98312 | tf_op jit(solution)/shard_map/ppermute | solution.py:334
  12.8 13.9 %collective-permute-start.1 = (f32[16,512]{1,0:T(8,128)}, f32[16,512]{1,0:T(8,128)S(1)}, u32[]{:S(2)}, u32[]{:S(2)}) collective-permute-start(f32[16,512]{1,0:T(8,128)} %pick_negatives.1), channel_id=1, source_target_pairs={{0,64},{32,96},{64,0},{96,32},{1,65},{33,97},{65,1},{97,33},{2,66}... | collective-permute-start | bytes 98312 | tf_op jit(solution)/shard_map/ppermute | solution.py:334
  16.3 10.4 %collective-permute-start.2 = (f32[16,512]{1,0:T(8,128)}, f32[16,512]{1,0:T(8,128)S(1)}, u32[]{:S(2)}, u32[]{:S(2)}) collective-permute-start(f32[16,512]{1,0:T(8,128)} %pick_negatives.1), channel_id=1, source_target_pairs={{0,96},{32,0},{64,32},{96,64},{1,97},{33,1},{65,33},{97,65},{2,98}... | collective-permute-start | bytes 98312 | tf_op jit(solution)/shard_map/ppermute | solution.py:334
  17.4 9.4 %copy-start.5 = (f32[16,512]{1,0:T(8,128)S(1)}, f32[16,512]{1,0:T(8,128)}, u32[]{:S(2)}) copy-start(f32[16,512]{1,0:T(8,128)} %pick_negatives.1) | copy-start | bytes 98308
  27.4 40.5 %all-to-all-start = ((f32[128,8,512]{2,1,0:T(8,128)}), f32[128,8,512]{2,1,0:T(8,128)S(1)}, u32[]{:S(2)}, u32[]{:S(2)}) async-start(f32[128,8,512]{2,1,0:T(8,128)} %bitcast.45), calls=%async_computation | async-start | bytes 4194304 | tf_op jit(solution)/shard_map/all_to_all | solution.py:395
  67.9 1.3 copy-start
  84.9 4.4 %collective-permute-start.3 = (f32[1024,512]{1,0:T(8,128)}, f32[1024,512]{1,0:T(8,128)S(1)}, u32[]{:S(2)}, u32[]{:S(2)}) collective-permute-start(f32[1024,512]{1,0:T(8,128)} %all-gather.2.cloned.1.call-done.neg_ref), channel_id=1, source_target_pairs={{0,1},{1,0},{2,3},{3,2},{4,5},{5,4},{6,7},{7,6},{8,9},{9,8},{10,11... | collective-permute-start | bytes 6291464 | tf_op jit(solution)/shard_map/ppermute | solution.py:425
  89.2 1.9 copy-start.7
  102.9 20.3 %collective-permute-start.4 = (f32[1024,512]{1,0:T(8,128)}, f32[1024,512]{1,0:T(8,128)}, u32[]{:S(2)}, u32[]{:S(2)}) collective-permute-start(f32[1024,512]{1,0:T(8,128)} %get-tuple-element.60), channel_id=1, source_target_pairs={{0,1},{1,0},{2,3},{3,2},{4,5},{5,4},{6,7},{7,6},{8,9},{9,8},{10,11... | collective-permute-start | bytes 6291464 | tf_op jit(solution)/shard_map/ppermute | solution.py:441
  103.1 38.5 %all-to-all-start.1 = ((f32[128,8,512]{2,1,0:T(8,128)}), f32[128,8,512]{2,1,0:T(8,128)S(1)}, u32[]{:S(2)}, u32[]{:S(2)}) async-start(f32[128,8,512]{2,1,0:T(8,128)} %bitcast.13), calls=%async_computation.1 | async-start | bytes 4194304 | tf_op jit(solution)/shard_map/all_to_all | solution.py:395
  111.2 103.1 %reduce-scatter.2.cloned.1.call-start = ((), (), s32[]{:S(2)}) async-start(), calls=%async_computation.6 | async-start | bytes 2621440 | tf_op jit(solution)/shard_map/reduce_scatter | solution.py:444
  141.6 1.3 copy-start.1
  151.1 3.2 %collective-permute-start.5 = (f32[64,40,128]{2,1,0:T(8,128)}, f32[64,40,128]{2,1,0:T(8,128)S(1)}, u32[]{:S(2)}, u32[]{:S(2)}) collective-permute-start(f32[64,40,128]{2,1,0:T(8,128)} %get-tuple-element.69), channel_id=1, source_target_pairs={{0,1},{1,0},{2,3},{3,2},{4,5},{5,4},{6,7},{7,6},{8,9},{9,8},{10,11... | collective-permute-start | bytes 3932168 | tf_op jit(solution)/shard_map/ppermute | solution.py:462
  156.9 27.1 %all-to-all-start.2 = ((f32[64,40,128]{2,1,0:T(8,128)}), f32[64,40,128]{2,1,0:T(8,128)S(1)}, u32[]{:S(2)}, u32[]{:S(2)}) async-start(f32[64,40,128]{2,1,0:T(8,128)} %add.67), calls=%async_computation.2 | async-start | bytes 2621440 | tf_op jit(solution)/shard_map/all_to_all | solution.py:466
  184.0 1.1 copy-start.3
  187.7 46.3 %copy-start.6 = (s32[16]{0:T(128)S(1)}, s32[16]{0:T(128)}, u32[]{:S(2)}) copy-start(s32[16]{0:T(128)} %rows_ref.1) | copy-start | bytes 196
  214.3 26.7 %copy-start.2 = (f32[64,40,128]{2,1,0:T(8,128)}, f32[64,40,128]{2,1,0:T(8,128)S(1)}, u32[]{:S(2)}) copy-start(f32[64,40,128]{2,1,0:T(8,128)S(1)} %all_to_all.20.mine_ref) | copy-start | bytes 3932164
  214.3 26.7 %collective-permute-start.12 = (f32[64,40,128]{2,1,0:T(8,128)S(1)}, f32[64,40,128]{2,1,0:T(8,128)S(1)}, u32[]{:S(2)}, u32[]{:S(2)}) collective-permute-start(f32[64,40,128]{2,1,0:T(8,128)S(1)} %all_to_all.20.mine_ref), channel_id=1, source_target_pairs={{0,1},{1,0},{2,3},{3,2},{4,5},{5,4},{6,7},{7,6},{8,9},{9,8},{10,11... | collective-permute-start | bytes 3932168 | tf_op jit(solution)/shard_map/ppermute | solution.py:528
  215.8 6.4 %collective-permute-start.6 = (f32[64,512]{1,0:T(8,128)S(1)}, f32[64,512]{1,0:T(8,128)S(1)}, u32[]{:S(2)}, u32[]{:S(2)}) collective-permute-start(f32[64,512]{1,0:T(8,128)S(1)} %get-tuple-element.89), channel_id=1, source_target_pairs={{2,0},{4,2},{6,4},{0,6},{3,1},{5,3},{7,5},{1,7},{10,8},{12,10},{14... | collective-permute-start | bytes 393224 | tf_op jit(solution)/shard_map/ppermute | solution.py:340
  216.6 7.8 %collective-permute-start.7 = (f32[64,512]{1,0:T(8,128)S(1)}, f32[64,512]{1,0:T(8,128)S(1)}, u32[]{:S(2)}, u32[]{:S(2)}) collective-permute-start(f32[64,512]{1,0:T(8,128)S(1)} %get-tuple-element.88), channel_id=1, source_target_pairs={{4,0},{6,2},{0,4},{2,6},{5,1},{7,3},{1,5},{3,7},{12,8},{14,10},{8,... | collective-permute-start | bytes 393224 | tf_op jit(solution)/shard_map/ppermute | solution.py:340
  218.8 7.3 %collective-permute-start.8 = (f32[64,512]{1,0:T(8,128)S(1)}, f32[64,512]{1,0:T(8,128)S(1)}, u32[]{:S(2)}, u32[]{:S(2)}) collective-permute-start(f32[64,512]{1,0:T(8,128)S(1)} %get-tuple-element.87), channel_id=1, source_target_pairs={{6,0},{0,2},{2,4},{4,6},{7,1},{1,3},{3,5},{5,7},{14,8},{8,10},{10,... | collective-permute-start | bytes 393224 | tf_op jit(solution)/shard_map/ppermute | solution.py:340
  227.0 5.5 %collective-permute-start.10 = (f32[16,512]{1,0:T(8,128)S(1)}, f32[16,512]{1,0:T(8,128)S(1)}, u32[]{:S(2)}, u32[]{:S(2)}) collective-permute-start(f32[16,512]{1,0:T(8,128)S(1)} %get-tuple-element.91), channel_id=1, source_target_pairs={{64,0},{96,32},{0,64},{32,96},{65,1},{97,33},{1,65},{33,97},{66,2}... | collective-permute-start | bytes 98312 | tf_op jit(solution)/shard_map/ppermute | solution.py:340
  228.2 5.1 %collective-permute-start.11 = (f32[16,512]{1,0:T(8,128)S(1)}, f32[16,512]{1,0:T(8,128)S(1)}, u32[]{:S(2)}, u32[]{:S(2)}) collective-permute-start(f32[16,512]{1,0:T(8,128)S(1)} %get-tuple-element.90), channel_id=1, source_target_pairs={{96,0},{0,32},{32,64},{64,96},{97,1},{1,33},{33,65},{65,97},{98,2}... | collective-permute-start | bytes 98312 | tf_op jit(solution)/shard_map/ppermute | solution.py:340
  228.9 4.5 %collective-permute-start.9 = (f32[16,512]{1,0:T(8,128)S(1)}, f32[16,512]{1,0:T(8,128)S(1)}, u32[]{:S(2)}, u32[]{:S(2)}) collective-permute-start(f32[16,512]{1,0:T(8,128)S(1)} %get-tuple-element.92), channel_id=1, source_target_pairs={{32,0},{64,32},{96,64},{0,96},{33,1},{65,33},{97,65},{1,97},{34,2}... | collective-permute-start | bytes 98312 | tf_op jit(solution)/shard_map/ppermute | solution.py:340
  241.0 1.1 copy-start.4
Sparse Core Ops, SparseCore 0:
  27.5 57.2 all-gather.1
  141.7 24.9 reduce-scatter.1

commit v4 on v3

--- a/solution.py
+++ b/solution.py
@@ -166,25 +166,55 @@
     out_ref[...] = jnp.where(iota(tails.shape, 1) == AUX, positive, slope * tails)
 
 
-def score(query_ref, neg_ref, grad_in, loss_in, back_ref, grad_ref, loss_ref):
-    qh, ql = split(query_ref[...])
-    grad, total = grad_in[...], loss_in[...]
+def log_one_plus(x):
+    series = x * (1.0 - x * (0.5 - x * (1.0 / 3.0)))
+    return jnp.where(x < 1e-3, series, jnp.log(1.0 + x))
+
+
+def score(core_ref, query_ref, neg_ref, near_ref, far_ref, grad_ref, loss_ref, qh_ref, ql_ref):
+    side = pl.program_id(0)
+
+    @pl.when((side == 0) & (pl.program_id(1) == 0))
+    def _():
+        high, low = split(query_ref[...])
+        qh_ref[...] = high
+        ql_ref[...] = low
+        grad_ref[...] = jnp.zeros_like(grad_ref)
+        loss_ref[...] = jnp.zeros_like(loss_ref)
+
+    qh, ql = qh_ref[...], ql_ref[...]
+    grad, total = grad_ref[...], loss_ref[...]
+    negs = neg_ref[...].reshape(-1, WIDE)
     step = 256
-    for first in range(0, neg_ref.shape[0], step):
-        nh, nl = split(neg_ref[first : first + step, :])
+    backs = []
+    for first in range(0, negs.shape[0], step):
+        nh, nl = split(negs[first : first + step, :])
         nt = ((1,), (1,))
         s = dot(qh, nh, nt) + (dot(qh, nl, nt) + dot(ql, nh, nt))
         small = jnp.exp(-jnp.abs(s))
-        loss = jnp.maximum(s, 0.0) + jnp.log1p(small)
+        loss = jnp.maximum(s, 0.0) + log_one_plus(small)
         for part in range(step // 128):
             total = total + loss[:, part * 128 : (part + 1) * 128]
-        weight = jnp.where(s >= 0.0, 1.0, small) / (1.0 + small) * (1.0 / ENT_NEGS)
+        whole = 1.0 + small
+        turn = pl.reciprocal(whole, approx=True)
+        turn = turn * (2.0 - whole * turn)
+        weight = jnp.where(s >= 0.0, turn, small * turn)
         gh, gl = split(weight)
         grad = grad + (dot(gh, nh) + (dot(gh, nl) + dot(gl, nh)))
         tn = ((0,), (0,))
-        back_ref[first : first + step, :] = dot(gh, qh, tn) + (dot(gh, ql, tn) + dot(gl, qh, tn))
+        back = dot(gh, qh, tn) + (dot(gh, ql, tn) + dot(gl, qh, tn))
+        backs.append(back * (1.0 / ENT_NEGS))
     grad_ref[...] = grad
     loss_ref[...] = total
+    back = jnp.concatenate(backs, axis=0).reshape(near_ref.shape)
+
+    @pl.when(side == 0)
+    def _():
+        near_ref[...] = back
+
+    @pl.when(side == 1)
+    def _():
+        far_ref[...] = back
 
 
 ENT_NEGS = 2 * CHIP_COUNT * NEG
@@ -204,7 +234,7 @@
     drop = -positive
     loss = jnp.maximum(drop, 0.0) + jnp.log1p(jnp.exp(-jnp.abs(drop))) + neg_loss
     out_ref[...] = jnp.broadcast_to(loss, (TRIP, 128)).T[:1]
-    grad = without_aux(tail) + gradq_ref[...]
+    grad = without_aux(tail) + gradq_ref[...] * (1.0 / ENT_NEGS)
     g_re, g_im = grad[:, :SIDE], grad[:, SIDE:]
     heads, rels = headv_ref[...], relv_ref[...]
     h_re, h_im, r_re, r_im = heads[:, :SIDE], heads[:, SIDE:], rels[:, :SIDE], rels[:, SIDE:]
@@ -396,7 +426,7 @@
         return got.reshape(SLOTS, WIDE)
 
     sent, near, own_arg = lax.optimization_barrier((sent, near, own_arg))
-    near = lax.all_gather(near, ("x", "y"), axis=0, tiled=True)
+    near = lax.all_gather(near, ("x", "y", "core"), axis=0, tiled=True)
     asked = exchange(sent)
     ent_high, ent_low, mine_rows = pl.pallas_call(
         turn_tables,
@@ -407,7 +437,7 @@
         out_specs=[VMEM] * 3,
         scratch_shapes=[pltpu.VMEM((WIDE, 128), F32)],
         compiler_params=params(),
-        cost_estimate=cost(1e6, 12e6),
+        cost_estimate=cost(1e6, 1e5),
         name="turn_tables",
     )(own_arg, ent_t, hub_t, rel_t, hub_accum.reshape(1, HUB), relation_accum.reshape(1, REL))
 
@@ -421,45 +451,68 @@
         compiler_params=params(),
         name="answer_queries",
     )(asked, ent_high, ent_low)
-    near, answer = lax.optimization_barrier((near, answer))
-    far = lax.ppermute(near, "core", SWAP)
+    near, _ = lax.optimization_barrier((near, answer))
     back = exchange(answer)
 
-    def scored(block, grad, loss):
-        return pl.pallas_call(
-            score,
-            out_shape=[shape(*block.shape), shape(TRIP, WIDE), shape(TRIP, 128)],
-            in_specs=[VMEM] * 4,
-            out_specs=[VMEM] * 3,
-            compiler_params=params(),
-            cost_estimate=cost(10e9, 8e6),
-            name="score",
-        )(query, block, grad, loss)
-
-    zeros = jnp.zeros((TRIP, WIDE), F32), jnp.zeros((TRIP, 128), F32)
-    far_back, grad_q, loss_sum = scored(far, *zeros)
+    group, steps, places = 8, 2, 16
+    near_back, far_back, grad_q, loss_sum = pl.pallas_call(
+        score,
+        out_shape=[
+            shape(places, 4 * NEG, WIDE), shape(places, 4 * NEG, WIDE), shape(TRIP, WIDE),
+            shape(TRIP, 128),
+        ],
+        grid_spec=pltpu.PrefetchScalarGridSpec(
+            num_scalar_prefetch=1,
+            grid=(2, steps),
+            in_specs=[
+                pl.BlockSpec((TRIP, WIDE), lambda i, c, core: (0, 0)),
+                pl.BlockSpec(
+                    (group, 1, 4 * NEG, WIDE), lambda i, c, core: (c, (i + core[0]) % 2, 0, 0)
+                ),
+            ],
+            out_specs=[
+                pl.BlockSpec(
+                    (group, 4 * NEG, WIDE),
+                    lambda i, c, core: (jnp.where(i == 0, c, steps - 1), 0, 0),
+                ),
+                pl.BlockSpec(
+                    (group, 4 * NEG, WIDE), lambda i, c, core: (jnp.where(i == 0, 0, c), 0, 0)
+                ),
+                pl.BlockSpec((TRIP, WIDE), lambda i, c, core: (0, 0)),
+                pl.BlockSpec((TRIP, 128), lambda i, c, core: (0, 0)),
+            ],
+            scratch_shapes=[pltpu.VMEM((TRIP, WIDE), BF16), pltpu.VMEM((TRIP, WIDE), BF16)],
+        ),
+        compiler_params=params(),
+        cost_estimate=cost(20e9, 12e6),
+        name="score",
+    )(core_arg, query, near.reshape(places, 2, 4 * NEG, WIDE))
+    near_back, far_back = near_back.reshape(-1, WIDE), far_back.reshape(-1, WIDE)
+
+    far_back, back = lax.optimization_barrier((far_back, back))
     far_back = lax.ppermute(far_back, "core", SWAP)
-    near_back, grad_q, loss_sum = scored(near, grad_q, loss_sum)
-    part, back = lax.optimization_barrier((near_back + far_back, back))
+    grad_head, both_mine, both_other, loss = pl.pallas_call(
+        close_triples,
+        out_shape=[
+            shape(TRIP, WIDE), shape(CHIP_COUNT, OWN, 128), shape(CHIP_COUNT, OWN, 128),
+            shape(1, TRIP),
+        ],
+        in_specs=[SMEM] + [VMEM] * 8,
+        out_specs=[VMEM] * 4,
+        compiler_params=params(),
+        name="close_triples",
+    )(core_arg, back, place, heads, rels, grad_q, loss_sum, head_row, rel_row)
+    both_swapped = lax.ppermute(both_other, "core", SWAP)
+
+    near_back, _ = lax.optimization_barrier((near_back, both_other))
+    part = near_back + far_back
+    part, both_mine = lax.optimization_barrier((part, both_mine))
     part = lax.psum_scatter(part, "x", scatter_dimension=0, tiled=True)
     y = lax.axis_index("y").astype(I32)
     blocks = part.reshape(4, 4 * NEG, WIDE)
     blocks = [lax.dynamic_index_in_dim(blocks, (y + 4 - k) & 3, 0, keepdims=False) for k in range(4)]
     part = add_around(blocks, "y")
     neg_grad = add_around(jnp.split(part, 4, axis=0), "z")
-
-    grad_head, both_mine, both_other, loss = pl.pallas_call(
-        close_triples,
-        out_shape=[
-            shape(TRIP, WIDE), shape(CHIP_COUNT, OWN, 128), shape(CHIP_COUNT, OWN, 128),
-            shape(1, TRIP),
-        ],
-        in_specs=[SMEM] + [VMEM] * 8,
-        out_specs=[VMEM] * 4,
-        compiler_params=params(),
-        name="close_triples",
-    )(core_arg, back, place, heads, rels, grad_q, loss_sum, head_row, rel_row)
-    both_swapped = lax.ppermute(both_other, "core", SWAP)
 
     paired = both_mine + both_swapped
     paired, asked, answer = lax.optimization_barrier((paired, asked, answer))
@@ -484,7 +537,7 @@
             pltpu.VMEM((SLOTS, 128), I32),
         ],
         compiler_params=params(),
-        cost_estimate=cost(10e9, 12e6),
+        cost_estimate=cost(1e6, 1e5),
         name="scatter_entities",
     )(head_row, grad_head, asked, answer)
 
@@ -515,7 +568,7 @@
             pl.BlockSpec((1, columns), lambda i: (0, i)),
         ],
         compiler_params=params(),
-        cost_estimate=cost(1e9, 14e6),
+        cost_estimate=cost(1e6, 1e5),
         name="update_entities",
     )(
         jnp.broadcast_to(negative_rows[:, None], (NEG, 128)),
@@ -525,8 +578,8 @@
         entity_grad,
     )
 
+    new_mine, entity_new = lax.optimization_barrier((new_mine, entity_new))
     new_other = lax.ppermute(new_mine, "core", SWAP)
-    new_mine, entity_new = lax.optimization_barrier((new_mine, entity_new))
     hub_new, hub_accum_new, rel_new, rel_accum_new = pl.pallas_call(
         place_new,
         out_shape=[shape(WIDTH, HUB), shape(1, HUB), shape(WIDTH, REL), shape(1, REL)],

time: 254 us -> 232 us (0.913)
  blocking collectives: 26.6 us -> 0 us
  waiting for transfers between devices: 72.1 us -> 81.2 us
  other arithmetic: 8.76 us -> 5.23 us
  starting transfers between devices: 35.5 us -> 38.7 us
    all_to_all x1 -> x0, blocking collectives: 26.6 us -> none  [body(): lax.all_to_all(own_new, CHIPS, split_axis=0, concat_axis=0, tiled=True)]
    ppermute x6, waiting for transfers between devices: 9.2 us -> 20.8 us  [add_around(): lax.ppermute(blocks[k + 1], axis, turn)]
    all_to_all x1, waiting for transfers between devices: 9.22 us -> 20.3 us  [body(): lax.all_to_all(paired, CHIPS, split_axis=0, concat_axis=0, tiled=True)]
    all_to_all x2, waiting for transfers between devices: 39.5 us -> 31.4 us  [exchange(): got = lax.all_to_all(parts, SHARD, split_axis=0, concat_axis=0, tiled=True)]
    all_to_all x0 -> x1, starting transfers between devices: none -> 5.13 us  [body(): lax.all_to_all(own_new, CHIPS, split_axis=0, concat_axis=0, tiled=True)]
    ppermute x1 -> x0, waiting for transfers between devices: 4.37 us -> none  [body(): far = lax.ppermute(near, 'core', SWAP)]
    all_gather x1, waiting for transfers between devices: 6.56 us -> 2.52 us  [body(): near = lax.all_gather(near, ('x', 'y', 'core'), axis=0, tiled=True)]
    ppermute x1, waiting for transfers between devices: 0.01 us -> 3.02 us  [body(): new_other = lax.ppermute(new_mine, 'core', SWAP)]
  transfers between devices with their start and end apart: 18 -> 18, of which waited for: 11 -> 11; matrix products, arithmetic and copies ran while one was open for 4% -> 2% of each run, Pallas kernels for 27% -> 34%
where the time goes in v4:
time: 232 us; the launch traced here: 231 us
  Pallas kernels  84.9 us (37%)
  waiting for transfers between devices  81.2 us (35%)
  starting transfers between devices  38.7 us (17%)
  between operations  14.2 us (6%)
  local copies, waits for them, and re-layouts  6.62 us (3%)
  other arithmetic  5.23 us (2%)
    all_to_all x2, waiting for transfers between devices, exchange(): got = lax.all_to_all(parts, SHARD, split_axis=0, concat_axis=0, tiled=True)  31.4 us
    pallas_call x1, Pallas kernels, body(): pl.pallas_call(score, out_shape=[shape(places, 4 * NEG, WIDE), shape(plac...  21.4 us
    ppermute x6, waiting for transfers between devices, add_around(): lax.ppermute(blocks[k + 1], axis, turn)  20.8 us
    all_to_all x1, waiting for transfers between devices, body(): lax.all_to_all(paired, CHIPS, split_axis=0, concat_axis=0, tiled=True)  20.3 us
    all_to_all x2, starting transfers between devices, exchange(): got = lax.all_to_all(parts, SHARD, split_axis=0, concat_axis=0, tiled=True)  14 us
    pallas_call x1, Pallas kernels, body(): pl.pallas_call(scatter_entities, out_shape=shape(WIDTH, ENT), grid=(ENT /...  13 us
    pallas_call x1, Pallas kernels, body(): pl.pallas_call(prepare, out_shape=[shape(TRIP, WIDE), shape(TRIP, WIDE),...  9.35 us
    ppermute x6, starting transfers between devices, add_around(): lax.ppermute(blocks[k + 1], axis, turn)  9.13 us
  transfers between devices with their start and end apart: 18, of which 11 were waited for; matrix products, arithmetic and copies ran while one was open for 2% of the time, Pallas kernels for 34%

profile of v4, /device:TPU:0, one launch (start us, length us, event | category | flops | bytes accessed | tf_op | source)
XLA Modules:
  0.0 230.8 jit_solution(9595363638964968509)
XLA Ops:
  7.2 3.6 %pick_negatives.1 = f32[16,512]{1,0:T(8,128)} custom-call(s32[16]{0:T(128)} %rows_ref.1, f32[400,2048]{1,0:T(8,128)} %bitcast.37), custom_call_target="tpu_custom_call" | custom-call | tf_op jit(solution)/shard_map/pick_negatives/pallas_call | solution.py:399
  10.8 4.1 %collective-permute-start.2 = (f32[16,512]{1,0:T(8,128)}, f32[16,512]{1,0:T(8,128)S(1)}, u32[]{:S(2)}, u32[]{:S(2)}) collective-permute-start(f32[16,512]{1,0:T(8,128)} %pick_negatives.1), channel_id=1, source_target_pairs={{0,96},{32,0},{64,32},{96,64},{1,97},{33,1},{65,33},{97,65},{2,98}... | collective-permute-start | bytes 98312 | tf_op jit(solution)/shard_map/ppermute | solution.py:364
  14.9 1.3 collective-permute-start
  16.2 9.4 %prepare.1 = (f32[512,512]{1,0:T(8,128)}, f32[512,512]{1,0:T(8,128)}, f32[512,512]{1,0:T(8,128)}, f32[1024,512]{1,0:T(8,128)}, s32[512,128]{1,0:T(8,128)}) custom-call(s32[1,512]{1,0:T(1,128)} %bitcast.53, s32[1,512]{1,0:T(1,128)} %bitcast.57, s32[1,512]{1,0:T(1,128)} %bitcast.60, s32[1,512]{1,0:T(1,128)} %bitcast.61, f32[400,2048]{1,0:T(8,128)} %bitcast.38, ...), custom_call_target="tpu_custom_call" | custom-call | tf_op jit(solution)/shard_map/prepare/pallas_call | solution.py:411
  26.2 9.3 %all-to-all-start = ((f32[128,8,512]{2,1,0:T(8,128)}), f32[128,8,512]{2,1,0:T(8,128)S(1)}, u32[]{:S(2)}, u32[]{:S(2)}) async-start(f32[128,8,512]{2,1,0:T(8,128)} %bitcast.50), calls=%async_computation | async-start | bytes 4194304 | tf_op jit(solution)/shard_map/all_to_all | solution.py:425
  35.5 7.3 %turn_tables.1 = (bf16[2048,512]{1,0:T(8,128)(2,1)}, bf16[2048,512]{1,0:T(8,128)(2,1)}, f32[40,128]{1,0:T(8,128)}) custom-call(s32[1]{0:T(128)} %bitcast.8.own_ref, f32[400,2048]{1,0:T(8,128)} %bitcast.39, f32[400,1024]{1,0:T(8,128)} %bitcast.46, f32[400,512]{1,0:T(8,128)} %bitcast.48, f32[1,1024]{1,0:T(1,128)} %bitcast.59, f32[1,512]{1,0:T(1,128)} %bitcast.62), custom_call_target="tpu_custom_call" | custom-call | flops 1000000 | bytes 100000 | tf_op jit(solution)/shard_map/turn_tables/pallas_call | solution.py:431
  42.8 25.2 %all-to-all-done = f32[128,8,512]{2,1,0:T(8,128)S(1)} async-done(((f32[128,8,512]{2,1,0:T(8,128)}), f32[128,8,512]{2,1,0:T(8,128)S(1)}, u32[]{:S(2)}, u32[]{:S(2)}) %all-to-all-start) | async-done | bytes 2097184 | tf_op jit(solution)/shard_map/all_to_all | solution.py:425
  68.0 1.4 copy-done
  69.4 9.1 %answer_queries.1.answer_ref = f32[1024,512]{1,0:T(8,128)} custom-call(f32[1024,512]{1,0:T(8,128)} %bitcast.41, bf16[2048,512]{1,0:T(8,128)(2,1)} %get-tuple-element.54.high_ref, bf16[2048,512]{1,0:T(8,128)(2,1)} %get-tuple-element.55.low_ref), custom_call_target="tpu_custom_call" | custom-call | tf_op jit(solution)/shard_map/answer_queries/pallas_call | solution.py:445
  78.5 4.6 %all-to-all-start.1 = ((f32[128,8,512]{2,1,0:T(8,128)}), f32[128,8,512]{2,1,0:T(8,128)S(1)}, u32[]{:S(2)}, u32[]{:S(2)}) async-start(f32[128,8,512]{2,1,0:T(8,128)} %bitcast.43), calls=%async_computation.1 | async-start | bytes 4194304 | tf_op jit(solution)/shard_map/all_to_all | solution.py:425
  83.3 2.5 %all-gather.2.cloned.1.call-done = f32[2048,512]{1,0:T(8,128)} async-done(((f32[64,512]{1,0:T(8,128)}), f32[2048,512]{1,0:T(8,128)}) %all-gather.2.cloned.1.call-update) | async-done | bytes 4194320 | tf_op jit(solution)/shard_map/all_gather | solution.py:429
  85.9 21.4 %score.1 = (f32[16,64,512]{2,1,0:T(8,128)}, f32[16,64,512]{2,1,0:T(8,128)}, f32[512,512]{1,0:T(8,128)}, f32[512,128]{1,0:T(8,128)}) custom-call(s32[1]{0:T(128)} %bitcast.core_ref, f32[512,512]{1,0:T(8,128)} %get-tuple-element.48.query_ref, f32[16,2,64,512]{3,2,1,0:T(8,128)} %bitcast.63), custom_call_target="tpu_custom_call" | custom-call | flops 20000000000 | bytes 12000000 | tf_op jit(solution)/shard_map/score/pallas_call | solution.py:458
  107.2 6.2 %all-to-all-done.1 = f32[128,8,512]{2,1,0:T(8,128)S(1)} async-done(((f32[128,8,512]{2,1,0:T(8,128)}), f32[128,8,512]{2,1,0:T(8,128)S(1)}, u32[]{:S(2)}, u32[]{:S(2)}) %all-to-all-start.1) | async-done | bytes 2097184 | tf_op jit(solution)/shard_map/all_to_all | solution.py:425
  113.5 1.3 copy-done.1
  114.8 8.3 %close_triples.1 = (f32[512,512]{1,0:T(8,128)}, f32[64,40,128]{2,1,0:T(8,128)}, f32[64,40,128]{2,1,0:T(8,128)}, f32[1,512]{1,0:T(1,128)}) custom-call(s32[1]{0:T(128)} %bitcast.core_ref, f32[1024,512]{1,0:T(8,128)} %bitcast.44, s32[512,128]{1,0:T(8,128)} %get-tuple-element.60.place_ref, f32[512,512]{1,0:T(8,128)} %get-tuple-element.61.headv_ref, ...), custom_call_target="tpu_custom_call" | custom-call | tf_op jit(solution)/shard_map/close_triples/pallas_call | solution.py:494
  123.1 1.8 add.66
  125.0 3.0 %collective-permute-done.4 = f32[64,40,128]{2,1,0:T(8,128)S(1)} collective-permute-done((f32[64,40,128]{2,1,0:T(8,128)S(1)}, f32[64,40,128]{2,1,0:T(8,128)S(1)}, u32[]{:S(2)}, u32[]{:S(2)}) %collective-permute-start.4) | collective-permute-done | bytes 1310752 | tf_op jit(solution)/shard_map/ppermute | solution.py:505
  128.1 1.2 add.67
  129.3 4.7 %all-to-all-start.2 = ((f32[64,40,128]{2,1,0:T(8,128)}), f32[64,40,128]{2,1,0:T(8,128)S(1)}, u32[]{:S(2)}, u32[]{:S(2)}) async-start(f32[64,40,128]{2,1,0:T(8,128)} %add.67), calls=%async_computation.2 | async-start | bytes 2621440 | tf_op jit(solution)/shard_map/all_to_all | solution.py:519
  133.9 13.0 %scatter_entities.1.grad_ref = f32[400,2048]{1,0:T(8,128)} custom-call(s32[1,512]{1,0:T(1,128)} %bitcast.55, f32[512,512]{1,0:T(8,128)} %get-tuple-element.71.gradh_ref, f32[1024,512]{1,0:T(8,128)} %bitcast.42, f32[1024,512]{1,0:T(8,128)} %answer_queries.1.answer_ref), custom_call_target="tpu_custom_call" | custom-call | flops 1000000 | bytes 100000 | tf_op jit(solution)/shard_map/scatter_entities/pallas_call | solution.py:523
  146.9 20.3 %all-to-all-done.2.sums_ref = f32[64,40,128]{2,1,0:T(8,128)S(1)} async-done(((f32[64,40,128]{2,1,0:T(8,128)}), f32[64,40,128]{2,1,0:T(8,128)S(1)}, u32[]{:S(2)}, u32[]{:S(2)}) %all-to-all-start.2) | async-done | bytes 1310752 | tf_op jit(solution)/shard_map/all_to_all | solution.py:519
  168.3 2.7 %update_own.1 = f32[64,40,128]{2,1,0:T(8,128)} custom-call(f32[64,40,128]{2,1,0:T(8,128)} %copy-done.3, f32[40,128]{1,0:T(8,128)} %get-tuple-element.75.mine_ref), custom_call_target="tpu_custom_call" | custom-call | tf_op jit(solution)/shard_map/update_own/pallas_call | solution.py:545
  171.0 5.1 %all-to-all-start.3 = ((f32[64,40,128]{2,1,0:T(8,128)}), f32[64,40,128]{2,1,0:T(8,128)S(1)}, u32[]{:S(2)}, u32[]{:S(2)}) async-start(f32[64,40,128]{2,1,0:T(8,128)} %update_own.1), calls=%async_computation.3 | async-start | bytes 2621440 | tf_op jit(solution)/shard_map/all_to_all | solution.py:553
  177.2 2.9 %collective-permute-start.5 = (f32[64,512]{1,0:T(8,128)S(1)}, f32[64,512]{1,0:T(8,128)S(1)}, u32[]{:S(2)}, u32[]{:S(2)}) collective-permute-start(f32[64,512]{1,0:T(8,128)S(1)} %get-tuple-element.89), channel_id=1, source_target_pairs={{2,0},{4,2},{6,4},{0,6},{3,1},{5,3},{7,5},{1,7},{10,8},{12,10},{14... | collective-permute-start | bytes 393224 | tf_op jit(solution)/shard_map/ppermute | solution.py:370
  181.8 13.8 %collective-permute-done.5 = f32[64,512]{1,0:T(8,128)S(1)} collective-permute-done((f32[64,512]{1,0:T(8,128)S(1)}, f32[64,512]{1,0:T(8,128)S(1)}, u32[]{:S(2)}, u32[]{:S(2)}) %collective-permute-start.5) | collective-permute-done | bytes 131104 | tf_op jit(solution)/shard_map/ppermute | solution.py:370
  195.6 1.4 collective-permute-done.6
  196.9 1.5 collective-permute-done.7
  199.4 3.0 %collective-permute-start.8 = (f32[16,512]{1,0:T(8,128)S(1)}, f32[16,512]{1,0:T(8,128)S(1)}, u32[]{:S(2)}, u32[]{:S(2)}) collective-permute-start(f32[16,512]{1,0:T(8,128)S(1)} %get-tuple-element.92), channel_id=1, source_target_pairs={{32,0},{64,32},{96,64},{0,96},{33,1},{65,33},{97,65},{1,97},{34,2}... | collective-permute-start | bytes 98312 | tf_op jit(solution)/shard_map/ppermute | solution.py:370
  204.0 3.8 %collective-permute-done.9 = f32[16,512]{1,0:T(8,128)S(1)} collective-permute-done((f32[16,512]{1,0:T(8,128)S(1)}, f32[16,512]{1,0:T(8,128)S(1)}, u32[]{:S(2)}, u32[]{:S(2)}) %collective-permute-start.9) | collective-permute-done | bytes 32800 | tf_op jit(solution)/shard_map/ppermute | solution.py:370
  209.5 6.4 %update_entities.1 = (f32[400,2048]{1,0:T(8,128)}, f32[1,2048]{1,0:T(1,128)}) custom-call(s32[16,128]{1,0:T(8,128)} %broadcast_in_dim.2.rows_ref, f32[16,512]{1,0:T(8,128)} %fusion.1.neg_ref, f32[400,2048]{1,0:T(8,128)} %bitcast.40, f32[1,2048]{1,0:T(1,128)} %bitcast.56, f32[400,2048]{1,0:T(8,128)} %scatter_entities.1.grad_ref), custom_call_target="tpu_custom_call" | custom-call | flops 1000000 | bytes 100000 | tf_op jit(solution)/shard_map/update_entities/pallas_call | solution.py:555
  215.9 3.0 %collective-permute-done.11.other_ref = f32[64,40,128]{2,1,0:T(8,128)S(1)} collective-permute-done((f32[64,40,128]{2,1,0:T(8,128)S(1)}, f32[64,40,128]{2,1,0:T(8,128)S(1)}, u32[]{:S(2)}, u32[]{:S(2)}) %collective-permute-start.11) | collective-permute-done | bytes 1310752 | tf_op jit(solution)/shard_map/ppermute | solution.py:582
  220.0 4.0 %place_new.1 = (f32[400,1024]{1,0:T(8,128)}, f32[1,1024]{1,0:T(1,128)}, f32[400,512]{1,0:T(8,128)}, f32[1,512]{1,0:T(1,128)}) custom-call(s32[1]{0:T(128)} %bitcast.core_ref, f32[64,40,128]{2,1,0:T(8,128)} %copy-done.2, f32[64,40,128]{2,1,0:T(8,128)} %copy-done.5), custom_call_target="tpu_custom_call" | custom-call | tf_op jit(solution)/shard_map/place_new/pallas_call | solution.py:583
  (44 shorter events, 10.3 us)
Async XLA Ops:
  7.2 78.7 %all-gather.2.cloned.1.call-start = ((), (), s32[]{:S(2)}) async-start(), calls=%async_computation.5 | async-start | bytes 4325376 | tf_op jit(solution)/shard_map/all_gather | solution.py:429
  10.8 14.7 %collective-permute-start.2 = (f32[16,512]{1,0:T(8,128)}, f32[16,512]{1,0:T(8,128)S(1)}, u32[]{:S(2)}, u32[]{:S(2)}) collective-permute-start(f32[16,512]{1,0:T(8,128)} %pick_negatives.1), channel_id=1, source_target_pairs={{0,96},{32,0},{64,32},{96,64},{1,97},{33,1},{65,33},{97,65},{2,98}... | collective-permute-start | bytes 98312 | tf_op jit(solution)/shard_map/ppermute | solution.py:364
  14.9 10.6 %collective-permute-start.1 = (f32[16,512]{1,0:T(8,128)}, f32[16,512]{1,0:T(8,128)S(1)}, u32[]{:S(2)}, u32[]{:S(2)}) collective-permute-start(f32[16,512]{1,0:T(8,128)} %pick_negatives.1), channel_id=1, source_target_pairs={{0,64},{32,96},{64,0},{96,32},{1,65},{33,97},{65,1},{97,33},{2,66}... | collective-permute-start | bytes 98312 | tf_op jit(solution)/shard_map/ppermute | solution.py:364
  14.9 10.6 %collective-permute-start = (f32[16,512]{1,0:T(8,128)}, f32[16,512]{1,0:T(8,128)S(1)}, u32[]{:S(2)}, u32[]{:S(2)}) collective-permute-start(f32[16,512]{1,0:T(8,128)} %pick_negatives.1), channel_id=1, source_target_pairs={{0,32},{32,64},{64,96},{96,0},{1,33},{33,65},{65,97},{97,1},{2,34}... | collective-permute-start | bytes 98312 | tf_op jit(solution)/shard_map/ppermute | solution.py:364
  16.2 9.4 %copy-start.7 = (f32[16,512]{1,0:T(8,128)S(1)}, f32[16,512]{1,0:T(8,128)}, u32[]{:S(2)}) copy-start(f32[16,512]{1,0:T(8,128)} %pick_negatives.1) | copy-start | bytes 98308
  26.2 41.8 %all-to-all-start = ((f32[128,8,512]{2,1,0:T(8,128)}), f32[128,8,512]{2,1,0:T(8,128)S(1)}, u32[]{:S(2)}, u32[]{:S(2)}) async-start(f32[128,8,512]{2,1,0:T(8,128)} %bitcast.50), calls=%async_computation | async-start | bytes 4194304 | tf_op jit(solution)/shard_map/all_to_all | solution.py:425
  68.0 1.4 copy-start
  78.5 35.0 %all-to-all-start.1 = ((f32[128,8,512]{2,1,0:T(8,128)}), f32[128,8,512]{2,1,0:T(8,128)S(1)}, u32[]{:S(2)}, u32[]{:S(2)}) async-start(f32[128,8,512]{2,1,0:T(8,128)} %bitcast.43), calls=%async_computation.1 | async-start | bytes 4194304 | tf_op jit(solution)/shard_map/all_to_all | solution.py:425
  83.1 93.0 %reduce-scatter.2.cloned.1.call-start = ((), (), s32[]{:S(2)}) async-start(), calls=%async_computation.6 | async-start | bytes 2621440 | tf_op jit(solution)/shard_map/reduce_scatter | solution.py:510
  113.5 1.4 copy-start.1
  113.5 9.6 %collective-permute-start.3 = (f32[1024,512]{1,0:T(8,128)}, f32[1024,512]{1,0:T(8,128)S(1)}, u32[]{:S(2)}, u32[]{:S(2)}) collective-permute-start(f32[1024,512]{1,0:T(8,128)} %bitcast.65), channel_id=1, source_target_pairs={{0,1},{1,0},{2,3},{3,2},{4,5},{5,4},{6,7},{7,6},{8,9},{9,8},{10,11... | collective-permute-start | bytes 6291464 | tf_op jit(solution)/shard_map/ppermute | solution.py:493
  114.8 8.3 %copy-start.4 = (f32[16,64,512]{2,1,0:T(8,128)S(1)}, f32[16,64,512]{2,1,0:T(8,128)}, u32[]{:S(2)}) copy-start(f32[16,64,512]{2,1,0:T(8,128)} %get-tuple-element.57) | copy-start | bytes 6291460
  123.1 1.8 copy-start.9
  124.9 3.2 %copy-start.6 = (f32[64,40,128]{2,1,0:T(8,128)S(1)}, f32[64,40,128]{2,1,0:T(8,128)}, u32[]{:S(2)}) copy-start(f32[64,40,128]{2,1,0:T(8,128)} %get-tuple-element.69) | copy-start | bytes 3932164
  125.0 3.1 %collective-permute-start.4 = (f32[64,40,128]{2,1,0:T(8,128)S(1)}, f32[64,40,128]{2,1,0:T(8,128)S(1)}, u32[]{:S(2)}, u32[]{:S(2)}) collective-permute-start(f32[64,40,128]{2,1,0:T(8,128)S(1)} %copy-done.9), channel_id=1, source_target_pairs={{0,1},{1,0},{2,3},{3,2},{4,5},{5,4},{6,7},{7,6},{8,9},{9,8},{10,11... | collective-permute-start | bytes 3932168 | tf_op jit(solution)/shard_map/ppermute | solution.py:505
  129.3 38.0 %all-to-all-start.2 = ((f32[64,40,128]{2,1,0:T(8,128)}), f32[64,40,128]{2,1,0:T(8,128)S(1)}, u32[]{:S(2)}, u32[]{:S(2)}) async-start(f32[64,40,128]{2,1,0:T(8,128)} %add.67), calls=%async_computation.2 | async-start | bytes 2621440 | tf_op jit(solution)/shard_map/all_to_all | solution.py:519
  167.2 1.1 copy-start.3
  171.0 37.8 %copy-start.8 = (s32[16]{0:T(128)S(1)}, s32[16]{0:T(128)}, u32[]{:S(2)}) copy-start(s32[16]{0:T(128)} %rows_ref.1) | copy-start | bytes 196
  171.0 44.9 %all-to-all-start.3 = ((f32[64,40,128]{2,1,0:T(8,128)}), f32[64,40,128]{2,1,0:T(8,128)S(1)}, u32[]{:S(2)}, u32[]{:S(2)}) async-start(f32[64,40,128]{2,1,0:T(8,128)} %update_own.1), calls=%async_computation.3 | async-start | bytes 2621440 | tf_op jit(solution)/shard_map/all_to_all | solution.py:553
  177.2 18.4 %collective-permute-start.5 = (f32[64,512]{1,0:T(8,128)S(1)}, f32[64,512]{1,0:T(8,128)S(1)}, u32[]{:S(2)}, u32[]{:S(2)}) collective-permute-start(f32[64,512]{1,0:T(8,128)S(1)} %get-tuple-element.89), channel_id=1, source_target_pairs={{2,0},{4,2},{6,4},{0,6},{3,1},{5,3},{7,5},{1,7},{10,8},{12,10},{14... | collective-permute-start | bytes 393224 | tf_op jit(solution)/shard_map/ppermute | solution.py:370
  180.1 16.9 %collective-permute-start.6 = (f32[64,512]{1,0:T(8,128)S(1)}, f32[64,512]{1,0:T(8,128)S(1)}, u32[]{:S(2)}, u32[]{:S(2)}) collective-permute-start(f32[64,512]{1,0:T(8,128)S(1)} %get-tuple-element.88), channel_id=1, source_target_pairs={{4,0},{6,2},{0,4},{2,6},{5,1},{7,3},{1,5},{3,7},{12,8},{14,10},{8,... | collective-permute-start | bytes 393224 | tf_op jit(solution)/shard_map/ppermute | solution.py:370
  180.9 17.5 %collective-permute-start.7 = (f32[64,512]{1,0:T(8,128)S(1)}, f32[64,512]{1,0:T(8,128)S(1)}, u32[]{:S(2)}, u32[]{:S(2)}) collective-permute-start(f32[64,512]{1,0:T(8,128)S(1)} %get-tuple-element.87), channel_id=1, source_target_pairs={{6,0},{0,2},{2,4},{4,6},{7,1},{1,3},{3,5},{5,7},{14,8},{8,10},{10,... | collective-permute-start | bytes 393224 | tf_op jit(solution)/shard_map/ppermute | solution.py:370
  199.4 4.6 %collective-permute-start.8 = (f32[16,512]{1,0:T(8,128)S(1)}, f32[16,512]{1,0:T(8,128)S(1)}, u32[]{:S(2)}, u32[]{:S(2)}) collective-permute-start(f32[16,512]{1,0:T(8,128)S(1)} %get-tuple-element.92), channel_id=1, source_target_pairs={{32,0},{64,32},{96,64},{0,96},{33,1},{65,33},{97,65},{1,97},{34,2}... | collective-permute-start | bytes 98312 | tf_op jit(solution)/shard_map/ppermute | solution.py:370
  202.4 5.4 %collective-permute-start.9 = (f32[16,512]{1,0:T(8,128)S(1)}, f32[16,512]{1,0:T(8,128)S(1)}, u32[]{:S(2)}, u32[]{:S(2)}) collective-permute-start(f32[16,512]{1,0:T(8,128)S(1)} %get-tuple-element.91), channel_id=1, source_target_pairs={{64,0},{96,32},{0,64},{32,96},{65,1},{97,33},{1,65},{33,97},{66,2}... | collective-permute-start | bytes 98312 | tf_op jit(solution)/shard_map/ppermute | solution.py:370
  203.0 5.1 %collective-permute-start.10 = (f32[16,512]{1,0:T(8,128)S(1)}, f32[16,512]{1,0:T(8,128)S(1)}, u32[]{:S(2)}, u32[]{:S(2)}) collective-permute-start(f32[16,512]{1,0:T(8,128)S(1)} %get-tuple-element.90), channel_id=1, source_target_pairs={{96,0},{0,32},{32,64},{64,96},{97,1},{1,33},{33,65},{65,97},{98,2}... | collective-permute-start | bytes 98312 | tf_op jit(solution)/shard_map/ppermute | solution.py:370
  215.8 3.1 %copy-start.2 = (f32[64,40,128]{2,1,0:T(8,128)}, f32[64,40,128]{2,1,0:T(8,128)S(1)}, u32[]{:S(2)}) copy-start(f32[64,40,128]{2,1,0:T(8,128)S(1)} %all-to-all-done.3.mine_ref) | copy-start | bytes 3932164
  215.8 3.1 %collective-permute-start.11 = (f32[64,40,128]{2,1,0:T(8,128)S(1)}, f32[64,40,128]{2,1,0:T(8,128)S(1)}, u32[]{:S(2)}, u32[]{:S(2)}) collective-permute-start(f32[64,40,128]{2,1,0:T(8,128)S(1)} %all-to-all-done.3.mine_ref), channel_id=1, source_target_pairs={{0,1},{1,0},{2,3},{3,2},{4,5},{5,4},{6,7},{7,6},{8,9},{9,8},{10,11... | collective-permute-start | bytes 3932168 | tf_op jit(solution)/shard_map/ppermute | solution.py:582
  219.0 1.1 copy-start.5
Sparse Core Ops, SparseCore 0:
  26.3 59.4 all-gather.1
  125.1 38.1 reduce-scatter.1

commit v5 on v4

--- a/solution.py
+++ b/solution.py
@@ -171,7 +171,7 @@
     return jnp.where(x < 1e-3, series, jnp.log(1.0 + x))
 
 
-def score(core_ref, query_ref, neg_ref, near_ref, far_ref, grad_ref, loss_ref, qh_ref, ql_ref):
+def score(at_ref, query_ref, neg_ref, near_ref, far_ref, grad_ref, loss_ref, qh_ref, ql_ref):
     side = pl.program_id(0)
 
     @pl.when((side == 0) & (pl.program_id(1) == 0))
@@ -187,10 +187,10 @@
     negs = neg_ref[...].reshape(-1, WIDE)
     step = 256
     backs = []
+    q_cols, q_rows = jnp.concatenate([qh, qh, ql], axis=1), jnp.concatenate([qh, ql, qh], axis=0)
     for first in range(0, negs.shape[0], step):
         nh, nl = split(negs[first : first + step, :])
-        nt = ((1,), (1,))
-        s = dot(qh, nh, nt) + (dot(qh, nl, nt) + dot(ql, nh, nt))
+        s = dot(q_cols, jnp.concatenate([nh, nl, nh], axis=1), ((1,), (1,)))
         small = jnp.exp(-jnp.abs(s))
         loss = jnp.maximum(s, 0.0) + log_one_plus(small)
         for part in range(step // 128):
@@ -200,21 +200,26 @@
         turn = turn * (2.0 - whole * turn)
         weight = jnp.where(s >= 0.0, turn, small * turn)
         gh, gl = split(weight)
-        grad = grad + (dot(gh, nh) + (dot(gh, nl) + dot(gl, nh)))
-        tn = ((0,), (0,))
-        back = dot(gh, qh, tn) + (dot(gh, ql, tn) + dot(gl, qh, tn))
+        grad = grad + dot(
+            jnp.concatenate([gh, gh, gl], axis=1), jnp.concatenate([nh, nl, nh], axis=0)
+        )
+        back = dot(jnp.concatenate([gh, gh, gl], axis=0), q_rows, ((0,), (0,)))
         backs.append(back * (1.0 / ENT_NEGS))
     grad_ref[...] = grad
     loss_ref[...] = total
-    back = jnp.concatenate(backs, axis=0).reshape(near_ref.shape)
+    back = jnp.concatenate(backs, axis=0).reshape(-1, 4, NEG, WIDE)
+
+    def put(ref):
+        for k in range(4):
+            ref[(at_ref[1] + 4 - k) & 3] = back[:, k]
 
     @pl.when(side == 0)
     def _():
-        near_ref[...] = back
+        put(near_ref)
 
     @pl.when(side == 1)
     def _():
-        far_ref[...] = back
+        put(far_ref)
 
 
 ENT_NEGS = 2 * CHIP_COUNT * NEG
@@ -338,14 +343,20 @@
                 relacc_ref[:, at] = last[88:89]
 
 
-def update_entities(rows_ref, neg_ref, ent_ref, acc_ref, grad_ref, new_ref, newacc_ref):
+def update_entities(rows_ref, neg_ref, ent_ref, acc_ref, grad_ref, new_ref, newacc_ref,
+                    high_ref, low_ref):
+    @pl.when(pl.program_id(0) == 0)
+    def _():
+        high, low = split(jnp.sum(neg_ref[...], axis=0))
+        high_ref[...] = high
+        low_ref[...] = low
+
     count = ent_ref.shape[1]
     first = pl.program_id(0) * count
     rows = rows_ref[...][:, :1]
     marks = hot(iota((NEG, count), 1) + first == rows)
-    high, low = split(neg_ref[...])
     tn = ((0,), (0,))
-    more = dot(high, marks, tn) + dot(low, marks, tn)
+    more = dot(high_ref[...], marks, tn) + dot(low_ref[...], marks, tn)
     g_re = grad_ref[:HALF, :] + more[:HALF]
     g_im = grad_ref[HALF:, :] + more[SIDE : SIDE + HALF]
     square = jnp.sum(g_re * g_re, axis=0, keepdims=True) + jnp.sum(
@@ -362,13 +373,6 @@
     count = SIZES[SHARD.index(axis)]
     turns = [[(i, (i + k) % count) for i in range(count)] for k in range(1, count)]
     return [block] + [lax.ppermute(block, axis, turn) for turn in turns]
-
-
-def add_around(blocks, axis):
-    count = SIZES[SHARD.index(axis)]
-    turns = [[((i + k) % count, i) for i in range(count)] for k in range(1, count)]
-    one, two, three = [lax.ppermute(blocks[k + 1], axis, turn) for k, turn in enumerate(turns)]
-    return (blocks[0] + one) + (two + three)
 
 
 def shape(*dims, dtype=F32):
@@ -458,39 +462,44 @@
     near_back, far_back, grad_q, loss_sum = pl.pallas_call(
         score,
         out_shape=[
-            shape(places, 4 * NEG, WIDE), shape(places, 4 * NEG, WIDE), shape(TRIP, WIDE),
+            shape(4, places, NEG, WIDE), shape(4, places, NEG, WIDE), shape(TRIP, WIDE),
             shape(TRIP, 128),
         ],
         grid_spec=pltpu.PrefetchScalarGridSpec(
             num_scalar_prefetch=1,
             grid=(2, steps),
             in_specs=[
-                pl.BlockSpec((TRIP, WIDE), lambda i, c, core: (0, 0)),
+                pl.BlockSpec((TRIP, WIDE), lambda i, c, at: (0, 0)),
                 pl.BlockSpec(
-                    (group, 1, 4 * NEG, WIDE), lambda i, c, core: (c, (i + core[0]) % 2, 0, 0)
+                    (group, 1, 4 * NEG, WIDE), lambda i, c, at: (c, (i + at[0]) % 2, 0, 0)
                 ),
             ],
             out_specs=[
                 pl.BlockSpec(
-                    (group, 4 * NEG, WIDE),
-                    lambda i, c, core: (jnp.where(i == 0, c, steps - 1), 0, 0),
+                    (4, group, NEG, WIDE),
+                    lambda i, c, at: (0, jnp.where(i == 0, c, steps - 1), 0, 0),
                 ),
                 pl.BlockSpec(
-                    (group, 4 * NEG, WIDE), lambda i, c, core: (jnp.where(i == 0, 0, c), 0, 0)
+                    (4, group, NEG, WIDE), lambda i, c, at: (0, jnp.where(i == 0, 0, c), 0, 0)
                 ),
-                pl.BlockSpec((TRIP, WIDE), lambda i, c, core: (0, 0)),
-                pl.BlockSpec((TRIP, 128), lambda i, c, core: (0, 0)),
+                pl.BlockSpec((TRIP, WIDE), lambda i, c, at: (0, 0)),
+                pl.BlockSpec((TRIP, 128), lambda i, c, at: (0, 0)),
             ],
             scratch_shapes=[pltpu.VMEM((TRIP, WIDE), BF16), pltpu.VMEM((TRIP, WIDE), BF16)],
         ),
         compiler_params=params(),
         cost_estimate=cost(20e9, 12e6),
         name="score",
-    )(core_arg, query, near.reshape(places, 2, 4 * NEG, WIDE))
-    near_back, far_back = near_back.reshape(-1, WIDE), far_back.reshape(-1, WIDE)
-
+    )(
+        jnp.stack([core, lax.axis_index("z").astype(I32)]),
+        query,
+        near.reshape(places, 2, 4 * NEG, WIDE),
+    )
     far_back, back = lax.optimization_barrier((far_back, back))
-    far_back = lax.ppermute(far_back, "core", SWAP)
+    part = near_back + lax.ppermute(far_back, "core", SWAP)
+    part, back = lax.optimization_barrier((part.reshape(CHIP_COUNT, NEG, WIDE), back))
+    neg_sums = lax.all_to_all(part, CHIPS, split_axis=0, concat_axis=0, tiled=True)
+
     grad_head, both_mine, both_other, loss = pl.pallas_call(
         close_triples,
         out_shape=[
@@ -504,18 +513,8 @@
     )(core_arg, back, place, heads, rels, grad_q, loss_sum, head_row, rel_row)
     both_swapped = lax.ppermute(both_other, "core", SWAP)
 
-    near_back, _ = lax.optimization_barrier((near_back, both_other))
-    part = near_back + far_back
-    part, both_mine = lax.optimization_barrier((part, both_mine))
-    part = lax.psum_scatter(part, "x", scatter_dimension=0, tiled=True)
-    y = lax.axis_index("y").astype(I32)
-    blocks = part.reshape(4, 4 * NEG, WIDE)
-    blocks = [lax.dynamic_index_in_dim(blocks, (y + 4 - k) & 3, 0, keepdims=False) for k in range(4)]
-    part = add_around(blocks, "y")
-    neg_grad = add_around(jnp.split(part, 4, axis=0), "z")
-
     paired = both_mine + both_swapped
-    paired, asked, answer = lax.optimization_barrier((paired, asked, answer))
+    paired, neg_sums, asked, answer = lax.optimization_barrier((paired, neg_sums, asked, answer))
     sums = lax.all_to_all(paired, CHIPS, split_axis=0, concat_axis=0, tiled=True)
 
     columns = 256
@@ -558,7 +557,7 @@
         grid=(ENT // columns,),
         in_specs=[
             pl.BlockSpec((NEG, 128), lambda i: (0, 0)),
-            pl.BlockSpec((NEG, WIDE), lambda i: (0, 0)),
+            pl.BlockSpec((CHIP_COUNT, NEG, WIDE), lambda i: (0, 0, 0)),
             pl.BlockSpec((WIDTH, columns), lambda i: (0, i)),
             pl.BlockSpec((1, columns), lambda i: (0, i)),
             pl.BlockSpec((WIDTH, columns), lambda i: (0, i)),
@@ -567,12 +566,13 @@
             pl.BlockSpec((WIDTH, columns), lambda i: (0, i)),
             pl.BlockSpec((1, columns), lambda i: (0, i)),
         ],
+        scratch_shapes=[pltpu.VMEM((NEG, WIDE), BF16), pltpu.VMEM((NEG, WIDE), BF16)],
         compiler_params=params(),
         cost_estimate=cost(1e6, 1e5),
         name="update_entities",
     )(
         jnp.broadcast_to(negative_rows[:, None], (NEG, 128)),
-        neg_grad,
+        neg_sums,
         ent_t,
         entity_accum.reshape(1, ENT),
         entity_grad,

time: 232 us -> 227 us (0.978)
  waiting for transfers between devices: 81.2 us -> 78.2 us
  starting transfers between devices: 38.7 us -> 35.8 us
  local copies, waits for them, and re-layouts: 6.62 us -> 4.16 us
    ppermute x7 -> x1, waiting for transfers between devices: 20.8 us -> 4.37 us  [body(): part = near_back + lax.ppermute(far_back, 'core', SWAP)]
    all_to_all x0 -> x1, waiting for transfers between devices: none -> 16.2 us  [body(): lax.all_to_all(part, CHIPS, split_axis=0, concat_axis=0, tiled=True)]
    all_to_all x1, waiting for transfers between devices: 20.3 us -> 7.42 us  [body(): lax.all_to_all(paired, CHIPS, split_axis=0, concat_axis=0, tiled=True)]
    all_to_all x1, waiting for transfers between devices: 0.01 us -> 11.1 us  [body(): lax.all_to_all(own_new, CHIPS, split_axis=0, concat_axis=0, tiled=True)]
    ppermute x7 -> x1, starting transfers between devices: 9.14 us -> 0.01 us  [body(): part = near_back + lax.ppermute(far_back, 'core', SWAP)]
    all_to_all x0 -> x1, starting transfers between devices: none -> 4.7 us  [body(): lax.all_to_all(part, CHIPS, split_axis=0, concat_axis=0, tiled=True)]
    unnamed x20 -> x16, local copies, waits for them, and re-layouts: 4.87 us -> 3.49 us
  transfers between devices with their start and end apart: 18 -> 12, of which waited for: 11 -> 9; matrix products, arithmetic and copies ran while one was open for 2% -> 2% of each run, Pallas kernels for 34% -> 34%
where the time goes in v5:
time: 227 us; the launch traced here: 226 us
  Pallas kernels  86.1 us (38%)
  waiting for transfers between devices  78.2 us (34%)
  starting transfers between devices  35.8 us (16%)
  between operations  14.1 us (6%)
  other arithmetic  7.16 us (3%)
  local copies, waits for them, and re-layouts  4.16 us (2%)
    all_to_all x2, waiting for transfers between devices, exchange(): got = lax.all_to_all(parts, SHARD, split_axis=0, concat_axis=0, tiled=True)  30.7 us
    pallas_call x1, Pallas kernels, body(): pl.pallas_call(score, out_shape=[shape(4, places, NEG, WIDE), shape(4, pl...  21.8 us
    all_to_all x1, waiting for transfers between devices, body(): lax.all_to_all(part, CHIPS, split_axis=0, concat_axis=0, tiled=True)  16.2 us
    pallas_call x1, Pallas kernels, body(): pl.pallas_call(scatter_entities, out_shape=shape(WIDTH, ENT), grid=(ENT /...  12.9 us
    all_to_all x2, starting transfers between devices, exchange(): got = lax.all_to_all(parts, SHARD, split_axis=0, concat_axis=0, tiled=True)  12.9 us
    all_to_all x1, waiting for transfers between devices, body(): lax.all_to_all(own_new, CHIPS, split_axis=0, concat_axis=0, tiled=True)  11.1 us
    pallas_call x1, Pallas kernels, body(): pl.pallas_call(prepare, out_shape=[shape(TRIP, WIDE), shape(TRIP, WIDE),...  9.35 us
    pallas_call x1, Pallas kernels, body(): pl.pallas_call(answer_queries, out_shape=shape(SLOTS, WIDE), grid=(SLOTS...  9.1 us
  transfers between devices with their start and end apart: 12, of which 9 were waited for; matrix products, arithmetic and copies ran while one was open for 2% of the time, Pallas kernels for 34%

profile of v5, /device:TPU:0, one launch (start us, length us, event | category | flops | bytes accessed | tf_op | source)
XLA Modules:
  0.0 225.6 jit_solution(6025560503312893999)
XLA Ops:
  7.2 3.5 %pick_negatives.1 = f32[16,512]{1,0:T(8,128)} custom-call(s32[16]{0:T(128)} %rows_ref.1, f32[400,2048]{1,0:T(8,128)} %bitcast.26), custom_call_target="tpu_custom_call" | custom-call | tf_op jit(solution)/shard_map/pick_negatives/pallas_call | solution.py:403
  10.8 2.0 collective-permute-start
  12.8 3.6 %collective-permute-start.1 = (f32[16,512]{1,0:T(8,128)}, f32[16,512]{1,0:T(8,128)S(1)}, u32[]{:S(2)}, u32[]{:S(2)}) collective-permute-start(f32[16,512]{1,0:T(8,128)} %pick_negatives.1), channel_id=1, source_target_pairs={{0,64},{32,96},{64,0},{96,32},{1,65},{33,97},{65,1},{97,33},{2,66}... | collective-permute-start | bytes 98312 | tf_op jit(solution)/shard_map/ppermute | solution.py:375
  16.4 1.0 collective-permute-start.2
  17.4 9.4 %prepare.1 = (f32[512,512]{1,0:T(8,128)}, f32[512,512]{1,0:T(8,128)}, f32[512,512]{1,0:T(8,128)}, f32[1024,512]{1,0:T(8,128)}, s32[512,128]{1,0:T(8,128)}) custom-call(s32[1,512]{1,0:T(1,128)} %bitcast.39, s32[1,512]{1,0:T(1,128)} %bitcast.42, s32[1,512]{1,0:T(1,128)} %bitcast.46, s32[1,512]{1,0:T(1,128)} %bitcast.47, f32[400,2048]{1,0:T(8,128)} %bitcast.27, ...), custom_call_target="tpu_custom_call" | custom-call | tf_op jit(solution)/shard_map/prepare/pallas_call | solution.py:415
  27.4 8.1 %all-to-all-start = ((f32[128,8,512]{2,1,0:T(8,128)}), f32[128,8,512]{2,1,0:T(8,128)S(1)}, u32[]{:S(2)}, u32[]{:S(2)}) async-start(f32[128,8,512]{2,1,0:T(8,128)} %bitcast.38), calls=%async_computation | async-start | bytes 4194304 | tf_op jit(solution)/shard_map/all_to_all | solution.py:429
  35.5 7.3 %turn_tables.1 = (bf16[2048,512]{1,0:T(8,128)(2,1)}, bf16[2048,512]{1,0:T(8,128)(2,1)}, f32[40,128]{1,0:T(8,128)}) custom-call(s32[1]{0:T(128)} %bitcast.9.own_ref, f32[400,2048]{1,0:T(8,128)} %bitcast.28, f32[400,1024]{1,0:T(8,128)} %bitcast.35, f32[400,512]{1,0:T(8,128)} %bitcast.37, f32[1,1024]{1,0:T(1,128)} %bitcast.45, f32[1,512]{1,0:T(1,128)} %bitcast.48), custom_call_target="tpu_custom_call" | custom-call | flops 1000000 | bytes 100000 | tf_op jit(solution)/shard_map/turn_tables/pallas_call | solution.py:435
  42.8 25.2 %all-to-all-done = f32[128,8,512]{2,1,0:T(8,128)S(1)} async-done(((f32[128,8,512]{2,1,0:T(8,128)}), f32[128,8,512]{2,1,0:T(8,128)S(1)}, u32[]{:S(2)}, u32[]{:S(2)}) %all-to-all-start) | async-done | bytes 2097184 | tf_op jit(solution)/shard_map/all_to_all | solution.py:429
  68.0 1.3 copy-done
  69.3 9.1 %answer_queries.1.answer_ref = f32[1024,512]{1,0:T(8,128)} custom-call(f32[1024,512]{1,0:T(8,128)} %bitcast.30, bf16[2048,512]{1,0:T(8,128)(2,1)} %get-tuple-element.54.high_ref, bf16[2048,512]{1,0:T(8,128)(2,1)} %get-tuple-element.55.low_ref), custom_call_target="tpu_custom_call" | custom-call | tf_op jit(solution)/shard_map/answer_queries/pallas_call | solution.py:449
  78.4 4.8 %all-to-all-start.1 = ((f32[128,8,512]{2,1,0:T(8,128)}), f32[128,8,512]{2,1,0:T(8,128)S(1)}, u32[]{:S(2)}, u32[]{:S(2)}) async-start(f32[128,8,512]{2,1,0:T(8,128)} %bitcast.32), calls=%async_computation.1 | async-start | bytes 4194304 | tf_op jit(solution)/shard_map/all_to_all | solution.py:429
  83.9 2.2 all-gather.2.cloned.1.call-done
  86.1 21.8 %score.1 = (f32[4,16,16,512]{3,2,1,0:T(8,128)}, f32[4,16,16,512]{3,2,1,0:T(8,128)}, f32[512,512]{1,0:T(8,128)}, f32[512,128]{1,0:T(8,128)}) custom-call(s32[2]{0:T(128)} %pad_add_fusion.at_ref, f32[512,512]{1,0:T(8,128)} %get-tuple-element.48.query_ref, f32[16,2,64,512]{3,2,1,0:T(8,128)} %bitcast.49), custom_call_target="tpu_custom_call" | custom-call | flops 20000000000 | bytes 12000000 | tf_op jit(solution)/shard_map/score/pallas_call | solution.py:462
  107.9 5.5 %all-to-all-done.1 = f32[128,8,512]{2,1,0:T(8,128)S(1)} async-done(((f32[128,8,512]{2,1,0:T(8,128)}), f32[128,8,512]{2,1,0:T(8,128)S(1)}, u32[]{:S(2)}, u32[]{:S(2)}) %all-to-all-start.1) | async-done | bytes 2097184 | tf_op jit(solution)/shard_map/all_to_all | solution.py:429
  113.4 4.4 %collective-permute-done.3 = f32[4,16,16,512]{3,2,1,0:T(8,128)S(1)} collective-permute-done((f32[4,16,16,512]{3,2,1,0:T(8,128)}, f32[4,16,16,512]{3,2,1,0:T(8,128)S(1)}, u32[]{:S(2)}, u32[]{:S(2)}) %collective-permute-start.3) | collective-permute-done | bytes 2097184 | tf_op jit(solution)/shard_map/ppermute | solution.py:499
  117.8 3.4 %add.18 = f32[4,16,16,512]{3,2,1,0:T(8,128)} add(f32[4,16,16,512]{3,2,1,0:T(8,128)} %get-tuple-element.57, f32[4,16,16,512]{3,2,1,0:T(8,128)S(1)} %collective-permute-done.3) | non-fusion elementwise | flops 524288 | bytes 6291456 | tf_op jit(solution)/shard_map/add | solution.py:499
  121.2 4.7 %all-to-all-start.2 = ((f32[64,16,512]{2,1,0:T(8,128)}), f32[64,16,512]{2,1,0:T(8,128)S(1)}, u32[]{:S(2)}, u32[]{:S(2)}) async-start(f32[64,16,512]{2,1,0:T(8,128)} %bitcast.17), calls=%async_computation.2 | async-start | bytes 4194304 | tf_op jit(solution)/shard_map/all_to_all | solution.py:501
  125.9 8.2 %close_triples.1 = (f32[512,512]{1,0:T(8,128)}, f32[64,40,128]{2,1,0:T(8,128)}, f32[64,40,128]{2,1,0:T(8,128)}, f32[1,512]{1,0:T(1,128)}) custom-call(s32[1]{0:T(128)} %bitcast.core_ref, f32[1024,512]{1,0:T(8,128)} %bitcast.33, s32[512,128]{1,0:T(8,128)} %get-tuple-element.62.place_ref, f32[512,512]{1,0:T(8,128)} %get-tuple-element.63.headv_ref, ...), custom_call_target="tpu_custom_call" | custom-call | tf_op jit(solution)/shard_map/close_triples/pallas_call | solution.py:503
  134.3 3.1 %collective-permute-done.4 = f32[64,40,128]{2,1,0:T(8,128)S(1)} collective-permute-done((f32[64,40,128]{2,1,0:T(8,128)}, f32[64,40,128]{2,1,0:T(8,128)S(1)}, u32[]{:S(2)}, u32[]{:S(2)}) %collective-permute-start.4) | collective-permute-done | bytes 1310752 | tf_op jit(solution)/shard_map/ppermute | solution.py:514
  137.4 2.5 %add.19 = f32[64,40,128]{2,1,0:T(8,128)} add(f32[64,40,128]{2,1,0:T(8,128)} %get-tuple-element.67, f32[64,40,128]{2,1,0:T(8,128)S(1)} %collective-permute-done.4) | non-fusion elementwise | flops 327680 | bytes 3932160 | tf_op jit(solution)/shard_map/add | solution.py:516
  139.9 16.2 %all-to-all-done.2.neg_ref = f32[64,16,512]{2,1,0:T(8,128)S(1)} async-done(((f32[64,16,512]{2,1,0:T(8,128)}), f32[64,16,512]{2,1,0:T(8,128)S(1)}, u32[]{:S(2)}, u32[]{:S(2)}) %all-to-all-start.2) | async-done | bytes 2097184 | tf_op jit(solution)/shard_map/all_to_all | solution.py:501
  156.1 6.3 %all-to-all-start.3 = ((f32[64,40,128]{2,1,0:T(8,128)}), f32[64,40,128]{2,1,0:T(8,128)S(1)}, u32[]{:S(2)}, u32[]{:S(2)}) async-start(f32[64,40,128]{2,1,0:T(8,128)} %add.19), calls=%async_computation.3 | async-start | bytes 2621440 | tf_op jit(solution)/shard_map/all_to_all | solution.py:518
  162.4 12.9 %scatter_entities.1.grad_ref = f32[400,2048]{1,0:T(8,128)} custom-call(s32[1,512]{1,0:T(1,128)} %bitcast.41, f32[512,512]{1,0:T(8,128)} %get-tuple-element.71.gradh_ref, f32[1024,512]{1,0:T(8,128)} %bitcast.31, f32[1024,512]{1,0:T(8,128)} %answer_queries.1.answer_ref), custom_call_target="tpu_custom_call" | custom-call | flops 1000000 | bytes 100000 | tf_op jit(solution)/shard_map/scatter_entities/pallas_call | solution.py:522
  175.4 7.4 %all-to-all-done.3.sums_ref = f32[64,40,128]{2,1,0:T(8,128)S(1)} async-done(((f32[64,40,128]{2,1,0:T(8,128)}), f32[64,40,128]{2,1,0:T(8,128)S(1)}, u32[]{:S(2)}, u32[]{:S(2)}) %all-to-all-start.3) | async-done | bytes 1310752 | tf_op jit(solution)/shard_map/all_to_all | solution.py:518
  182.8 1.1 copy-done.4
  183.8 2.7 %update_own.1 = f32[64,40,128]{2,1,0:T(8,128)} custom-call(f32[64,40,128]{2,1,0:T(8,128)} %copy-done.4, f32[40,128]{1,0:T(8,128)} %get-tuple-element.75.mine_ref), custom_call_target="tpu_custom_call" | custom-call | tf_op jit(solution)/shard_map/update_own/pallas_call | solution.py:544
  186.5 5.1 %all-to-all-start.4 = ((f32[64,40,128]{2,1,0:T(8,128)}), f32[64,40,128]{2,1,0:T(8,128)S(1)}, u32[]{:S(2)}, u32[]{:S(2)}) async-start(f32[64,40,128]{2,1,0:T(8,128)} %update_own.1), calls=%async_computation.4 | async-start | bytes 2621440 | tf_op jit(solution)/shard_map/all_to_all | solution.py:552
  192.3 7.2 %update_entities.1 = (f32[400,2048]{1,0:T(8,128)}, f32[1,2048]{1,0:T(1,128)}) custom-call(s32[16,128]{1,0:T(8,128)} %broadcast_in_dim.2.rows_ref, f32[64,16,512]{2,1,0:T(8,128)} %copy-done.1, f32[400,2048]{1,0:T(8,128)} %bitcast.29, f32[1,2048]{1,0:T(1,128)} %bitcast.44, f32[400,2048]{1,0:T(8,128)} %scatter_entities.1.grad_ref), custom_call_target="tpu_custom_call" | custom-call | flops 1000000 | bytes 100000 | tf_op jit(solution)/shard_map/update_entities/pallas_call | solution.py:554
  199.6 11.1 %all-to-all-done.4.mine_ref = f32[64,40,128]{2,1,0:T(8,128)S(1)} async-done(((f32[64,40,128]{2,1,0:T(8,128)}), f32[64,40,128]{2,1,0:T(8,128)S(1)}, u32[]{:S(2)}, u32[]{:S(2)}) %all-to-all-start.4) | async-done | bytes 1310752 | tf_op jit(solution)/shard_map/all_to_all | solution.py:552
  210.7 3.0 %collective-permute-done.5.other_ref = f32[64,40,128]{2,1,0:T(8,128)S(1)} collective-permute-done((f32[64,40,128]{2,1,0:T(8,128)S(1)}, f32[64,40,128]{2,1,0:T(8,128)S(1)}, u32[]{:S(2)}, u32[]{:S(2)}) %collective-permute-start.5) | collective-permute-done | bytes 1310752 | tf_op jit(solution)/shard_map/ppermute | solution.py:582
  213.7 1.1 copy-done.5
  214.8 4.0 %place_new.1 = (f32[400,1024]{1,0:T(8,128)}, f32[1,1024]{1,0:T(1,128)}, f32[400,512]{1,0:T(8,128)}, f32[1,512]{1,0:T(1,128)}) custom-call(s32[1]{0:T(128)} %bitcast.core_ref, f32[64,40,128]{2,1,0:T(8,128)} %copy-done.3, f32[64,40,128]{2,1,0:T(8,128)} %copy-done.5), custom_call_target="tpu_custom_call" | custom-call | tf_op jit(solution)/shard_map/place_new/pallas_call | solution.py:583
  (24 shorter events, 2.2 us)
Async XLA Ops:
  7.2 78.9 %all-gather.2.cloned.1.call-start = ((), (), s32[]{:S(2)}) async-start(), calls=%async_computation.5 | async-start | bytes 4325376 | tf_op jit(solution)/shard_map/all_gather | solution.py:433
  10.8 15.9 %collective-permute-start = (f32[16,512]{1,0:T(8,128)}, f32[16,512]{1,0:T(8,128)S(1)}, u32[]{:S(2)}, u32[]{:S(2)}) collective-permute-start(f32[16,512]{1,0:T(8,128)} %pick_negatives.1), channel_id=1, source_target_pairs={{0,32},{32,64},{64,96},{96,0},{1,33},{33,65},{65,97},{97,1},{2,34}... | collective-permute-start | bytes 98312 | tf_op jit(solution)/shard_map/ppermute | solution.py:375
  12.8 13.9 %collective-permute-start.1 = (f32[16,512]{1,0:T(8,128)}, f32[16,512]{1,0:T(8,128)S(1)}, u32[]{:S(2)}, u32[]{:S(2)}) collective-permute-start(f32[16,512]{1,0:T(8,128)} %pick_negatives.1), channel_id=1, source_target_pairs={{0,64},{32,96},{64,0},{96,32},{1,65},{33,97},{65,1},{97,33},{2,66}... | collective-permute-start | bytes 98312 | tf_op jit(solution)/shard_map/ppermute | solution.py:375
  16.4 10.4 %collective-permute-start.2 = (f32[16,512]{1,0:T(8,128)}, f32[16,512]{1,0:T(8,128)S(1)}, u32[]{:S(2)}, u32[]{:S(2)}) collective-permute-start(f32[16,512]{1,0:T(8,128)} %pick_negatives.1), channel_id=1, source_target_pairs={{0,96},{32,0},{64,32},{96,64},{1,97},{33,1},{65,33},{97,65},{2,98}... | collective-permute-start | bytes 98312 | tf_op jit(solution)/shard_map/ppermute | solution.py:375
  17.4 9.4 %copy-start.6 = (f32[16,512]{1,0:T(8,128)S(1)}, f32[16,512]{1,0:T(8,128)}, u32[]{:S(2)}) copy-start(f32[16,512]{1,0:T(8,128)} %pick_negatives.1) | copy-start | bytes 98308
  27.4 40.5 %all-to-all-start = ((f32[128,8,512]{2,1,0:T(8,128)}), f32[128,8,512]{2,1,0:T(8,128)S(1)}, u32[]{:S(2)}, u32[]{:S(2)}) async-start(f32[128,8,512]{2,1,0:T(8,128)} %bitcast.38), calls=%async_computation | async-start | bytes 4194304 | tf_op jit(solution)/shard_map/all_to_all | solution.py:429
  68.0 1.3 copy-start
  78.4 35.0 %all-to-all-start.1 = ((f32[128,8,512]{2,1,0:T(8,128)}), f32[128,8,512]{2,1,0:T(8,128)S(1)}, u32[]{:S(2)}, u32[]{:S(2)}) async-start(f32[128,8,512]{2,1,0:T(8,128)} %bitcast.32), calls=%async_computation.1 | async-start | bytes 4194304 | tf_op jit(solution)/shard_map/all_to_all | solution.py:429
  113.4 7.8 %copy-start.2 = (f32[128,8,512]{2,1,0:T(8,128)}, f32[128,8,512]{2,1,0:T(8,128)S(1)}, u32[]{:S(2)}) copy-start(f32[128,8,512]{2,1,0:T(8,128)S(1)} %all-to-all-done.1) | copy-start | bytes 6291460
  113.4 4.4 %collective-permute-start.3 = (f32[4,16,16,512]{3,2,1,0:T(8,128)}, f32[4,16,16,512]{3,2,1,0:T(8,128)S(1)}, u32[]{:S(2)}, u32[]{:S(2)}) collective-permute-start(f32[4,16,16,512]{3,2,1,0:T(8,128)} %get-tuple-element.59), channel_id=1, source_target_pairs={{0,1},{1,0},{2,3},{3,2},{4,5},{5,4},{6,7},{7,6},{8,9},{9,8},{10,11... | collective-permute-start | bytes 6291464 | tf_op jit(solution)/shard_map/ppermute | solution.py:499
  121.2 34.9 %all-to-all-start.2 = ((f32[64,16,512]{2,1,0:T(8,128)}), f32[64,16,512]{2,1,0:T(8,128)S(1)}, u32[]{:S(2)}, u32[]{:S(2)}) async-start(f32[64,16,512]{2,1,0:T(8,128)} %bitcast.17), calls=%async_computation.2 | async-start | bytes 4194304 | tf_op jit(solution)/shard_map/all_to_all | solution.py:501
  134.1 3.2 %collective-permute-start.4 = (f32[64,40,128]{2,1,0:T(8,128)}, f32[64,40,128]{2,1,0:T(8,128)S(1)}, u32[]{:S(2)}, u32[]{:S(2)}) collective-permute-start(f32[64,40,128]{2,1,0:T(8,128)} %get-tuple-element.68), channel_id=1, source_target_pairs={{0,1},{1,0},{2,3},{3,2},{4,5},{5,4},{6,7},{7,6},{8,9},{9,8},{10,11... | collective-permute-start | bytes 3932168 | tf_op jit(solution)/shard_map/ppermute | solution.py:514
  156.1 19.3 %copy-start.1 = (f32[64,16,512]{2,1,0:T(8,128)}, f32[64,16,512]{2,1,0:T(8,128)S(1)}, u32[]{:S(2)}) copy-start(f32[64,16,512]{2,1,0:T(8,128)S(1)} %all-to-all-done.2.neg_ref) | copy-start | bytes 6291460
  156.1 26.7 %all-to-all-start.3 = ((f32[64,40,128]{2,1,0:T(8,128)}), f32[64,40,128]{2,1,0:T(8,128)S(1)}, u32[]{:S(2)}, u32[]{:S(2)}) async-start(f32[64,40,128]{2,1,0:T(8,128)} %add.19), calls=%async_computation.3 | async-start | bytes 2621440 | tf_op jit(solution)/shard_map/all_to_all | solution.py:518
  182.8 1.1 copy-start.4
  183.8 7.8 %copy-start.7 = (s32[16]{0:T(128)S(1)}, s32[16]{0:T(128)}, u32[]{:S(2)}) copy-start(s32[16]{0:T(128)} %rows_ref.1) | copy-start | bytes 196
  186.5 24.1 %all-to-all-start.4 = ((f32[64,40,128]{2,1,0:T(8,128)}), f32[64,40,128]{2,1,0:T(8,128)S(1)}, u32[]{:S(2)}, u32[]{:S(2)}) async-start(f32[64,40,128]{2,1,0:T(8,128)} %update_own.1), calls=%async_computation.4 | async-start | bytes 2621440 | tf_op jit(solution)/shard_map/all_to_all | solution.py:552
  210.7 3.0 %copy-start.3 = (f32[64,40,128]{2,1,0:T(8,128)}, f32[64,40,128]{2,1,0:T(8,128)S(1)}, u32[]{:S(2)}) copy-start(f32[64,40,128]{2,1,0:T(8,128)S(1)} %all-to-all-done.4.mine_ref) | copy-start | bytes 3932164
  210.7 3.0 %collective-permute-start.5 = (f32[64,40,128]{2,1,0:T(8,128)S(1)}, f32[64,40,128]{2,1,0:T(8,128)S(1)}, u32[]{:S(2)}, u32[]{:S(2)}) collective-permute-start(f32[64,40,128]{2,1,0:T(8,128)S(1)} %all-to-all-done.4.mine_ref), channel_id=1, source_target_pairs={{0,1},{1,0},{2,3},{3,2},{4,5},{5,4},{6,7},{7,6},{8,9},{9,8},{10,11... | collective-permute-start | bytes 3932168 | tf_op jit(solution)/shard_map/ppermute | solution.py:582
  213.7 1.1 copy-start.5
Sparse Core Ops, SparseCore 0:
  27.6 58.4 all-gather.1

commit v6 on v5

--- a/solution.py
+++ b/solution.py
@@ -171,29 +171,31 @@
     return jnp.where(x < 1e-3, series, jnp.log(1.0 + x))
 
 
-def score(at_ref, query_ref, neg_ref, near_ref, far_ref, grad_ref, loss_ref, qh_ref, ql_ref):
-    side = pl.program_id(0)
-
-    @pl.when((side == 0) & (pl.program_id(1) == 0))
+def score(at_ref, query_ref, other_ref, neg_ref, back_ref, grad_ref, gradother_ref,
+          qh_ref, ql_ref, sum_ref, loss_ref):
+    step, last = pl.program_id(0), pl.num_programs(0) - 1
+
+    @pl.when(step == 0)
     def _():
-        high, low = split(query_ref[...])
-        qh_ref[...] = high
-        ql_ref[...] = low
-        grad_ref[...] = jnp.zeros_like(grad_ref)
+        for first, ref in ((0, query_ref), (TRIP, other_ref)):
+            high, low = split(ref[...])
+            qh_ref[first : first + TRIP, :] = high
+            ql_ref[first : first + TRIP, :] = low
+        sum_ref[...] = jnp.zeros_like(sum_ref)
         loss_ref[...] = jnp.zeros_like(loss_ref)
 
     qh, ql = qh_ref[...], ql_ref[...]
-    grad, total = grad_ref[...], loss_ref[...]
+    grad, total = sum_ref[...], loss_ref[...]
     negs = neg_ref[...].reshape(-1, WIDE)
-    step = 256
+    chunk = 256
     backs = []
     q_cols, q_rows = jnp.concatenate([qh, qh, ql], axis=1), jnp.concatenate([qh, ql, qh], axis=0)
-    for first in range(0, negs.shape[0], step):
-        nh, nl = split(negs[first : first + step, :])
+    for first in range(0, negs.shape[0], chunk):
+        nh, nl = split(negs[first : first + chunk, :])
         s = dot(q_cols, jnp.concatenate([nh, nl, nh], axis=1), ((1,), (1,)))
         small = jnp.exp(-jnp.abs(s))
         loss = jnp.maximum(s, 0.0) + log_one_plus(small)
-        for part in range(step // 128):
+        for part in range(chunk // 128):
             total = total + loss[:, part * 128 : (part + 1) * 128]
         whole = 1.0 + small
         turn = pl.reciprocal(whole, approx=True)
@@ -205,27 +207,24 @@
         )
         back = dot(jnp.concatenate([gh, gh, gl], axis=0), q_rows, ((0,), (0,)))
         backs.append(back * (1.0 / ENT_NEGS))
-    grad_ref[...] = grad
+    sum_ref[...] = grad
     loss_ref[...] = total
     back = jnp.concatenate(backs, axis=0).reshape(-1, 4, NEG, WIDE)
-
-    def put(ref):
-        for k in range(4):
-            ref[(at_ref[1] + 4 - k) & 3] = back[:, k]
-
-    @pl.when(side == 0)
+    for k in range(4):
+        back_ref[(at_ref[0] + 4 - k) & 3] = back[:, k]
+
+    @pl.when(step == last)
     def _():
-        put(near_ref)
-
-    @pl.when(side == 1)
-    def _():
-        put(far_ref)
+        for first, ref in ((0, grad_ref), (TRIP, gradother_ref)):
+            loss = jnp.sum(loss_ref[first : first + TRIP, :], axis=1, keepdims=True)
+            grad = sum_ref[first : first + TRIP, :]
+            ref[...] = jnp.where(iota(grad.shape, 1) == AUX, loss, grad) * (1.0 / ENT_NEGS)
 
 
 ENT_NEGS = 2 * CHIP_COUNT * NEG
 
 
-def close_triples(core_ref, back_ref, place_ref, headv_ref, relv_ref, gradq_ref, loss_ref,
+def close_triples(core_ref, back_ref, place_ref, headv_ref, relv_ref, gradq_ref, gradmore_ref,
                   head_ref, rel_ref, gradh_ref, mine_ref, other_ref, out_ref):
     place = place_ref[...]
     lane = iota((TRIP, 128), 1)
@@ -235,11 +234,12 @@
     high, low = split(back_ref[...])
     tail = dot(marks, high) + dot(marks, low)
     positive = aux_column(tail)
-    neg_loss = jnp.sum(loss_ref[...], axis=1, keepdims=True) * (1.0 / ENT_NEGS)
+    from_negs = gradq_ref[...] + gradmore_ref[...]
+    neg_loss = aux_column(from_negs)
     drop = -positive
     loss = jnp.maximum(drop, 0.0) + jnp.log1p(jnp.exp(-jnp.abs(drop))) + neg_loss
     out_ref[...] = jnp.broadcast_to(loss, (TRIP, 128)).T[:1]
-    grad = without_aux(tail) + gradq_ref[...] * (1.0 / ENT_NEGS)
+    grad = without_aux(tail + from_negs)
     g_re, g_im = grad[:, :SIDE], grad[:, SIDE:]
     heads, rels = headv_ref[...], relv_ref[...]
     h_re, h_im, r_re, r_im = heads[:, :SIDE], heads[:, SIDE:], rels[:, :SIDE], rels[:, SIDE:]
@@ -313,34 +313,32 @@
         out_ref[:, k * 8 : (k + 1) * 8, :] = jnp.broadcast_to(new[k][None], (CHIP_COUNT, 8, 128))
 
 
-def place_new(core_ref, mine_ref, other_ref, hub_ref, hubacc_ref, rel_ref, relacc_ref, held_ref):
-    core = core_ref[0]
-    for part_ref, side in ((mine_ref, core), (other_ref, 1 - core)):
-        def turned(k):
-            return part_ref[:, k * 8 : (k + 1) * 8, :].reshape(CHIP_COUNT * 8, 128).T
-
-        at = pl.ds(pl.multiple_of(side * (HUB // 2), 128), HUB // 2)
-        hub_ref[0:128, at] = turned(0)
-        hub_ref[HALF : HALF + 128, at] = turned(1)
-        mixed = turned(3)
-        hub_ref[128:HALF, at] = mixed[:72]
-        hub_ref[HALF + 128 : HALF + 184, at] = mixed[72:]
-        last = turned(4)
-        hub_ref[HALF + 184 : WIDTH, at] = last[:16]
-        hubacc_ref[:, at] = last[89:90]
-        for chip in range(CHIP_COUNT):
-            here = slice(chip * REL_OWN, (chip + 1) * REL_OWN)
-            held_ref[0, here, :] = part_ref[chip, 16:20, :]
-            held_ref[1, here, :] = part_ref[chip, 32:36, :]
-            held_ref[2, here, :] = part_ref[chip, 20:24, :]
-            held_ref[3, here, :] = part_ref[chip, 36:40, :]
-        at = pl.ds(pl.multiple_of(side * (REL // 2), 128), REL // 2)
-        for half in range(2):
-            rel_ref[half * HALF : half * HALF + 128, at] = held_ref[2 * half].T
-            last = held_ref[2 * half + 1].T
-            rel_ref[half * HALF + 128 : (half + 1) * HALF, at] = last[16:88]
-            if half == 0:
-                relacc_ref[:, at] = last[88:89]
+def place_new(side_ref, part_ref, *refs):
+    hub_ref, hubacc_ref, rel_ref, relacc_ref, held_ref = refs[-5:]
+
+    def turned(k):
+        return part_ref[:, k * 8 : (k + 1) * 8, :].reshape(CHIP_COUNT * 8, 128).T
+
+    hub_ref[0:128, :] = turned(0)
+    hub_ref[HALF : HALF + 128, :] = turned(1)
+    mixed = turned(3)
+    hub_ref[128:HALF, :] = mixed[:72]
+    hub_ref[HALF + 128 : HALF + 184, :] = mixed[72:]
+    last = turned(4)
+    hub_ref[HALF + 184 : WIDTH, :] = last[:16]
+    hubacc_ref[...] = last[89:90]
+    for chip in range(CHIP_COUNT):
+        here = slice(chip * REL_OWN, (chip + 1) * REL_OWN)
+        held_ref[0, here, :] = part_ref[chip, 16:20, :]
+        held_ref[1, here, :] = part_ref[chip, 32:36, :]
+        held_ref[2, here, :] = part_ref[chip, 20:24, :]
+        held_ref[3, here, :] = part_ref[chip, 36:40, :]
+    for half in range(2):
+        rel_ref[half * HALF : half * HALF + 128, :] = held_ref[2 * half].T
+        last = held_ref[2 * half + 1].T
+        rel_ref[half * HALF + 128 : (half + 1) * HALF, :] = last[16:88]
+        if half == 0:
+            relacc_ref[...] = last[88:89]
 
 
 def update_entities(rows_ref, neg_ref, ent_ref, acc_ref, grad_ref, new_ref, newacc_ref,
@@ -430,7 +428,8 @@
         return got.reshape(SLOTS, WIDE)
 
     sent, near, own_arg = lax.optimization_barrier((sent, near, own_arg))
-    near = lax.all_gather(near, ("x", "y", "core"), axis=0, tiled=True)
+    near = lax.all_gather(near, ("x", "y"), axis=0, tiled=True)
+    query_other = lax.ppermute(query, "core", SWAP)
     asked = exchange(sent)
     ent_high, ent_low, mine_rows = pl.pallas_call(
         turn_tables,
@@ -458,45 +457,36 @@
     near, _ = lax.optimization_barrier((near, answer))
     back = exchange(answer)
 
-    group, steps, places = 8, 2, 16
-    near_back, far_back, grad_q, loss_sum = pl.pallas_call(
+    group, places = 8, 16
+    whole = pl.BlockSpec((TRIP, WIDE), lambda i, at: (0, 0))
+    part, grad_q, grad_other = pl.pallas_call(
         score,
-        out_shape=[
-            shape(4, places, NEG, WIDE), shape(4, places, NEG, WIDE), shape(TRIP, WIDE),
-            shape(TRIP, 128),
-        ],
+        out_shape=[shape(4, places, NEG, WIDE), shape(TRIP, WIDE), shape(TRIP, WIDE)],
         grid_spec=pltpu.PrefetchScalarGridSpec(
             num_scalar_prefetch=1,
-            grid=(2, steps),
+            grid=(places // group,),
             in_specs=[
-                pl.BlockSpec((TRIP, WIDE), lambda i, c, at: (0, 0)),
-                pl.BlockSpec(
-                    (group, 1, 4 * NEG, WIDE), lambda i, c, at: (c, (i + at[0]) % 2, 0, 0)
-                ),
+                whole, whole, pl.BlockSpec((group, 4 * NEG, WIDE), lambda i, at: (i, 0, 0))
             ],
             out_specs=[
-                pl.BlockSpec(
-                    (4, group, NEG, WIDE),
-                    lambda i, c, at: (0, jnp.where(i == 0, c, steps - 1), 0, 0),
-                ),
-                pl.BlockSpec(
-                    (4, group, NEG, WIDE), lambda i, c, at: (0, jnp.where(i == 0, 0, c), 0, 0)
-                ),
-                pl.BlockSpec((TRIP, WIDE), lambda i, c, at: (0, 0)),
-                pl.BlockSpec((TRIP, 128), lambda i, c, at: (0, 0)),
+                pl.BlockSpec((4, group, NEG, WIDE), lambda i, at: (0, i, 0, 0)), whole, whole
             ],
-            scratch_shapes=[pltpu.VMEM((TRIP, WIDE), BF16), pltpu.VMEM((TRIP, WIDE), BF16)],
+            scratch_shapes=[
+                pltpu.VMEM((2 * TRIP, WIDE), BF16), pltpu.VMEM((2 * TRIP, WIDE), BF16),
+                pltpu.VMEM((2 * TRIP, WIDE), F32), pltpu.VMEM((2 * TRIP, 128), F32),
+            ],
         ),
         compiler_params=params(),
         cost_estimate=cost(20e9, 12e6),
         name="score",
     )(
-        jnp.stack([core, lax.axis_index("z").astype(I32)]),
+        lax.axis_index("z").astype(I32).reshape(1),
         query,
-        near.reshape(places, 2, 4 * NEG, WIDE),
+        query_other,
+        near.reshape(places, 4 * NEG, WIDE),
     )
-    far_back, back = lax.optimization_barrier((far_back, back))
-    part = near_back + lax.ppermute(far_back, "core", SWAP)
+    grad_other, back = lax.optimization_barrier((grad_other, back))
+    grad_more = lax.ppermute(grad_other, "core", SWAP)
     part, back = lax.optimization_barrier((part.reshape(CHIP_COUNT, NEG, WIDE), back))
     neg_sums = lax.all_to_all(part, CHIPS, split_axis=0, concat_axis=0, tiled=True)
 
@@ -510,7 +500,7 @@
         out_specs=[VMEM] * 4,
         compiler_params=params(),
         name="close_triples",
-    )(core_arg, back, place, heads, rels, grad_q, loss_sum, head_row, rel_row)
+    )(core_arg, back, place, heads, rels, grad_q, grad_more, head_row, rel_row)
     both_swapped = lax.ppermute(both_other, "core", SWAP)
 
     paired = both_mine + both_swapped
@@ -580,15 +570,30 @@
 
     new_mine, entity_new = lax.optimization_barrier((new_mine, entity_new))
     new_other = lax.ppermute(new_mine, "core", SWAP)
-    hub_new, hub_accum_new, rel_new, rel_accum_new = pl.pallas_call(
-        place_new,
-        out_shape=[shape(WIDTH, HUB), shape(1, HUB), shape(WIDTH, REL), shape(1, REL)],
-        in_specs=[SMEM, VMEM, VMEM],
-        out_specs=[VMEM] * 4,
-        scratch_shapes=[pltpu.VMEM((4, REL // 2, 128), F32)],
-        compiler_params=params(),
-        name="place_new",
-    )(core_arg, new_mine, new_other)
+
+    def placed(side, part, *before):
+        sizes = ((WIDTH, HUB), (1, HUB), (WIDTH, REL), (1, REL))
+        return pl.pallas_call(
+            place_new,
+            out_shape=[shape(*size) for size in sizes],
+            grid_spec=pltpu.PrefetchScalarGridSpec(
+                num_scalar_prefetch=1,
+                grid=(1,),
+                in_specs=[pl.BlockSpec((CHIP_COUNT, OWN, 128), lambda i, side: (0, 0, 0))]
+                + [pl.BlockSpec(memory_space=pl.ANY)] * len(before),
+                out_specs=[
+                    pl.BlockSpec((rows, count // 2), lambda i, side: (0, side[0]))
+                    for rows, count in sizes
+                ],
+                scratch_shapes=[pltpu.VMEM((4, REL // 2, 128), F32)],
+            ),
+            input_output_aliases={k + 2: k for k in range(len(before))},
+            compiler_params=params(),
+            name="place_new",
+        )(side, part, *before)
+
+    halves = placed(core_arg, new_mine)
+    hub_new, hub_accum_new, rel_new, rel_accum_new = placed(1 - core_arg, new_other, *halves)
     return (
         entity_new.T,
         entity_accum_new.reshape(ENT),

time: 227 us -> 218 us (0.960)
  waiting for transfers between devices: 78.2 us -> 69 us
  other arithmetic: 7.16 us -> 3.16 us
  local copies, waits for them, and re-layouts: 4.16 us -> 7.53 us
    ppermute x1 -> x2, waiting for transfers between devices: 4.37 us -> 0.01 us  [the longest x1 0.01 us: body(): query_other = lax.ppermute(query, 'core', SWAP)]
    add x1 -> x0, other arithmetic: 3.39 us -> none  [body(): part = near_back + lax.ppermute(far_back, 'core', SWAP)]
    unnamed x16 -> x18, local copies, waits for them, and re-layouts: 3.49 us -> 6.86 us
    ppermute x1, waiting for transfers between devices: 3.03 us -> 0.01 us  [body(): new_other = lax.ppermute(new_mine, 'core', SWAP)]
    pallas_call x2 -> x3, Pallas kernels: 25.8 us -> 26.2 us  [the longest x1 20.9 us: body(): pl.pallas_call(score, out_shape=[shape(4, places, NEG, WIDE), shape(TRIP,...]
  transfers between devices with their start and end apart: 12 -> 13, of which waited for: 9 -> 7; matrix products, arithmetic and copies ran while one was open for 2% -> 1% of each run, Pallas kernels for 34% -> 36%
where the time goes in v6:
time: 218 us; the launch traced here: 217 us
  Pallas kernels  86.6 us (40%)
  waiting for transfers between devices  69 us (32%)
  starting transfers between devices  36.4 us (17%)
  between operations  14.2 us (7%)
  local copies, waits for them, and re-layouts  7.53 us (3%)
  other arithmetic  3.16 us (1%)
    all_to_all x2, waiting for transfers between devices, exchange(): got = lax.all_to_all(parts, SHARD, split_axis=0, concat_axis=0, tiled=True)  32.8 us
    pallas_call x1, Pallas kernels, body(): pl.pallas_call(score, out_shape=[shape(4, places, NEG, WIDE), shape(TRIP,...  20.9 us
    all_to_all x1, waiting for transfers between devices, body(): lax.all_to_all(part, CHIPS, split_axis=0, concat_axis=0, tiled=True)  14.4 us
    pallas_call x1, Pallas kernels, body(): pl.pallas_call(scatter_entities, out_shape=shape(WIDTH, ENT), grid=(ENT /...  12.9 us
    all_to_all x2, starting transfers between devices, exchange(): got = lax.all_to_all(parts, SHARD, split_axis=0, concat_axis=0, tiled=True)  12.9 us
    all_to_all x1, waiting for transfers between devices, body(): lax.all_to_all(own_new, CHIPS, split_axis=0, concat_axis=0, tiled=True)  10.2 us
    pallas_call x1, Pallas kernels, body(): pl.pallas_call(prepare, out_shape=[shape(TRIP, WIDE), shape(TRIP, WIDE),...  9.35 us
    pallas_call x1, Pallas kernels, body(): pl.pallas_call(answer_queries, out_shape=shape(SLOTS, WIDE), grid=(SLOTS...  9.03 us
  transfers between devices with their start and end apart: 13, of which 7 were waited for; matrix products, arithmetic and copies ran while one was open for 1% of the time, Pallas kernels for 36%

profile of v6, /device:TPU:0, one launch (start us, length us, event | category | flops | bytes accessed | tf_op | source)
XLA Modules:
  0.0 216.7 jit_solution(13046980794682761793)
XLA Ops:
  7.2 3.6 %pick_negatives.1 = f32[16,512]{1,0:T(8,128)} custom-call(s32[16]{0:T(128)} %rows_ref.1, f32[400,2048]{1,0:T(8,128)} %bitcast.26), custom_call_target="tpu_custom_call" | custom-call | tf_op jit(solution)/shard_map/pick_negatives/pallas_call | solution.py:401
  10.8 2.0 collective-permute-start.1
  12.8 3.6 %collective-permute-start.2 = (f32[16,512]{1,0:T(8,128)}, f32[16,512]{1,0:T(8,128)S(1)}, u32[]{:S(2)}, u32[]{:S(2)}) collective-permute-start(f32[16,512]{1,0:T(8,128)} %pick_negatives.1), channel_id=1, source_target_pairs={{0,64},{32,96},{64,0},{96,32},{1,65},{33,97},{65,1},{97,33},{2,66}... | collective-permute-start | bytes 98312 | tf_op jit(solution)/shard_map/ppermute | solution.py:373
  16.4 1.0 collective-permute-start.3
  17.4 9.4 %prepare.1 = (f32[512,512]{1,0:T(8,128)}, f32[512,512]{1,0:T(8,128)}, f32[512,512]{1,0:T(8,128)}, f32[1024,512]{1,0:T(8,128)}, s32[512,128]{1,0:T(8,128)}) custom-call(s32[1,512]{1,0:T(1,128)} %bitcast.42, s32[1,512]{1,0:T(1,128)} %bitcast.45, s32[1,512]{1,0:T(1,128)} %bitcast.50, s32[1,512]{1,0:T(1,128)} %bitcast.51, f32[400,2048]{1,0:T(8,128)} %bitcast.27, ...), custom_call_target="tpu_custom_call" | custom-call | tf_op jit(solution)/shard_map/prepare/pallas_call | solution.py:413
  27.4 8.0 %all-to-all-start = ((f32[128,8,512]{2,1,0:T(8,128)}), f32[128,8,512]{2,1,0:T(8,128)S(1)}, u32[]{:S(2)}, u32[]{:S(2)}) async-start(f32[128,8,512]{2,1,0:T(8,128)} %bitcast.39), calls=%async_computation | async-start | bytes 4194304 | tf_op jit(solution)/shard_map/all_to_all | solution.py:427
  35.6 7.3 %turn_tables.1 = (bf16[2048,512]{1,0:T(8,128)(2,1)}, bf16[2048,512]{1,0:T(8,128)(2,1)}, f32[40,128]{1,0:T(8,128)}) custom-call(s32[1]{0:T(128)} %bitcast.9.own_ref, f32[400,2048]{1,0:T(8,128)} %bitcast.28, f32[400,1024]{1,0:T(8,128)} %bitcast.35, f32[400,512]{1,0:T(8,128)} %bitcast.37, f32[1,1024]{1,0:T(1,128)} %bitcast.48, f32[1,512]{1,0:T(1,128)} %bitcast.52), custom_call_target="tpu_custom_call" | custom-call | flops 1000000 | bytes 100000 | tf_op jit(solution)/shard_map/turn_tables/pallas_call | solution.py:434
  42.9 25.1 %all-to-all-done = f32[128,8,512]{2,1,0:T(8,128)S(1)} async-done(((f32[128,8,512]{2,1,0:T(8,128)}), f32[128,8,512]{2,1,0:T(8,128)S(1)}, u32[]{:S(2)}, u32[]{:S(2)}) %all-to-all-start) | async-done | bytes 2097184 | tf_op jit(solution)/shard_map/all_to_all | solution.py:427
  68.0 1.3 copy-done
  69.3 9.0 %answer_queries.1.answer_ref = f32[1024,512]{1,0:T(8,128)} custom-call(f32[1024,512]{1,0:T(8,128)} %bitcast.30, bf16[2048,512]{1,0:T(8,128)(2,1)} %get-tuple-element.57.high_ref, bf16[2048,512]{1,0:T(8,128)(2,1)} %get-tuple-element.58.low_ref), custom_call_target="tpu_custom_call" | custom-call | tf_op jit(solution)/shard_map/answer_queries/pallas_call | solution.py:448
  78.3 4.8 %all-to-all-start.1 = ((f32[128,8,512]{2,1,0:T(8,128)}), f32[128,8,512]{2,1,0:T(8,128)S(1)}, u32[]{:S(2)}, u32[]{:S(2)}) async-start(f32[128,8,512]{2,1,0:T(8,128)} %bitcast.32), calls=%async_computation.1 | async-start | bytes 4194304 | tf_op jit(solution)/shard_map/all_to_all | solution.py:427
  83.2 1.6 all-gather.2.cloned.1.call-done
  84.7 20.9 %score.1 = (f32[4,16,16,512]{3,2,1,0:T(8,128)}, f32[512,512]{1,0:T(8,128)}, f32[512,512]{1,0:T(8,128)}) custom-call(s32[1]{0:T(128)} %bitcast.1.at_ref, f32[512,512]{1,0:T(8,128)} %get-tuple-element.51.query_ref, f32[512,512]{1,0:T(8,128)} %collective-permute-done.other_ref, f32[16,64,512]{2,1,0:T(8,128)} %bitcast.55), custom_call_target="tpu_custom_call" | custom-call | flops 20000000000 | bytes 12000000 | tf_op jit(solution)/shard_map/score/pallas_call | solution.py:462
  105.6 7.7 %all-to-all-done.1 = f32[128,8,512]{2,1,0:T(8,128)S(1)} async-done(((f32[128,8,512]{2,1,0:T(8,128)}), f32[128,8,512]{2,1,0:T(8,128)S(1)}, u32[]{:S(2)}, u32[]{:S(2)}) %all-to-all-start.1) | async-done | bytes 2097184 | tf_op jit(solution)/shard_map/all_to_all | solution.py:427
  113.3 1.3 copy-done.1
  114.7 5.6 %all-to-all-start.2 = ((f32[64,16,512]{2,1,0:T(8,128)}), f32[64,16,512]{2,1,0:T(8,128)}, u32[]{:S(2)}, u32[]{:S(2)}) async-start(f32[64,16,512]{2,1,0:T(8,128)} %bitcast.38), calls=%async_computation.2 | async-start | bytes 4194304 | tf_op jit(solution)/shard_map/all_to_all | solution.py:491
  121.2 8.3 %close_triples.1 = (f32[512,512]{1,0:T(8,128)}, f32[64,40,128]{2,1,0:T(8,128)}, f32[64,40,128]{2,1,0:T(8,128)}, f32[1,512]{1,0:T(1,128)}) custom-call(s32[1]{0:T(128)} %bitcast.core_ref.side_ref, f32[1024,512]{1,0:T(8,128)} %bitcast.33, s32[512,128]{1,0:T(8,128)} %get-tuple-element.64.place_ref, f32[512,512]{1,0:T(8,128)} %get-tuple-element.65.headv_ref, ...), custom_call_target="tpu_custom_call" | custom-call | tf_op jit(solution)/shard_map/close_triples/pallas_call | solution.py:493
  129.6 3.2 %collective-permute-done.5 = f32[64,40,128]{2,1,0:T(8,128)S(1)} collective-permute-done((f32[64,40,128]{2,1,0:T(8,128)}, f32[64,40,128]{2,1,0:T(8,128)S(1)}, u32[]{:S(2)}, u32[]{:S(2)}) %collective-permute-start.5) | collective-permute-done | bytes 1310752 | tf_op jit(solution)/shard_map/ppermute | solution.py:504
  132.8 2.5 %add.15 = f32[64,40,128]{2,1,0:T(8,128)} add(f32[64,40,128]{2,1,0:T(8,128)} %get-tuple-element.69, f32[64,40,128]{2,1,0:T(8,128)S(1)} %collective-permute-done.5) | non-fusion elementwise | flops 327680 | bytes 3932160 | tf_op jit(solution)/shard_map/add | solution.py:506
  135.3 14.4 %all-to-all-done.2.neg_ref = f32[64,16,512]{2,1,0:T(8,128)} async-done(((f32[64,16,512]{2,1,0:T(8,128)}), f32[64,16,512]{2,1,0:T(8,128)}, u32[]{:S(2)}, u32[]{:S(2)}) %all-to-all-start.2) | async-done | bytes 2097184 | tf_op jit(solution)/shard_map/all_to_all | solution.py:491
  149.8 6.2 %all-to-all-start.3 = ((f32[64,40,128]{2,1,0:T(8,128)}), f32[64,40,128]{2,1,0:T(8,128)S(1)}, u32[]{:S(2)}, u32[]{:S(2)}) async-start(f32[64,40,128]{2,1,0:T(8,128)} %add.15), calls=%async_computation.3 | async-start | bytes 2621440 | tf_op jit(solution)/shard_map/all_to_all | solution.py:508
  156.0 12.9 %scatter_entities.1.grad_ref = f32[400,2048]{1,0:T(8,128)} custom-call(s32[1,512]{1,0:T(1,128)} %bitcast.44, f32[512,512]{1,0:T(8,128)} %get-tuple-element.73.gradh_ref, f32[1024,512]{1,0:T(8,128)} %bitcast.31, f32[1024,512]{1,0:T(8,128)} %answer_queries.1.answer_ref), custom_call_target="tpu_custom_call" | custom-call | flops 1000000 | bytes 100000 | tf_op jit(solution)/shard_map/scatter_entities/pallas_call | solution.py:512
  168.8 6.7 %all-to-all-done.3.sums_ref = f32[64,40,128]{2,1,0:T(8,128)S(1)} async-done(((f32[64,40,128]{2,1,0:T(8,128)}), f32[64,40,128]{2,1,0:T(8,128)S(1)}, u32[]{:S(2)}, u32[]{:S(2)}) %all-to-all-start.3) | async-done | bytes 1310752 | tf_op jit(solution)/shard_map/all_to_all | solution.py:508
  175.5 1.1 copy-done.3
  176.6 2.7 %update_own.1 = f32[64,40,128]{2,1,0:T(8,128)} custom-call(f32[64,40,128]{2,1,0:T(8,128)} %copy-done.3, f32[40,128]{1,0:T(8,128)} %get-tuple-element.77.mine_ref), custom_call_target="tpu_custom_call" | custom-call | tf_op jit(solution)/shard_map/update_own/pallas_call | solution.py:534
  179.3 5.0 %all-to-all-start.4 = ((f32[64,40,128]{2,1,0:T(8,128)}), f32[64,40,128]{2,1,0:T(8,128)S(1)}, u32[]{:S(2)}, u32[]{:S(2)}) async-start(f32[64,40,128]{2,1,0:T(8,128)} %update_own.1), calls=%async_computation.4 | async-start | bytes 2621440 | tf_op jit(solution)/shard_map/all_to_all | solution.py:542
  185.0 7.2 %update_entities.1 = (f32[400,2048]{1,0:T(8,128)}, f32[1,2048]{1,0:T(1,128)}) custom-call(s32[16,128]{1,0:T(8,128)} %broadcast_in_dim.2.rows_ref, f32[64,16,512]{2,1,0:T(8,128)} %all-to-all-done.2.neg_ref, f32[400,2048]{1,0:T(8,128)} %bitcast.29, f32[1,2048]{1,0:T(1,128)} %bitcast.47, f32[400,2048]{1,0:T(8,128)} %scatter_entities.1.grad_ref), custom_call_target="tpu_custom_call" | custom-call | flops 1000000 | bytes 100000 | tf_op jit(solution)/shard_map/update_entities/pallas_call | solution.py:544
  192.2 10.2 %all-to-all-done.4.part_ref = f32[64,40,128]{2,1,0:T(8,128)S(1)} async-done(((f32[64,40,128]{2,1,0:T(8,128)}), f32[64,40,128]{2,1,0:T(8,128)S(1)}, u32[]{:S(2)}, u32[]{:S(2)}) %all-to-all-start.4) | async-done | bytes 1310752 | tf_op jit(solution)/shard_map/all_to_all | solution.py:542
  202.4 1.1 copy-done.2
  203.5 2.7 %place_new.2 = (f32[400,1024]{1,0:T(8,128)}, f32[1,1024]{1,0:T(1,128)}, f32[400,512]{1,0:T(8,128)}, f32[1,512]{1,0:T(1,128)}) custom-call(s32[1]{0:T(128)} %bitcast.core_ref.side_ref, f32[64,40,128]{2,1,0:T(8,128)} %copy-done.2), custom_call_target="tpu_custom_call" | custom-call | tf_op jit(solution)/shard_map/place_new/pallas_call | solution.py:576
  206.2 1.1 copy-done.4
  207.2 2.7 %place_new.3 = (f32[400,1024]{1,0:T(8,128)}, f32[1,1024]{1,0:T(1,128)}, f32[400,512]{1,0:T(8,128)}, f32[1,512]{1,0:T(1,128)}) custom-call(s32[1]{0:T(128)S(6)} %sub.3.side_ref, f32[64,40,128]{2,1,0:T(8,128)} %copy-done.4, f32[400,1024]{1,0:T(8,128)} %get-tuple-element.84.refs_0_, ...), custom_call_target="tpu_custom_call", output_to_operand_aliasing={{0}: (2, {}), {1}: (3, {}), {2}: (4, {}), {3}: (5, {})} | custom-call | tf_op jit(solution)/shard_map/place_new/pallas_call | solution.py:576
  (27 shorter events, 2.5 us)
Async XLA Ops:
  7.2 77.5 %all-gather.2.cloned.1.call-start = ((), (), s32[]{:S(2)}) async-start(), calls=%async_computation.5 | async-start | bytes 2228224 | tf_op jit(solution)/shard_map/all_gather | solution.py:431
  10.8 16.0 %collective-permute-start.1 = (f32[16,512]{1,0:T(8,128)}, f32[16,512]{1,0:T(8,128)S(1)}, u32[]{:S(2)}, u32[]{:S(2)}) collective-permute-start(f32[16,512]{1,0:T(8,128)} %pick_negatives.1), channel_id=1, source_target_pairs={{0,32},{32,64},{64,96},{96,0},{1,33},{33,65},{65,97},{97,1},{2,34}... | collective-permute-start | bytes 98312 | tf_op jit(solution)/shard_map/ppermute | solution.py:373
  12.8 13.9 %collective-permute-start.2 = (f32[16,512]{1,0:T(8,128)}, f32[16,512]{1,0:T(8,128)S(1)}, u32[]{:S(2)}, u32[]{:S(2)}) collective-permute-start(f32[16,512]{1,0:T(8,128)} %pick_negatives.1), channel_id=1, source_target_pairs={{0,64},{32,96},{64,0},{96,32},{1,65},{33,97},{65,1},{97,33},{2,66}... | collective-permute-start | bytes 98312 | tf_op jit(solution)/shard_map/ppermute | solution.py:373
  16.4 10.4 %collective-permute-start.3 = (f32[16,512]{1,0:T(8,128)}, f32[16,512]{1,0:T(8,128)S(1)}, u32[]{:S(2)}, u32[]{:S(2)}) collective-permute-start(f32[16,512]{1,0:T(8,128)} %pick_negatives.1), channel_id=1, source_target_pairs={{0,96},{32,0},{64,32},{96,64},{1,97},{33,1},{65,33},{97,65},{2,98}... | collective-permute-start | bytes 98312 | tf_op jit(solution)/shard_map/ppermute | solution.py:373
  17.4 9.4 %copy-start.6 = (f32[16,512]{1,0:T(8,128)S(1)}, f32[16,512]{1,0:T(8,128)}, u32[]{:S(2)}) copy-start(f32[16,512]{1,0:T(8,128)} %pick_negatives.1) | copy-start | bytes 98308
  27.4 8.1 %copy-start.8 = (f32[512,512]{1,0:T(8,128)S(1)}, f32[512,512]{1,0:T(8,128)}, u32[]{:S(2)}) copy-start(f32[512,512]{1,0:T(8,128)} %get-tuple-element.51.query_ref) | copy-start | bytes 3145732
  27.4 40.5 %all-to-all-start = ((f32[128,8,512]{2,1,0:T(8,128)}), f32[128,8,512]{2,1,0:T(8,128)S(1)}, u32[]{:S(2)}, u32[]{:S(2)}) async-start(f32[128,8,512]{2,1,0:T(8,128)} %bitcast.39), calls=%async_computation | async-start | bytes 4194304 | tf_op jit(solution)/shard_map/all_to_all | solution.py:427
  35.5 49.2 %collective-permute-start = (f32[512,512]{1,0:T(8,128)S(1)}, f32[512,512]{1,0:T(8,128)}, u32[]{:S(2)}, u32[]{:S(2)}) collective-permute-start(f32[512,512]{1,0:T(8,128)S(1)} %copy-done.8), channel_id=1, source_target_pairs={{0,1},{1,0},{2,3},{3,2},{4,5},{5,4},{6,7},{7,6},{8,9},{9,8},{10,11... | collective-permute-start | bytes 3145736 | tf_op jit(solution)/shard_map/ppermute | solution.py:432
  68.0 1.3 copy-start
  78.3 35.0 %all-to-all-start.1 = ((f32[128,8,512]{2,1,0:T(8,128)}), f32[128,8,512]{2,1,0:T(8,128)S(1)}, u32[]{:S(2)}, u32[]{:S(2)}) async-start(f32[128,8,512]{2,1,0:T(8,128)} %bitcast.32), calls=%async_computation.1 | async-start | bytes 4194304 | tf_op jit(solution)/shard_map/all_to_all | solution.py:427
  113.3 1.4 copy-start.1
  113.3 6.9 %collective-permute-start.4 = (f32[512,512]{1,0:T(8,128)}, f32[512,512]{1,0:T(8,128)S(1)}, u32[]{:S(2)}, u32[]{:S(2)}) collective-permute-start(f32[512,512]{1,0:T(8,128)} %get-tuple-element.68), channel_id=1, source_target_pairs={{0,1},{1,0},{2,3},{3,2},{4,5},{5,4},{6,7},{7,6},{8,9},{9,8},{10,11... | collective-permute-start | bytes 3145736 | tf_op jit(solution)/shard_map/ppermute | solution.py:489
  114.7 35.1 %all-to-all-start.2 = ((f32[64,16,512]{2,1,0:T(8,128)}), f32[64,16,512]{2,1,0:T(8,128)}, u32[]{:S(2)}, u32[]{:S(2)}) async-start(f32[64,16,512]{2,1,0:T(8,128)} %bitcast.38), calls=%async_computation.2 | async-start | bytes 4194304 | tf_op jit(solution)/shard_map/all_to_all | solution.py:491
  120.3 1.0 copy-start.5
  129.6 3.2 %collective-permute-start.5 = (f32[64,40,128]{2,1,0:T(8,128)}, f32[64,40,128]{2,1,0:T(8,128)S(1)}, u32[]{:S(2)}, u32[]{:S(2)}) collective-permute-start(f32[64,40,128]{2,1,0:T(8,128)} %get-tuple-element.70), channel_id=1, source_target_pairs={{0,1},{1,0},{2,3},{3,2},{4,5},{5,4},{6,7},{7,6},{8,9},{9,8},{10,11... | collective-permute-start | bytes 3932168 | tf_op jit(solution)/shard_map/ppermute | solution.py:504
  149.8 25.8 %all-to-all-start.3 = ((f32[64,40,128]{2,1,0:T(8,128)}), f32[64,40,128]{2,1,0:T(8,128)S(1)}, u32[]{:S(2)}, u32[]{:S(2)}) async-start(f32[64,40,128]{2,1,0:T(8,128)} %add.15), calls=%async_computation.3 | async-start | bytes 2621440 | tf_op jit(solution)/shard_map/all_to_all | solution.py:508
  175.5 1.1 copy-start.3
  176.6 7.7 %copy-start.7 = (s32[16]{0:T(128)S(1)}, s32[16]{0:T(128)}, u32[]{:S(2)}) copy-start(s32[16]{0:T(128)} %rows_ref.1) | copy-start | bytes 196
  179.3 23.1 %all-to-all-start.4 = ((f32[64,40,128]{2,1,0:T(8,128)}), f32[64,40,128]{2,1,0:T(8,128)S(1)}, u32[]{:S(2)}, u32[]{:S(2)}) async-start(f32[64,40,128]{2,1,0:T(8,128)} %update_own.1), calls=%async_computation.4 | async-start | bytes 2621440 | tf_op jit(solution)/shard_map/all_to_all | solution.py:542
  202.4 1.1 copy-start.2
  202.4 3.7 %collective-permute-start.6 = (f32[64,40,128]{2,1,0:T(8,128)S(1)}, f32[64,40,128]{2,1,0:T(8,128)S(1)}, u32[]{:S(2)}, u32[]{:S(2)}) collective-permute-start(f32[64,40,128]{2,1,0:T(8,128)S(1)} %all-to-all-done.4.part_ref), channel_id=1, source_target_pairs={{0,1},{1,0},{2,3},{3,2},{4,5},{5,4},{6,7},{7,6},{8,9},{9,8},{10,11... | collective-permute-start | bytes 3932168 | tf_op jit(solution)/shard_map/ppermute | solution.py:572
  206.2 1.1 copy-start.4
Sparse Core Ops, SparseCore 0:
  27.6 57.1 all-gather.1

commit v7 on v6

--- a/solution.py
+++ b/solution.py
@@ -15,13 +15,14 @@
 WIDTH, HALF, SIDE, WIDE, AUX = 400, 200, 256, 512, 200
 ENT, HUB, REL, TRIP, CHIP_COUNT, CAP, NEG = 2048, 1024, 512, 512, 64, 8, 16
 SLOTS = 2 * CHIP_COUNT * CAP
+NEG_PACKED = 56
 HUB_OWN, REL_OWN, OWN = 8, 4, 40
 VMEM = pl.BlockSpec(memory_space=pltpu.VMEM)
 SMEM = pl.BlockSpec(memory_space=pltpu.SMEM)
 
 
-def params():
-    return pltpu.CompilerParams(vmem_limit_bytes=56 << 20)
+def params(mib=56):
+    return pltpu.CompilerParams(vmem_limit_bytes=mib << 20)
 
 
 def cost(flops, nbytes):
@@ -80,8 +81,7 @@
     out_ref[...] = held_ref[...].T[:NEG]
 
 
-def prepare(head_ref, rel_ref, owner_ref, tail_ref, ent_ref, hub_ref, relt_ref,
-            query_ref, headv_ref, relv_ref, sent_ref, place_ref):
+def embed(head_ref, rel_ref, ent_ref, hub_ref, relt_ref):
     head = head_ref[...]
 
     def gather(table, ids):
@@ -94,10 +94,19 @@
     h_re, h_im, r_re, r_im = heads[:HALF], heads[HALF:], rels[:HALF], rels[HALF:]
     q_re = h_re * r_re - h_im * r_im
     q_im = h_re * r_im + h_im * r_re
-    headv_ref[...] = widen(h_re, h_im).T
-    relv_ref[...] = widen(r_re, r_im).T
-    query_ref[...] = widen(q_re, q_im).T
-
+    return (h_re, h_im), (r_re, r_im), (q_re, q_im)
+
+
+def embed_rows(head_ref, rel_ref, ent_ref, hub_ref, relt_ref, query_ref, headv_ref, relv_ref):
+    heads, rels, queries = embed(head_ref, rel_ref, ent_ref, hub_ref, relt_ref)
+    headv_ref[...] = widen(*heads).T
+    relv_ref[...] = widen(*rels).T
+    query_ref[...] = widen(*queries).T
+
+
+def prepare(head_ref, rel_ref, owner_ref, tail_ref, ent_ref, hub_ref, relt_ref,
+            sent_ref, place_ref):
+    _, _, queries = embed(head_ref, rel_ref, ent_ref, hub_ref, relt_ref)
     owner = owner_ref[...]
     owned = hot(iota((2 * CHIP_COUNT, TRIP), 0) == owner)
     before = hot(iota((TRIP, TRIP), 0) < iota((TRIP, TRIP), 1))
@@ -106,7 +115,7 @@
     place_ref[...] = jnp.broadcast_to(place.astype(F32), (128, TRIP)).T.astype(I32)
 
     marks = hot(iota((SLOTS, TRIP), 0) == place)
-    high, low = split(widen(q_re, q_im, tail_ref[...].astype(F32) + 1.0).T)
+    high, low = split(widen(*queries, tail_ref[...].astype(F32) + 1.0).T)
     sent_ref[...] = dot(marks, high) + dot(marks, low)
 
 
@@ -209,9 +218,19 @@
         backs.append(back * (1.0 / ENT_NEGS))
     sum_ref[...] = grad
     loss_ref[...] = total
-    back = jnp.concatenate(backs, axis=0).reshape(-1, 4, NEG, WIDE)
+    back = jnp.concatenate(backs, axis=0)
+    tiles = [back[:, k * 128 : (k + 1) * 128] for k in range(4)]
+    lane = iota(tiles[0].shape, 1)
+    turned = pltpu.roll(tiles[3], 72, 1)
+    tiles = tiles[0], tiles[2], jnp.where(lane < 72, tiles[1], turned), turned
+    tiles = [tile.reshape(-1, 4, NEG, 128) for tile in tiles]
+    rest = jnp.where(lane < 32, pltpu.roll(turned, 16, 1), 0.0).reshape(-1, 4, NEG, 128)
+    low = iota((1, 8, 128), 2) < 16
     for k in range(4):
-        back_ref[(at_ref[0] + 4 - k) & 3] = back[:, k]
+        at = (at_ref[0] + 4 - k) & 3
+        for j in range(3):
+            back_ref[at, :, j * NEG : (j + 1) * NEG, :] = tiles[j][:, k]
+        back_ref[at, :, 3 * NEG :, :] = jnp.where(low, tiles[3][:, k, :8], rest[:, k, 8:])
 
     @pl.when(step == last)
     def _():
@@ -345,7 +364,14 @@
                     high_ref, low_ref):
     @pl.when(pl.program_id(0) == 0)
     def _():
-        high, low = split(jnp.sum(neg_ref[...], axis=0))
+        total = jnp.sum(neg_ref[...], axis=0)
+        first, second, mixed = [total[j * NEG : (j + 1) * NEG] for j in range(3)]
+        rest = total[3 * NEG :]
+        rest = jnp.concatenate([rest, pltpu.roll(rest, 112, 1)], axis=0)
+        lane = iota(mixed.shape, 1)
+        fourth = jnp.where(lane < 56, pltpu.roll(mixed, 56, 1), pltpu.roll(rest, 56, 1))
+        parts = [first, jnp.where(lane < 72, mixed, 0.0), second, jnp.where(lane < 72, fourth, 0.0)]
+        high, low = split(jnp.concatenate(parts, axis=1))
         high_ref[...] = high
         low_ref[...] = low
 
@@ -410,14 +436,11 @@
     picked, head_row = lax.optimization_barrier((picked, head_row))
     near = jnp.concatenate(around(picked, "z"), axis=0)
 
-    query, heads, rels, sent, place = pl.pallas_call(
+    sent, place = pl.pallas_call(
         prepare,
-        out_shape=[
-            shape(TRIP, WIDE), shape(TRIP, WIDE), shape(TRIP, WIDE), shape(SLOTS, WIDE),
-            shape(TRIP, 128, dtype=I32),
-        ],
+        out_shape=[shape(SLOTS, WIDE), shape(TRIP, 128, dtype=I32)],
         in_specs=[VMEM] * 7,
-        out_specs=[VMEM] * 5,
+        out_specs=[VMEM] * 2,
         compiler_params=params(),
         name="prepare",
     )(head_row, rel_row, owner_row, tail_row, ent_t, hub_t, rel_t)
@@ -427,7 +450,16 @@
         got = lax.all_to_all(parts, SHARD, split_axis=0, concat_axis=0, tiled=True)
         return got.reshape(SLOTS, WIDE)
 
-    sent, near, own_arg = lax.optimization_barrier((sent, near, own_arg))
+    sent, near, own_arg, rel_row = lax.optimization_barrier((sent, near, own_arg, rel_row))
+    query, heads, rels = pl.pallas_call(
+        embed_rows,
+        out_shape=[shape(TRIP, WIDE)] * 3,
+        in_specs=[VMEM] * 5,
+        out_specs=[VMEM] * 3,
+        compiler_params=params(),
+        cost_estimate=cost(1e6, 1e5),
+        name="embed_rows",
+    )(head_row, rel_row, ent_t, hub_t, rel_t)
     near = lax.all_gather(near, ("x", "y"), axis=0, tiled=True)
     query_other = lax.ppermute(query, "core", SWAP)
     asked = exchange(sent)
@@ -461,7 +493,9 @@
     whole = pl.BlockSpec((TRIP, WIDE), lambda i, at: (0, 0))
     part, grad_q, grad_other = pl.pallas_call(
         score,
-        out_shape=[shape(4, places, NEG, WIDE), shape(TRIP, WIDE), shape(TRIP, WIDE)],
+        out_shape=[
+            shape(4, places, NEG_PACKED, 128), shape(TRIP, WIDE), shape(TRIP, WIDE)
+        ],
         grid_spec=pltpu.PrefetchScalarGridSpec(
             num_scalar_prefetch=1,
             grid=(places // group,),
@@ -469,7 +503,8 @@
                 whole, whole, pl.BlockSpec((group, 4 * NEG, WIDE), lambda i, at: (i, 0, 0))
             ],
             out_specs=[
-                pl.BlockSpec((4, group, NEG, WIDE), lambda i, at: (0, i, 0, 0)), whole, whole
+                pl.BlockSpec((4, group, NEG_PACKED, 128), lambda i, at: (0, i, 0, 0)),
+                whole, whole
             ],
             scratch_shapes=[
                 pltpu.VMEM((2 * TRIP, WIDE), BF16), pltpu.VMEM((2 * TRIP, WIDE), BF16),
@@ -487,7 +522,7 @@
     )
     grad_other, back = lax.optimization_barrier((grad_other, back))
     grad_more = lax.ppermute(grad_other, "core", SWAP)
-    part, back = lax.optimization_barrier((part.reshape(CHIP_COUNT, NEG, WIDE), back))
+    part, back = lax.optimization_barrier((part.reshape(CHIP_COUNT, NEG_PACKED, 128), back))
     neg_sums = lax.all_to_all(part, CHIPS, split_axis=0, concat_axis=0, tiled=True)
 
     grad_head, both_mine, both_other, loss = pl.pallas_call(
@@ -536,7 +571,7 @@
         out_shape=shape(CHIP_COUNT, OWN, 128),
         in_specs=[VMEM] * 2,
         out_specs=VMEM,
-        compiler_params=params(),
+        compiler_params=params(12),
         name="update_own",
     )(sums, mine_rows)
     new_mine = lax.all_to_all(own_new, CHIPS, split_axis=0, concat_axis=0, tiled=True)
@@ -547,7 +582,7 @@
         grid=(ENT // columns,),
         in_specs=[
             pl.BlockSpec((NEG, 128), lambda i: (0, 0)),
-            pl.BlockSpec((CHIP_COUNT, NEG, WIDE), lambda i: (0, 0, 0)),
+            pl.BlockSpec((CHIP_COUNT, NEG_PACKED, 128), lambda i: (0, 0, 0)),
             pl.BlockSpec((WIDTH, columns), lambda i: (0, i)),
             pl.BlockSpec((1, columns), lambda i: (0, i)),
             pl.BlockSpec((WIDTH, columns), lambda i: (0, i)),
@@ -588,7 +623,7 @@
                 scratch_shapes=[pltpu.VMEM((4, REL // 2, 128), F32)],
             ),
             input_output_aliases={k + 2: k for k in range(len(before))},
-            compiler_params=params(),
+            compiler_params=params(16),
             name="place_new",
         )(side, part, *before)
 

time: 218 us -> 209 us (0.959)
  waiting for transfers between devices: 69 us -> 58.6 us
  Pallas kernels: 86.6 us -> 90.5 us
    all_to_all x2, waiting for transfers between devices: 32.8 us -> 23.7 us  [exchange(): got = lax.all_to_all(parts, SHARD, split_axis=0, concat_axis=0, tiled=True)]
    pallas_call x2 -> x3, Pallas kernels: 30.2 us -> 38.2 us  [the longest x1 21.1 us: body(): pl.pallas_call(score, out_shape=[shape(4, places, NEG_PACKED, 128), shape...]
    all_to_all x1, waiting for transfers between devices: 14.4 us -> 11.5 us  [body(): lax.all_to_all(part, CHIPS, split_axis=0, concat_axis=0, tiled=True)]
    pallas_call x2, Pallas kernels: 5.31 us -> 2.68 us  [placed(): pl.pallas_call(place_new, out_shape=[shape(*size) for size in sizes], gri...]
    unnamed x18 -> x14, local copies, waits for them, and re-layouts: 6.86 us -> 4.72 us
  transfers between devices with their start and end apart: 13 -> 13, of which waited for: 7 -> 8; matrix products, arithmetic and copies ran while one was open for 1% -> 2% of each run, Pallas kernels for 36% -> 41%
where the time goes in v7:
time: 209 us; the launch traced here: 208 us
  Pallas kernels  90.5 us (43%)
  waiting for transfers between devices  58.6 us (28%)
  starting transfers between devices  36 us (17%)
  between operations  14.1 us (7%)
  local copies, waits for them, and re-layouts  5.39 us (3%)
  other arithmetic  3.16 us (2%)
    all_to_all x2, waiting for transfers between devices, exchange(): got = lax.all_to_all(parts, SHARD, split_axis=0, concat_axis=0, tiled=True)  23.7 us
    pallas_call x1, Pallas kernels, body(): pl.pallas_call(score, out_shape=[shape(4, places, NEG_PACKED, 128), shape...  21.1 us
    pallas_call x1, Pallas kernels, body(): pl.pallas_call(scatter_entities, out_shape=shape(WIDTH, ENT), grid=(ENT /...  12.9 us
    all_to_all x2, starting transfers between devices, exchange(): got = lax.all_to_all(parts, SHARD, split_axis=0, concat_axis=0, tiled=True)  12.7 us
    all_to_all x1, waiting for transfers between devices, body(): lax.all_to_all(part, CHIPS, split_axis=0, concat_axis=0, tiled=True)  11.5 us
    all_to_all x1, waiting for transfers between devices, body(): lax.all_to_all(own_new, CHIPS, split_axis=0, concat_axis=0, tiled=True)  10.2 us
    pallas_call x1, Pallas kernels, body(): pl.pallas_call(prepare, out_shape=[shape(SLOTS, WIDE), shape(TRIP, 128, d...  9.05 us
    pallas_call x1, Pallas kernels, body(): pl.pallas_call(answer_queries, out_shape=shape(SLOTS, WIDE), grid=(SLOTS...  9.01 us
  transfers between devices with their start and end apart: 13, of which 8 were waited for; matrix products, arithmetic and copies ran while one was open for 2% of the time, Pallas kernels for 41%

profile of v7, /device:TPU:0, one launch (start us, length us, event | category | flops | bytes accessed | tf_op | source)
XLA Modules:
  0.0 207.8 jit_solution(3323075291857883613)
XLA Ops:
  7.2 3.6 %pick_negatives.1 = f32[16,512]{1,0:T(8,128)} custom-call(s32[16]{0:T(128)} %rows_ref.1, f32[400,2048]{1,0:T(8,128)} %bitcast.26), custom_call_target="tpu_custom_call" | custom-call | tf_op jit(solution)/shard_map/pick_negatives/pallas_call | solution.py:427
  10.8 2.0 collective-permute-start
  12.8 3.6 %collective-permute-start.1 = (f32[16,512]{1,0:T(8,128)}, f32[16,512]{1,0:T(8,128)S(1)}, u32[]{:S(2)}, u32[]{:S(2)}) collective-permute-start(f32[16,512]{1,0:T(8,128)} %pick_negatives.1), channel_id=1, source_target_pairs={{0,64},{32,96},{64,0},{96,32},{1,65},{33,97},{65,1},{97,33},{2,66}... | collective-permute-start | bytes 98312 | tf_op jit(solution)/shard_map/ppermute | solution.py:399
  16.4 1.0 collective-permute-start.2
  17.4 9.0 %prepare.1 = (f32[1024,512]{1,0:T(8,128)}, s32[512,128]{1,0:T(8,128)}) custom-call(s32[1,512]{1,0:T(1,128)} %bitcast.45, s32[1,512]{1,0:T(1,128)} %bitcast.49, s32[1,512]{1,0:T(1,128)} %bitcast.55, s32[1,512]{1,0:T(1,128)} %bitcast.56, f32[400,2048]{1,0:T(8,128)} %bitcast.27, f32[400,1024]{1,0:T(8,128)} %bitcast.34, f32[400,512]{1,0:T(8,128)} %bitcast.38), custom_call_target="tpu_custom_call" | custom-call | tf_op jit(solution)/shard_map/prepare/pallas_call | solution.py:439
  27.1 8.0 %all-to-all-start = ((f32[128,8,512]{2,1,0:T(8,128)}), f32[128,8,512]{2,1,0:T(8,128)S(1)}, u32[]{:S(2)}, u32[]{:S(2)}) async-start(f32[128,8,512]{2,1,0:T(8,128)} %bitcast.41), calls=%async_computation | async-start | bytes 4194304 | tf_op jit(solution)/shard_map/all_to_all | solution.py:450
  35.2 8.1 %embed_rows.1 = (f32[512,512]{1,0:T(8,128)}, f32[512,512]{1,0:T(8,128)}, f32[512,512]{1,0:T(8,128)}) custom-call(s32[1,512]{1,0:T(1,128)} %bitcast.46, s32[1,512]{1,0:T(1,128)} %bitcast.50, f32[400,2048]{1,0:T(8,128)} %bitcast.28, f32[400,1024]{1,0:T(8,128)} %bitcast.35, f32[400,512]{1,0:T(8,128)} %bitcast.39), custom_call_target="tpu_custom_call" | custom-call | flops 1000000 | bytes 100000 | tf_op jit(solution)/shard_map/embed_rows/pallas_call | solution.py:454
  43.3 7.2 %turn_tables.1 = (bf16[2048,512]{1,0:T(8,128)(2,1)}, bf16[2048,512]{1,0:T(8,128)(2,1)}, f32[40,128]{1,0:T(8,128)}) custom-call(s32[1]{0:T(128)} %bitcast.9.own_ref, f32[400,2048]{1,0:T(8,128)} %bitcast.29, f32[400,1024]{1,0:T(8,128)} %bitcast.36, f32[400,512]{1,0:T(8,128)} %bitcast.40, f32[1,1024]{1,0:T(1,128)} %bitcast.53, f32[1,512]{1,0:T(1,128)} %bitcast.57), custom_call_target="tpu_custom_call" | custom-call | flops 1000000 | bytes 100000 | tf_op jit(solution)/shard_map/turn_tables/pallas_call | solution.py:466
  50.4 17.2 %all-to-all-done = f32[128,8,512]{2,1,0:T(8,128)S(1)} async-done(((f32[128,8,512]{2,1,0:T(8,128)}), f32[128,8,512]{2,1,0:T(8,128)S(1)}, u32[]{:S(2)}, u32[]{:S(2)}) %all-to-all-start) | async-done | bytes 2097184 | tf_op jit(solution)/shard_map/all_to_all | solution.py:450
  67.6 1.3 copy-done.1
  69.0 9.0 %answer_queries.1.answer_ref = f32[1024,512]{1,0:T(8,128)} custom-call(f32[1024,512]{1,0:T(8,128)} %bitcast.31, bf16[2048,512]{1,0:T(8,128)(2,1)} %get-tuple-element.59.high_ref, bf16[2048,512]{1,0:T(8,128)(2,1)} %get-tuple-element.60.low_ref), custom_call_target="tpu_custom_call" | custom-call | tf_op jit(solution)/shard_map/answer_queries/pallas_call | solution.py:480
  78.0 4.6 %all-to-all-start.1 = ((f32[128,8,512]{2,1,0:T(8,128)}), f32[128,8,512]{2,1,0:T(8,128)S(1)}, u32[]{:S(2)}, u32[]{:S(2)}) async-start(f32[128,8,512]{2,1,0:T(8,128)} %bitcast.33), calls=%async_computation.1 | async-start | bytes 4194304 | tf_op jit(solution)/shard_map/all_to_all | solution.py:450
  82.6 1.7 all-gather.2.cloned.1.call-done
  84.4 1.0 copy-done.6
  85.4 21.1 %score.1 = (f32[4,16,56,128]{3,2,1,0:T(8,128)}, f32[512,512]{1,0:T(8,128)}, f32[512,512]{1,0:T(8,128)}) custom-call(s32[1]{0:T(128)} %bitcast.1.at_ref, f32[512,512]{1,0:T(8,128)} %get-tuple-element.55.query_ref, f32[512,512]{1,0:T(8,128)} %copy-done.6, f32[16,64,512]{2,1,0:T(8,128)} %bitcast.60), custom_call_target="tpu_custom_call" | custom-call | flops 20000000000 | bytes 12000000 | tf_op jit(solution)/shard_map/score/pallas_call | solution.py:494
  106.5 6.5 %all-to-all-done.1 = f32[128,8,512]{2,1,0:T(8,128)S(1)} async-done(((f32[128,8,512]{2,1,0:T(8,128)}), f32[128,8,512]{2,1,0:T(8,128)S(1)}, u32[]{:S(2)}, u32[]{:S(2)}) %all-to-all-start.1) | async-done | bytes 2097184 | tf_op jit(solution)/shard_map/all_to_all | solution.py:450
  113.0 1.4 copy-done.2
  114.4 5.7 %all-to-all-start.2 = ((f32[64,56,128]{2,1,0:T(8,128)}), f32[64,56,128]{2,1,0:T(8,128)}, u32[]{:S(2)}, u32[]{:S(2)}) async-start(f32[64,56,128]{2,1,0:T(8,128)} %bitcast.42), calls=%async_computation.2 | async-start | bytes 3670016 | tf_op jit(solution)/shard_map/all_to_all | solution.py:526
  121.1 8.3 %close_triples.1 = (f32[512,512]{1,0:T(8,128)}, f32[64,40,128]{2,1,0:T(8,128)}, f32[64,40,128]{2,1,0:T(8,128)}, f32[1,512]{1,0:T(1,128)}) custom-call(s32[1]{0:T(128)} %bitcast.core_ref.side_ref, f32[1024,512]{1,0:T(8,128)} %bitcast.37, s32[512,128]{1,0:T(8,128)} %get-tuple-element.66.place_ref, f32[512,512]{1,0:T(8,128)} %get-tuple-element.67.headv_ref, ...), custom_call_target="tpu_custom_call" | custom-call | tf_op jit(solution)/shard_map/close_triples/pallas_call | solution.py:528
  129.5 3.2 %collective-permute-done.5 = f32[64,40,128]{2,1,0:T(8,128)S(1)} collective-permute-done((f32[64,40,128]{2,1,0:T(8,128)}, f32[64,40,128]{2,1,0:T(8,128)S(1)}, u32[]{:S(2)}, u32[]{:S(2)}) %collective-permute-start.5) | collective-permute-done | bytes 1310752 | tf_op jit(solution)/shard_map/ppermute | solution.py:539
  132.7 2.5 %add.15 = f32[64,40,128]{2,1,0:T(8,128)} add(f32[64,40,128]{2,1,0:T(8,128)} %get-tuple-element.71, f32[64,40,128]{2,1,0:T(8,128)S(1)} %collective-permute-done.5) | non-fusion elementwise | flops 327680 | bytes 3932160 | tf_op jit(solution)/shard_map/add | solution.py:541
  135.2 11.5 %all-to-all-done.2.neg_ref = f32[64,56,128]{2,1,0:T(8,128)} async-done(((f32[64,56,128]{2,1,0:T(8,128)}), f32[64,56,128]{2,1,0:T(8,128)}, u32[]{:S(2)}, u32[]{:S(2)}) %all-to-all-start.2) | async-done | bytes 1835040 | tf_op jit(solution)/shard_map/all_to_all | solution.py:526
  146.7 5.8 %all-to-all-start.3 = ((f32[64,40,128]{2,1,0:T(8,128)}), f32[64,40,128]{2,1,0:T(8,128)S(1)}, u32[]{:S(2)}, u32[]{:S(2)}) async-start(f32[64,40,128]{2,1,0:T(8,128)} %add.15), calls=%async_computation.3 | async-start | bytes 2621440 | tf_op jit(solution)/shard_map/all_to_all | solution.py:543
  152.6 12.9 %scatter_entities.1.grad_ref = f32[400,2048]{1,0:T(8,128)} custom-call(s32[1,512]{1,0:T(1,128)} %bitcast.48, f32[512,512]{1,0:T(8,128)} %get-tuple-element.75.gradh_ref, f32[1024,512]{1,0:T(8,128)} %bitcast.32, f32[1024,512]{1,0:T(8,128)} %answer_queries.1.answer_ref), custom_call_target="tpu_custom_call" | custom-call | flops 1000000 | bytes 100000 | tf_op jit(solution)/shard_map/scatter_entities/pallas_call | solution.py:547
  165.5 6.6 %all-to-all-done.3.sums_ref = f32[64,40,128]{2,1,0:T(8,128)S(1)} async-done(((f32[64,40,128]{2,1,0:T(8,128)}), f32[64,40,128]{2,1,0:T(8,128)S(1)}, u32[]{:S(2)}, u32[]{:S(2)}) %all-to-all-start.3) | async-done | bytes 1310752 | tf_op jit(solution)/shard_map/all_to_all | solution.py:543
  172.1 1.3 update_own.1
  173.4 5.1 %all-to-all-start.4 = ((f32[64,40,128]{2,1,0:T(8,128)}), f32[64,40,128]{2,1,0:T(8,128)S(1)}, u32[]{:S(2)}, u32[]{:S(2)}) async-start(f32[64,40,128]{2,1,0:T(8,128)} %update_own.1), calls=%async_computation.4 | async-start | bytes 2621440 | tf_op jit(solution)/shard_map/all_to_all | solution.py:577
  179.2 7.2 %update_entities.1 = (f32[400,2048]{1,0:T(8,128)}, f32[1,2048]{1,0:T(1,128)}) custom-call(s32[16,128]{1,0:T(8,128)} %broadcast_in_dim.2.rows_ref, f32[64,56,128]{2,1,0:T(8,128)} %all-to-all-done.2.neg_ref, f32[400,2048]{1,0:T(8,128)} %bitcast.30, f32[1,2048]{1,0:T(1,128)} %bitcast.52, f32[400,2048]{1,0:T(8,128)} %scatter_entities.1.grad_ref), custom_call_target="tpu_custom_call" | custom-call | flops 1000000 | bytes 100000 | tf_op jit(solution)/shard_map/update_entities/pallas_call | solution.py:579
  186.4 10.2 %all-to-all-done.4.part_ref = f32[64,40,128]{2,1,0:T(8,128)S(1)} async-done(((f32[64,40,128]{2,1,0:T(8,128)}), f32[64,40,128]{2,1,0:T(8,128)S(1)}, u32[]{:S(2)}, u32[]{:S(2)}) %all-to-all-start.4) | async-done | bytes 1310752 | tf_op jit(solution)/shard_map/all_to_all | solution.py:577
  196.6 1.3 place_new.2
  197.9 1.7 collective-permute-done.6.part_ref
  199.6 1.3 place_new.3
  (24 shorter events, 2.4 us)
Async XLA Ops:
  7.2 77.2 %all-gather.2.cloned.1.call-start = ((), (), s32[]{:S(2)}) async-start(), calls=%async_computation.5 | async-start | bytes 2228224 | tf_op jit(solution)/shard_map/all_gather | solution.py:463
  10.8 15.6 %collective-permute-start = (f32[16,512]{1,0:T(8,128)}, f32[16,512]{1,0:T(8,128)S(1)}, u32[]{:S(2)}, u32[]{:S(2)}) collective-permute-start(f32[16,512]{1,0:T(8,128)} %pick_negatives.1), channel_id=1, source_target_pairs={{0,32},{32,64},{64,96},{96,0},{1,33},{33,65},{65,97},{97,1},{2,34}... | collective-permute-start | bytes 98312 | tf_op jit(solution)/shard_map/ppermute | solution.py:399
  12.8 13.7 %collective-permute-start.1 = (f32[16,512]{1,0:T(8,128)}, f32[16,512]{1,0:T(8,128)S(1)}, u32[]{:S(2)}, u32[]{:S(2)}) collective-permute-start(f32[16,512]{1,0:T(8,128)} %pick_negatives.1), channel_id=1, source_target_pairs={{0,64},{32,96},{64,0},{96,32},{1,65},{33,97},{65,1},{97,33},{2,66}... | collective-permute-start | bytes 98312 | tf_op jit(solution)/shard_map/ppermute | solution.py:399
  16.4 10.1 %collective-permute-start.2 = (f32[16,512]{1,0:T(8,128)}, f32[16,512]{1,0:T(8,128)S(1)}, u32[]{:S(2)}, u32[]{:S(2)}) collective-permute-start(f32[16,512]{1,0:T(8,128)} %pick_negatives.1), channel_id=1, source_target_pairs={{0,96},{32,0},{64,32},{96,64},{1,97},{33,1},{65,33},{97,65},{2,98}... | collective-permute-start | bytes 98312 | tf_op jit(solution)/shard_map/ppermute | solution.py:399
  17.4 9.1 %copy-start.4 = (f32[16,512]{1,0:T(8,128)S(1)}, f32[16,512]{1,0:T(8,128)}, u32[]{:S(2)}) copy-start(f32[16,512]{1,0:T(8,128)} %pick_negatives.1) | copy-start | bytes 98308
  27.1 40.5 %all-to-all-start = ((f32[128,8,512]{2,1,0:T(8,128)}), f32[128,8,512]{2,1,0:T(8,128)S(1)}, u32[]{:S(2)}, u32[]{:S(2)}) async-start(f32[128,8,512]{2,1,0:T(8,128)} %bitcast.41), calls=%async_computation | async-start | bytes 4194304 | tf_op jit(solution)/shard_map/all_to_all | solution.py:450
  43.2 41.1 %collective-permute-start.3 = (f32[512,512]{1,0:T(8,128)}, f32[512,512]{1,0:T(8,128)S(1)}, u32[]{:S(2)}, u32[]{:S(2)}) collective-permute-start(f32[512,512]{1,0:T(8,128)} %get-tuple-element.55.query_ref), channel_id=1, source_target_pairs={{0,1},{1,0},{2,3},{3,2},{4,5},{5,4},{6,7},{7,6},{8,9},{9,8},{10,11... | collective-permute-start | bytes 3145736 | tf_op jit(solution)/shard_map/ppermute | solution.py:464
  67.6 1.3 copy-start.1
  78.0 35.0 %all-to-all-start.1 = ((f32[128,8,512]{2,1,0:T(8,128)}), f32[128,8,512]{2,1,0:T(8,128)S(1)}, u32[]{:S(2)}, u32[]{:S(2)}) async-start(f32[128,8,512]{2,1,0:T(8,128)} %bitcast.33), calls=%async_computation.1 | async-start | bytes 4194304 | tf_op jit(solution)/shard_map/all_to_all | solution.py:450
  84.4 1.0 copy-start.6
  113.0 1.4 copy-start.2
  113.0 7.2 %collective-permute-start.4 = (f32[512,512]{1,0:T(8,128)}, f32[512,512]{1,0:T(8,128)S(1)}, u32[]{:S(2)}, u32[]{:S(2)}) collective-permute-start(f32[512,512]{1,0:T(8,128)} %get-tuple-element.70), channel_id=1, source_target_pairs={{0,1},{1,0},{2,3},{3,2},{4,5},{5,4},{6,7},{7,6},{8,9},{9,8},{10,11... | collective-permute-start | bytes 3145736 | tf_op jit(solution)/shard_map/ppermute | solution.py:524
  114.4 32.3 %all-to-all-start.2 = ((f32[64,56,128]{2,1,0:T(8,128)}), f32[64,56,128]{2,1,0:T(8,128)}, u32[]{:S(2)}, u32[]{:S(2)}) async-start(f32[64,56,128]{2,1,0:T(8,128)} %bitcast.42), calls=%async_computation.2 | async-start | bytes 3670016 | tf_op jit(solution)/shard_map/all_to_all | solution.py:526
  120.2 1.0 copy-start.3
  129.5 3.2 %collective-permute-start.5 = (f32[64,40,128]{2,1,0:T(8,128)}, f32[64,40,128]{2,1,0:T(8,128)S(1)}, u32[]{:S(2)}, u32[]{:S(2)}) collective-permute-start(f32[64,40,128]{2,1,0:T(8,128)} %get-tuple-element.72), channel_id=1, source_target_pairs={{0,1},{1,0},{2,3},{3,2},{4,5},{5,4},{6,7},{7,6},{8,9},{9,8},{10,11... | collective-permute-start | bytes 3932168 | tf_op jit(solution)/shard_map/ppermute | solution.py:539
  146.7 25.3 %all-to-all-start.3 = ((f32[64,40,128]{2,1,0:T(8,128)}), f32[64,40,128]{2,1,0:T(8,128)S(1)}, u32[]{:S(2)}, u32[]{:S(2)}) async-start(f32[64,40,128]{2,1,0:T(8,128)} %add.15), calls=%async_computation.3 | async-start | bytes 2621440 | tf_op jit(solution)/shard_map/all_to_all | solution.py:543
  152.6 19.5 %copy-start = (f32[40,128]{1,0:T(8,128)S(1)}, f32[40,128]{1,0:T(8,128)}, u32[]{:S(2)}) copy-start(f32[40,128]{1,0:T(8,128)} %get-tuple-element.79.mine_ref) | copy-start | bytes 61444
  173.4 5.1 %copy-start.5 = (s32[16]{0:T(128)S(1)}, s32[16]{0:T(128)}, u32[]{:S(2)}) copy-start(s32[16]{0:T(128)} %rows_ref.1) | copy-start | bytes 196
  173.4 23.2 %all-to-all-start.4 = ((f32[64,40,128]{2,1,0:T(8,128)}), f32[64,40,128]{2,1,0:T(8,128)S(1)}, u32[]{:S(2)}, u32[]{:S(2)}) async-start(f32[64,40,128]{2,1,0:T(8,128)} %update_own.1), calls=%async_computation.4 | async-start | bytes 2621440 | tf_op jit(solution)/shard_map/all_to_all | solution.py:577
  196.6 3.0 %collective-permute-start.6 = (f32[64,40,128]{2,1,0:T(8,128)S(1)}, f32[64,40,128]{2,1,0:T(8,128)S(1)}, u32[]{:S(2)}, u32[]{:S(2)}) collective-permute-start(f32[64,40,128]{2,1,0:T(8,128)S(1)} %all-to-all-done.4.part_ref), channel_id=1, source_target_pairs={{0,1},{1,0},{2,3},{3,2},{4,5},{5,4},{6,7},{7,6},{8,9},{9,8},{10,11... | collective-permute-start | bytes 3932168 | tf_op jit(solution)/shard_map/ppermute | solution.py:607
Sparse Core Ops, SparseCore 0:
  27.2 57.0 all-gather.1
